TPU v7x, 32 devices: a whole 2x2x4 slice. The times are simulated.
32 devices in a mesh: expert: 16 (over z, y, x), dp: 2 (over core).
Axes of the slice: x: 2, y: 2, z: 4, core: 2. Of those that a mesh axis runs over, the one named last changes fastest.
Arguments:
- tokens: bfloat16 [4096, 7168], P(('expert', 'dp')), may hold values from -6 to 6
- cotangent: bfloat16 [4096, 7168], P(('expert', 'dp')), may hold values from -6 to 6
- logits: float32 [4096, 32], P(('expert', 'dp')), may hold values from -8 to 8
- expert_ids: int32 [4096, 8], P(('expert', 'dp')), may hold values from 0 to 31, all different within a row; in each aligned block of 128 rows (0 to 127, 128 to 255, ...) at most 40 rows name the same one
- gate_proj: bfloat16 [16, 7168, 128], P('expert'), may hold values from -0.0625 to 0.0625
- up_proj: bfloat16 [16, 7168, 128], P('expert'), may hold values from -0.0625 to 0.0625
- down_proj: bfloat16 [16, 128, 7168], P('expert'), may hold values from -0.125 to 0.125
Outputs:
- token_grad: bfloat16 [4096, 7168], P(('expert', 'dp'))
- logit_grad: float32 [4096, 32], P(('expert', 'dp'))
- down_grad: bfloat16 [16, 128, 7168], P('expert', None, 'dp')
Inputs may be any that keep to these rules, and one draw needn't show every extreme that they name: `expert_ids`: each row names 8 different experts. Within the 128 rows of one device no expert is named more than 40 times, a bound that some block reaches.
All inputs are finite; a program needn't handle non-finite values.
Results may differ from a plain program's by a relative error of at most 0.012.
Values may be sent and summed in bfloat16 or wider, within the bound.
No kernel may reach another device: no remote copies, remote signals or barrier semaphores. Data moves between devices by JAX's collectives and lax.ppermute only.
A program may use at most 192 MiB of HBM per device.

v0:
```python
import jax
import jax.numpy as jnp
from jax import lax
from jax.sharding import PartitionSpec as P

SPLIT = 16


SCALE = 2.5


def slot_ranks(block_ids, experts):
    flat = block_ids.reshape(-1)
    onehot = (flat[:, None] == jnp.arange(experts, dtype=jnp.int32)[None, :]).astype(jnp.int32)
    before = jnp.cumsum(onehot, axis=0) - onehot
    return jnp.sum(before * onehot, axis=1)


def router_weights(logits, expert_ids):
    experts = logits.shape[1]
    pick = (expert_ids[:, :, None] == jnp.arange(experts, dtype=jnp.int32)[None, None, :]).astype(
        jnp.float32
    )
    chosen = jnp.sum(pick * jax.nn.sigmoid(logits)[:, None, :], axis=2)
    total = jnp.sum(chosen, axis=1, keepdims=True)
    return (pick, chosen, total, SCALE * chosen / total)


def router_grad(pick, chosen, total, dweight):
    inner = jnp.sum(dweight * chosen, axis=1, keepdims=True) / total
    dchosen = SCALE / total * (dweight - inner)
    dlogit = dchosen * chosen * (1.0 - chosen)
    return jnp.sum(pick * dlogit[:, :, None], axis=1)


def expert_forward(rows, gate, up):
    gated = jnp.dot(rows, gate, preferred_element_type=jnp.float32)
    upped = jnp.dot(rows, up, preferred_element_type=jnp.float32)
    sig = jax.nn.sigmoid(gated)
    active = gated * sig
    hidden = (active * upped).astype(jnp.bfloat16)
    return (gated, upped, sig, active, hidden)


def expert_backward(forward, cot, weight_b, gate, up, down):
    gated, upped, sig, active, hidden = forward
    contract = (((1,), (1,)), ((), ()))
    proj = lax.dot_general(cot, down, contract, preferred_element_type=jnp.float32)
    dots = jnp.sum(hidden.astype(jnp.float32) * proj, axis=1).astype(jnp.bfloat16)
    dhidden = weight_b.astype(jnp.float32)[:, None] * proj
    dgate = (dhidden * upped * sig * (1.0 + gated * (1.0 - sig))).astype(jnp.bfloat16)
    dup = (dhidden * active).astype(jnp.bfloat16)
    back = lax.dot_general(dgate, gate, contract, preferred_element_type=jnp.float32)
    back = back + lax.dot_general(dup, up, contract, preferred_element_type=jnp.float32)
    scaled = (weight_b.astype(jnp.float32)[:, None] * cot.astype(jnp.float32)).astype(jnp.bfloat16)
    dweight = lax.dot_general(
        hidden, scaled, (((0,), (0,)), ((), ())), preferred_element_type=jnp.float32
    )
    return (dots, back.astype(jnp.bfloat16), dweight)


def widen(array, held_count):
    shape = array.shape
    grown = jnp.broadcast_to(array[:, None], (held_count, SPLIT) + shape[1:])
    return grown.reshape((held_count * SPLIT,) + shape[1:])


def per_device(tokens, cotangent, logits, expert_ids, gate_proj, up_proj, down_proj):
    devices = lax.axis_size("expert")
    held = devices // SPLIT
    tok_count, top = expert_ids.shape
    experts = logits.shape[1]
    width = tokens.shape[1]
    capacity = max(2, 5 * tok_count * top // (4 * experts))
    send_count = held * capacity
    slot_count = devices * capacity
    pick, chosen, total, weight = router_weights(logits, expert_ids)
    weight_b = weight.astype(jnp.bfloat16).reshape(-1)
    ranks = slot_ranks(expert_ids, experts)
    flat_ids = expert_ids.reshape(-1)
    inside = flat_ids < held
    position = jnp.where(inside, flat_ids * capacity + ranks, -1)
    match = (position[:, None] == jnp.arange(send_count, dtype=jnp.int32)[None, :]).astype(
        jnp.int32
    )
    filled = jnp.sum(match, axis=0) > 0
    source_entry = jnp.sum(match * jnp.arange(tok_count * top, dtype=jnp.int32)[:, None], axis=0)
    source_tok = source_entry // top
    zero_b = jnp.zeros((), jnp.bfloat16)
    rows_block = jnp.where(filled[:, None], tokens[source_tok], zero_b).reshape(
        held, capacity, width
    )
    cot_block = jnp.where(filled[:, None], cotangent[source_tok], zero_b).reshape(
        held, capacity, width
    )
    send_weight = widen(
        jnp.where(filled, weight_b[source_entry], zero_b).reshape(held, capacity), held
    )
    gate = gate_proj[0]
    up = up_proj[0]
    down = down_proj[0]
    send_rows = widen(rows_block, held)
    send_cot = widen(cot_block, held)
    got_rows, got_cot, got_weight = (
        lax.all_to_all(send_rows, "expert", split_axis=0, concat_axis=0, tiled=True),
        lax.all_to_all(send_cot, "expert", split_axis=0, concat_axis=0, tiled=True),
        lax.all_to_all(send_weight, "expert", split_axis=0, concat_axis=0, tiled=True),
    )
    forward = expert_forward(got_rows.reshape(slot_count, width), gate, up)
    cot_rows = got_cot.reshape(slot_count, width)
    dots, back, dweight = expert_backward(
        forward, cot_rows, got_weight.reshape(slot_count), gate, up, down
    )
    back_got, dots_got = (
        lax.all_to_all(
            back.reshape(devices, capacity, width),
            "expert",
            split_axis=0,
            concat_axis=0,
            tiled=True,
        ),
        lax.all_to_all(
            dots.reshape(devices, capacity), "expert", split_axis=0, concat_axis=0, tiled=True
        ),
    )
    per_token = jnp.sum(match.reshape(tok_count, top, send_count), axis=1).reshape(
        tok_count, held, capacity
    )
    combine = widen(jnp.transpose(per_token, (1, 0, 2)), held).reshape(
        held, SPLIT, tok_count, capacity
    )
    combine = (
        jnp.transpose(combine, (2, 0, 1, 3)).reshape(tok_count, slot_count).astype(jnp.bfloat16)
    )
    token_grad = jnp.dot(
        combine, back_got.reshape(slot_count, width), preferred_element_type=jnp.float32
    ).astype(jnp.bfloat16)
    dots_sum = jnp.sum(dots_got.astype(jnp.float32).reshape(held, SPLIT, capacity), axis=1).reshape(
        send_count
    )
    safe = jnp.where(inside, position, 0)
    dweight_tk = jnp.where(inside, dots_sum[safe], jnp.zeros((), jnp.float32)).reshape(
        tok_count, top
    )
    logit_grad = router_grad(pick, chosen, total, dweight_tk)
    down_part = lax.psum_scatter(dweight, "dp", scatter_dimension=1, tiled=True)
    down_grad = down_part.astype(jnp.bfloat16)[None]
    return (token_grad, logit_grad, down_grad)


def solution(mesh):
    in_specs = (
        P(("expert", "dp"), None),
        P(("expert", "dp"), None),
        P(("expert", "dp"), None),
        P(("expert", "dp"), None),
        P("expert", None, None),
        P("expert", None, None),
        P("expert", None, None),
    )
    out_specs = (P(("expert", "dp"), None), P(("expert", "dp"), None), P("expert", None, "dp"))
    return jax.shard_map(
        per_device, mesh=mesh, in_specs=in_specs, out_specs=out_specs, check_vma=False
    )
```

profile of v0, /device:TPU:12, one launch (start us, length us, event | category | flops | bytes accessed | tf_op | source)
XLA Modules:
  0.0 742.7 jit_solution(17529818756144019375)
XLA Ops:
  7.2 0.0 copy-start
  7.2 0.9 copy.31
  8.1 0.1 eq.62
  8.2 0.1 eq.58
  8.3 9.0 %reduce-window.6 = s32[32,8,128]{2,1,0:T(8,128)S(1)} reduce-window(s32[32,8,128]{2,1,0:T(8,128)S(1)} %fusion.19, s32[]{:T(128)} %constant.16.clone.1), window={size=1x1x128 pad=0_0x0_0x127_0}, to_apply=%region_0.0 | reduce-window | flops 4161536 | bytes 262148 | tf_op jit(solution)/shard_map/reduce-window
  17.3 0.1 slice.55
  17.4 0.1 copy.33
  17.6 0.1 copy.34
  17.7 0.1 broadcast_add_fusion
  17.8 0.1 convert_reduce_fusion
  18.0 3.2 gather_fusion.1
  21.2 3.2 gather_fusion.2
  24.4 0.1 broadcast_select_fusion.1
  24.5 1.1 reshape.297
  25.6 206.4 %all_to_all.27 = bf16[16,40,7168]{2,1,0:T(8,128)(2,1)} all-to-all(bf16[16,40,7168]{2,1,0:T(8,128)(2,1)S(1)} %reshape.297), channel_id=1, replica_groups=mesh['expert'=16,'dp'=2] {'expert'}, dimensions={0} | all-to-all | bytes 18350080 | tf_op jit(solution)/shard_map/all_to_all | solution.py:105
  232.0 4.7 reshape.295
  236.7 0.0 copy-start.4
  236.7 0.0 copy-start.5
  236.7 6.5 all-to-all-start.1
  243.2 0.1 reduce_sum.97
  243.4 0.0 copy-done.4
  243.4 0.0 copy-start.2
  243.4 0.0 copy-done.5
  243.4 0.0 copy-done
  243.4 6.5 fusion.5
  249.9 0.0 copy-done.2
  250.0 6.4 fusion.8
  256.4 189.2 %all-to-all-done.1 = bf16[16,40,7168]{2,1,0:T(8,128)(2,1)} async-done(((bf16[16,40,7168]{2,1,0:T(8,128)(2,1)}), bf16[16,40,7168]{2,1,0:T(8,128)(2,1)}, u32[]{:S(2)}, u32[]{:S(2)}) %all-to-all-start.1) | async-done | bytes 9175072 | tf_op jit(solution)/shard_map/all_to_all | solution.py:106
  445.6 7.2 multiply_reduce_fusion
  452.7 0.7 convert_element_type.111
  453.4 8.5 %all-to-all-start.4 = ((bf16[16,1,40]{2,1,0:T(2,128)(2,1)}), bf16[16,1,40]{2,1,0:T(2,128)(2,1)S(1)}, u32[]{:S(2)}, u32[]{:S(2)}) async-start(bf16[16,1,40]{2,1,0:T(2,128)(2,1)} %convert_element_type.111), calls=%async_computation.4 | async-start | bytes 16384 | tf_op jit(solution)/shard_map/all_to_all | solution.py:122
  462.0 0.1 select_reduce_fusion
  462.0 0.1 copy.37
  462.1 0.1 lt.66
  462.2 0.1 copy.38
  462.3 0.1 mul.131
  462.4 4.5 all-to-all-done.4
  466.9 0.7 fusion.27
  467.7 0.7 fusion.26
  468.4 0.6 fusion.28
  469.1 4.4 compare_select_fusion.1
  473.5 0.4 compare_reduce_fusion.32
  473.9 20.7 %select_select_fusion.1 = f32[1024]{0:T(1024)S(1)} fusion(pred[1024]{0:T(1024)(128)(4,1)S(1)} %get-tuple-element.37, pred[1024]{0:T(1024)(128)(4,1)S(1)} %get-tuple-element.36, pred[1024]{0:T(1024)(128)(4,1)S(1)} %get-tuple-element.35, pred[1024]{0:T(1024)(128)(4,1)S(1)} %get-tuple-element.34, pred[1024]{0:T(1024)(128)(4,1)S(1)} %get-tuple-element.33, ...), kind=kLoop, calls=%fused_computation.94 | loop fusion | flops 33792 | bytes 42116 | tf_op jit(solution)/shard_map/gather | solution.py:142
  494.6 0.1 gather.18
  494.8 0.1 copy.36
  494.9 0.1 convert_element_type.95
  495.0 0.8 gather_fusion
  495.8 9.8 %all_to_all.28 = bf16[16,1,40]{2,1,0:T(2,128)(2,1)S(1)} all-to-all(bf16[16,1,40]{2,1,0:T(2,128)(2,1)S(1)} %reshape.294), channel_id=1, replica_groups=mesh['expert'=16,'dp'=2] {'expert'}, dimensions={0} | all-to-all | bytes 2560 | tf_op jit(solution)/shard_map/all_to_all | solution.py:107
  505.7 0.1 reshape.300
  505.8 0.0 copy-start.3
  505.8 8.9 %fusion.3 = f32[640,7168]{1,0:T(8,128)} fusion(bf16[1,7168,128]{2,1,0:T(8,128)(2,1)S(1)} %copy-done, f32[640,128]{0,1:T(8,128)S(1)} %fusion.5, f32[640,128]{0,1:T(8,128)S(1)} %fusion.8, f32[640,128]{0,1:T(8,128)S(1)} %get-tuple-element.95, f32[640]{0:T(1024)S(1)} %reshape.300), kind=kOutput, calls=%fused_computation.9 | convolution fusion | flops 1175306240 | bytes 21170688 | tf_op jit(solution)/shard_map/dot_general | solution.py:53
  514.7 0.0 copy-done.3
  514.7 12.4 %add_convert_fusion = bf16[640,7168]{1,0:T(8,128)(2,1)} fusion(f32[640,7168]{1,0:T(8,128)} %fusion.3, bf16[1,7168,128]{2,1,0:T(8,128)(2,1)S(1)} %copy-done.3, f32[640,128]{0,1:T(8,128)S(1)} %get-tuple-element.95, f32[640]{0:T(1024)S(1)} %reshape.300, f32[640,128]{0,1:T(8,128)S(1)} %fusion.5), kind=kOutput, calls=%fused_computation.4 | convolution fusion | flops 1184153600 | bytes 30018048 | tf_op jit(solution)/shard_map/dot_general | solution.py:54
  527.1 6.9 all-to-all-start.3
  534.0 0.0 reduce-scatter.2.cloned.1.call-start
  534.0 7.3 fusion
  541.3 0.0 copy-start.1
  541.3 0.0 reduce-scatter.2.cloned.1.call-update
  541.4 0.6 select_reduce_fusion.3
  542.0 12.2 %reduce-scatter.2.cloned.1.call-done = f32[128,3584]{1,0:T(8,128)} async-done(((f32[128,7168]{1,0:T(8,128)}), f32[128,3584]{1,0:T(8,128)}) %reduce-scatter.2.cloned.1.call-update) | async-done | bytes 1835024 | tf_op jit(solution)/shard_map/reduce_scatter | solution.py:146
  554.2 2.5 convert_bitcast_fusion
  556.7 172.6 %all-to-all-done.3 = bf16[16,40,7168]{2,1,0:T(8,128)(2,1)} async-done(((bf16[16,40,7168]{2,1,0:T(8,128)(2,1)}), bf16[16,40,7168]{2,1,0:T(8,128)(2,1)}, u32[]{:S(2)}, u32[]{:S(2)}) %all-to-all-start.3) | async-done | bytes 9175072 | tf_op jit(solution)/shard_map/all_to_all | solution.py:115
  729.3 6.5 fusion.2
  735.8 0.0 copy-done.1
  (21 shorter events, 0.4 us)
Async XLA Ops:
  7.2 236.3 %copy-start = (bf16[1,7168,128]{2,1,0:T(8,128)(2,1)S(1)}, bf16[1,7168,128]{2,1,0:T(8,128)(2,1)}, u32[]{:S(2)}) copy-start(bf16[1,7168,128]{2,1,0:T(8,128)(2,1)} %param.11) | copy-start | bytes 5505028
  236.7 6.7 copy-start.4
  236.7 6.7 copy-start.5
  236.7 208.9 %all-to-all-start.1 = ((bf16[16,40,7168]{2,1,0:T(8,128)(2,1)}), bf16[16,40,7168]{2,1,0:T(8,128)(2,1)}, u32[]{:S(2)}, u32[]{:S(2)}) async-start(bf16[16,40,7168]{2,1,0:T(8,128)(2,1)} %reshape.295), calls=%async_computation.1 | async-start | bytes 18350080 | tf_op jit(solution)/shard_map/all_to_all | solution.py:106
  243.4 6.6 copy-start.2
  453.4 13.5 %all-to-all-start.4 = ((bf16[16,1,40]{2,1,0:T(2,128)(2,1)}), bf16[16,1,40]{2,1,0:T(2,128)(2,1)S(1)}, u32[]{:S(2)}, u32[]{:S(2)}) async-start(bf16[16,1,40]{2,1,0:T(2,128)(2,1)} %convert_element_type.111), calls=%async_computation.4 | async-start | bytes 16384 | tf_op jit(solution)/shard_map/all_to_all | solution.py:122
  505.8 8.9 %copy-start.3 = (bf16[1,7168,128]{2,1,0:T(8,128)(2,1)S(1)}, bf16[1,7168,128]{2,1,0:T(8,128)(2,1)}, u32[]{:S(2)}) copy-start(bf16[1,7168,128]{2,1,0:T(8,128)(2,1)} %param.12) | copy-start | bytes 5505028
  527.1 202.3 %all-to-all-start.3 = ((bf16[16,40,7168]{2,1,0:T(8,128)(2,1)}), bf16[16,40,7168]{2,1,0:T(8,128)(2,1)}, u32[]{:S(2)}, u32[]{:S(2)}) async-start(bf16[16,40,7168]{2,1,0:T(8,128)(2,1)} %bitcast.106), calls=%async_computation.3 | async-start | bytes 18350080 | tf_op jit(solution)/shard_map/all_to_all | solution.py:115
  534.0 20.3 %reduce-scatter.2.cloned.1.call-start = ((), (), s32[]{:S(2)}) async-start(), calls=%async_computation.6 | async-start | bytes 5505024 | tf_op jit(solution)/shard_map/reduce_scatter | solution.py:146
  541.3 194.5 %copy-start.1 = (bf16[1,7168,128]{2,1,0:T(8,128)(2,1)S(1)}, bf16[1,7168,128]{2,1,0:T(8,128)(2,1)}, u32[]{:S(2)}) copy-start(bf16[1,7168,128]{2,1,0:T(8,128)(2,1)} %param.11) | copy-start | bytes 5505028
Sparse Core Ops, SparseCore 0:
  541.5 12.7 reduce-scatter.1
where the time goes:
time: 744 us; the launch traced here: 743 us
  waiting for transfers between devices  378 us (51%)
  blocking collectives  216 us (29%)
  matrix products  55.2 us (7%)
  other arithmetic  38.4 us (5%)
  starting transfers between devices  22 us (3%)
  local copies, waits for them, and re-layouts  18.2 us (2%)
  between operations  14.3 us (2%)
    all_to_all x1, blocking collectives, per_device(): lax.all_to_all(send_rows, 'expert', split_axis=0, concat_axis=0, tiled=True)  206 us
    all_to_all x1, waiting for transfers between devices, per_device(): lax.all_to_all(send_cot, 'expert', split_axis=0, concat_axis=0, tiled=True)  189 us
    all_to_all x1, waiting for transfers between devices, per_device(): lax.all_to_all(back.reshape(devices, capacity, width), 'expert', split_ax...  173 us
    gather x3, other arithmetic, per_device(): dots_sum[safe]  25.5 us
  transfers between devices with their start and end apart: 4, of which 4 were waited for; matrix products, arithmetic and copies ran while one was open for 3% of the time, Pallas kernels for 0%

commit v1 on v0

v1 whole, which is shorter than its diff:
```python
import jax
import jax.numpy as jnp
from jax import lax
from jax.sharding import PartitionSpec as P

SPLIT = 16
SCALE = 2.5
PAIR = 2


def router(logits, expert_ids):
    experts = logits.shape[1]
    lane = jnp.arange(experts, dtype=jnp.int32)[None, None, :]
    has = jnp.any(expert_ids[:, :, None] == lane, axis=1)
    chosen = jnp.where(has, jax.nn.sigmoid(logits), 0.0)
    total = jnp.sum(chosen, axis=1, keepdims=True)
    return has, chosen, total, SCALE * chosen / total


def select_matrix(has, held, capacity):
    count = has.shape[0]
    live = has[:, :held]
    row = jnp.arange(count, dtype=jnp.int32)
    before = (row[None, :] < row[:, None]).astype(jnp.bfloat16)
    rank = jnp.dot(before, live.astype(jnp.bfloat16), preferred_element_type=jnp.float32)
    slot = jnp.arange(capacity, dtype=jnp.float32)
    pick = live[:, :, None] & (rank[:, :, None] == slot[None, None, :])
    return pick.astype(jnp.bfloat16)


def per_device(tokens, cotangent, logits, expert_ids, gate_proj, up_proj, down_proj):
    devices = lax.axis_size("expert")
    cores = lax.axis_size("dp")
    core = lax.axis_index("dp")
    held = devices // SPLIT
    tok_count, top = expert_ids.shape
    experts = logits.shape[1]
    width = tokens.shape[1]
    capacity = max(2, 5 * tok_count * top // (4 * experts))
    members = SPLIT // PAIR
    index = lax.axis_index("expert")
    across = [[e * SPLIT + j for e in range(held)] for j in range(SPLIT)]
    within = [
        [e * SPLIT + m * PAIR + p for m in range(members)] for e in range(held) for p in range(PAIR)
    ]
    swap = [(i, i ^ 1) for i in range(devices)]

    part = width // cores
    gate, up, down = gate_proj[0], up_proj[0], down_proj[0]
    send_w = jnp.concatenate(
        [
            lax.dynamic_slice_in_dim(gate, core * part, part, 0),
            lax.dynamic_slice_in_dim(up, core * part, part, 0),
        ],
        axis=1,
    )
    send_d = lax.dynamic_slice_in_dim(down, core * part, part, 1)
    got_w = lax.ppermute(send_w, "expert", swap)
    got_d = lax.ppermute(send_d, "expert", swap)
    pair_w = lax.all_gather(got_w, "dp", axis=0, tiled=True)
    pair_d = lax.all_gather(got_d, "dp", axis=0, tiled=False)
    pair_d = jnp.transpose(pair_d, (1, 0, 2)).reshape(down.shape)

    has, chosen, total, weight = router(logits, expert_ids)
    weight_b = weight[:, :held].astype(jnp.bfloat16)
    pick = select_matrix(has, held, capacity)
    pick2 = pick.reshape(tok_count, held * capacity)
    contract0 = (((0,), (0,)), ((), ()))
    rows = lax.dot_general(pick2, tokens, contract0, preferred_element_type=jnp.float32)
    cots = lax.dot_general(pick2, cotangent, contract0, preferred_element_type=jnp.float32)
    slot_w = jnp.sum(
        pick.astype(jnp.float32) * weight_b.astype(jnp.float32)[:, :, None], axis=0
    ).reshape(held * capacity, 1)
    rows = rows.astype(jnp.bfloat16).reshape(held, capacity, width)
    scaled = (cots * slot_w).astype(jnp.bfloat16).reshape(held, capacity, width)

    def gather(block):
        if held > 1:
            block = lax.all_to_all(
                block, "expert", 0, 0, axis_index_groups=across, tiled=True
            )
        full = lax.all_gather(block, "expert", axis_index_groups=within, axis=0, tiled=True)
        return full.reshape(members * held * capacity, width)

    x = gather(rows)
    sc = gather(scaled)

    gu_w = jnp.concatenate([gate, up], axis=1)
    ff = gate.shape[1]
    own = jnp.dot(x, gu_w, preferred_element_type=jnp.float32)
    oth = jnp.dot(x, pair_w, preferred_element_type=jnp.float32)
    g = jnp.concatenate([own[:, :ff], oth[:, :ff]], axis=1)
    u = jnp.concatenate([own[:, ff:], oth[:, ff:]], axis=1)
    contract = (((1,), (1,)), ((), ()))
    dn = jnp.concatenate([down, pair_d], axis=0)
    proj = lax.dot_general(sc, dn, contract, preferred_element_type=jnp.float32)
    sig = jax.nn.sigmoid(g)
    active = g * sig
    hidden = (active * u).astype(jnp.bfloat16)
    dots = jnp.sum(hidden.astype(jnp.float32) * proj, axis=1)
    dgate = (proj * u * sig * (1.0 + g * (1.0 - sig))).astype(jnp.bfloat16)
    dup = (proj * active).astype(jnp.bfloat16)
    d_own = jnp.concatenate([dgate[:, :ff], dup[:, :ff]], axis=1)
    d_oth = jnp.concatenate([dgate[:, ff:], dup[:, ff:]], axis=1)
    back = lax.dot_general(d_own, gu_w, contract, preferred_element_type=jnp.float32)
    back = back + lax.dot_general(d_oth, pair_w, contract, preferred_element_type=jnp.float32)
    back = back.astype(jnp.bfloat16)

    dots_all = lax.all_gather(dots, "expert", axis_index_groups=within, axis=0)
    back_sum = lax.psum_scatter(
        back.reshape(members * held, capacity, width),
        "expert",
        scatter_dimension=0,
        axis_index_groups=within,
        tiled=True,
    )
    member = (index % SPLIT) // PAIR
    dots_sum = jnp.sum(dots_all, axis=0).reshape(members, held, capacity)
    dots_mine = lax.dynamic_index_in_dim(dots_sum, member, 0, keepdims=False)
    if held > 1:
        back_sum = lax.all_to_all(
            back_sum, "expert", 0, 0, axis_index_groups=across, tiled=True
        )
        dots_mine = lax.all_to_all(
            dots_mine, "expert", 0, 0, axis_index_groups=across, tiled=True
        )
    grad_d = lax.dot_general(hidden, sc, contract0, preferred_element_type=jnp.float32)
    grad_part = lax.psum_scatter(
        grad_d.astype(jnp.bfloat16), "dp", scatter_dimension=1, tiled=True
    )
    grad_got = lax.ppermute(grad_part[ff:], "expert", swap)
    down_grad = (grad_part[:ff].astype(jnp.float32) + grad_got.astype(jnp.float32)).astype(
        jnp.bfloat16
    )[None]

    token_grad = jnp.dot(
        pick2, back_sum.reshape(held * capacity, width), preferred_element_type=jnp.float32
    ).astype(jnp.bfloat16)
    dw = jnp.sum(pick.astype(jnp.float32) * dots_mine[None], axis=2)
    live = has[:, :held]
    dw = jnp.where(live, dw / jnp.where(live, weight_b.astype(jnp.float32), 1.0), 0.0)
    dw = jnp.pad(dw, ((0, 0), (0, experts - held)))
    inner = jnp.sum(dw * chosen, axis=1, keepdims=True) / total
    dchosen = SCALE / total * (dw - inner)
    logit_grad = jnp.where(has, dchosen * chosen * (1.0 - chosen), 0.0)
    return (token_grad, logit_grad, down_grad)


def solution(mesh):
    in_specs = (
        P(("expert", "dp"), None),
        P(("expert", "dp"), None),
        P(("expert", "dp"), None),
        P(("expert", "dp"), None),
        P("expert", None, None),
        P("expert", None, None),
        P("expert", None, None),
    )
    out_specs = (P(("expert", "dp"), None), P(("expert", "dp"), None), P("expert", None, "dp"))
    return jax.shard_map(
        per_device, mesh=mesh, in_specs=in_specs, out_specs=out_specs, check_vma=False
    )
```

time: 744 us -> 374 us (0.50)
  the two profiles are of different devices: /device:TPU:12 before, /device:TPU:0 now
where the time goes in v1:
time: 374 us
  waiting for transfers between devices  269 us (72%)
  blocking collectives  35.5 us (9%)
  matrix products  29.5 us (8%)
  local copies, waits for them, and re-layouts  15.6 us (4%)
  between operations  15 us (4%)
  other arithmetic  4.73 us (1%)
  starting transfers between devices  4.67 us (1%)
    all_gather x2, waiting for transfers between devices, gather(): lax.all_gather(block, 'expert', axis_index_groups=within, axis=0, tiled=T...  153 us
    reduce_scatter x1, waiting for transfers between devices, per_device(): lax.psum_scatter(back.reshape(members * held, capacity, width), 'expert',...  45.3 us
    ppermute x1, waiting for transfers between devices, per_device(): got_w = lax.ppermute(send_w, 'expert', swap)  37.6 us
    unnamed x1, blocking collectives  35.5 us
    ppermute x1, waiting for transfers between devices, per_device(): got_d = lax.ppermute(send_d, 'expert', swap)  18.1 us
    ppermute x1, waiting for transfers between devices, per_device(): grad_got = lax.ppermute(grad_part[ff:], 'expert', swap)  12.5 us
  transfers between devices with their start and end apart: 9, of which 7 were waited for; matrix products, arithmetic and copies ran while one was open for 9% of the time, Pallas kernels for 0%

profile of v1, /device:TPU:0, one launch (start us, length us, event | category | flops | bytes accessed | tf_op | source)
XLA Modules:
  0.0 373.7 jit_solution(4802877967684690616)
XLA Ops:
  7.2 0.0 copy-start
  7.2 0.0 all-gather.13.cloned.1.call-start
  7.2 1.4 dynamic-slice_bitcast_fusion.2
  8.6 3.0 collective-permute-start
  11.6 1.6 dynamic-slice_bitcast_fusion
  13.2 0.0 copy-start.7
  13.2 1.4 pad_maximum_fusion.3
  14.6 0.0 copy-start.6
  14.6 0.0 collective-permute-start.1
  14.6 18.1 %collective-permute-done = bf16[128,3584]{1,0:T(8,128)(2,1)S(1)} collective-permute-done((bf16[128,3584]{1,0:T(8,128)(2,1)S(1)}, bf16[128,3584]{1,0:T(8,128)(2,1)S(1)}, u32[]{:S(2)}, u32[]{:S(2)}) %collective-permute-start) | collective-permute-done | bytes 917536 | tf_op jit(solution)/shard_map/ppermute | solution.py:59
  32.8 0.0 copy-start.5
  32.8 0.9 copy-done.5
  33.7 0.0 all-gather.13.cloned.1.call-update
  33.7 0.0 all-gather.9.cloned.1.call-start
  33.8 37.6 %collective-permute-done.1 = bf16[3584,256]{1,0:T(8,128)(2,1)} collective-permute-done((bf16[3584,256]{1,0:T(8,128)(2,1)}, bf16[3584,256]{1,0:T(8,128)(2,1)}, u32[]{:S(2)}, u32[]{:S(2)}) %collective-permute-start.1) | collective-permute-done | bytes 1835040 | tf_op jit(solution)/shard_map/ppermute | solution.py:58
  71.4 0.0 all-gather.9.cloned.1.call-update
  71.4 0.0 all-gather.15.cloned.1.call-start
  71.5 0.0 copy-done.7
  71.5 0.1 convolution_bitcast_fusion
  71.6 0.0 copy-done
  71.6 1.3 convolution_convert_fusion.2
  73.0 0.0 all-gather.15.cloned.1.call-update
  73.0 0.0 all-gather.11.cloned.1.call-start
  73.0 0.0 copy-done.6
  73.1 0.1 fusion.25
  73.2 2.8 fusion.1
  76.0 0.0 all-gather.11.cloned.1.call-update
  76.1 0.0 reduce-scatter.5.cloned.1.call-start
  76.1 3.9 %copy.15 = bf16[1,128,7168]{1,2,0:T(8,128)(2,1)} copy(bf16[1,128,7168]{2,1,0:T(8,128)(2,1)} %param.13) | data formatting | bytes 3670016 | tf_op args[6]
  80.0 0.0 all-gather.13.cloned.1.call-done
  80.0 4.0 %copy.16 = bf16[128,2,3584]{0,2,1:T(8,128)(2,1)} copy(bf16[128,2,3584]{2,0,1:T(8,128)(2,1)} %bitcast.48) | data formatting | bytes 3670016 | tf_op jit(solution)/shard_map/transpose | solution.py:62
  84.0 1.9 all-gather.9.cloned.1.call-done
  86.0 81.7 %all-gather.15.cloned.1.call-done = bf16[320,7168]{1,0:T(8,128)(2,1)} async-done(((bf16[40,7168]{1,0:T(8,128)(2,1)}), bf16[320,7168]{1,0:T(8,128)(2,1)}) %all-gather.15.cloned.1.call-update) | async-done | bytes 4587536 | tf_op jit(solution)/shard_map/all_gather | solution.py:82
  167.7 4.9 %fusion.54 = f32[320,256]{1,0:T(8,128)S(1)} fusion(bf16[320,7168]{1,0:T(8,128)(2,1)} %all-gather.15.cloned.1.call-done, bf16[7168,256]{1,0:T(8,128)(2,1)} %all-gather.9.cloned.1.call-done), kind=kOutput, calls=%fused_computation.85 | convolution fusion | flops 1174405120 | bytes 8585216 | tf_op jit(solution)/shard_map/dot_general | solution.py:91
  172.6 0.0 copy-done.2
  172.6 0.0 copy-done.3
  172.6 0.9 copy-done.8
  173.5 1.3 fusion.7
  174.9 71.3 %all-gather.11.cloned.1.call-done = bf16[320,7168]{1,0:T(8,128)(2,1)} async-done(((bf16[40,7168]{1,0:T(8,128)(2,1)}), bf16[320,7168]{1,0:T(8,128)(2,1)}) %all-gather.11.cloned.1.call-update) | async-done | bytes 4587536 | tf_op jit(solution)/shard_map/all_gather | solution.py:82
  246.1 5.0 %multiply_reduce_fusion = (f32[320]{0:T(512)S(1)}, bf16[320,256]{1,0:T(8,128)(2,1)S(1)}, bf16[320,256]{1,0:T(8,128)(2,1)S(1)}, bf16[320,256]{1,0:T(8,128)(2,1)S(1)}) fusion(f32[320,128]{1,0:T(8,128)S(1)} %get-tuple-element.11, f32[320,128]{1,0:T(8,128)S(1)} %get-tuple-element.9, f32[320,128]{1,0:T(8,128)S(1)} %get-tuple-element.12, ...), kind=kOutput, calls=%fused_computation.24 | convolution fusion | flops 1183383296 | bytes 9405696 | tf_op jit(solution)/shard_map/dot_general | solution.py:96
  251.2 0.0 copy-done.1
  251.2 3.9 %convolution_convert_fusion = bf16[256,7168]{1,0:T(8,128)(2,1)} fusion(bf16[320,256]{1,0:T(8,128)(2,1)S(1)} %get-tuple-element.4, bf16[320,7168]{1,0:T(8,128)(2,1)S(1)} %copy-done.1), kind=kOutput, calls=%fused_computation.2 | convolution fusion | flops 1176240128 | bytes 8421376 | tf_op jit(solution)/shard_map/dot_general | solution.py:127
  255.1 0.0 reduce-scatter.5.cloned.1.call-update
  255.1 0.0 reduce-scatter.3.cloned.1.call-start
  255.2 0.0 copy-start.4
  255.2 3.6 fusion.6
  258.8 0.0 copy-done.4
  258.8 3.5 fusion
  262.3 0.0 reduce-scatter.3.cloned.1.call-update
  262.3 0.6 copy-done.9
  262.9 0.6 dynamic-slice.3
  264.2 0.3 dynamic-update-slice
  264.5 35.5 %all-reduce.1 = f32[2560]{0:T(1024)S(1)} all-reduce(f32[2560]{0:T(1024)S(1)} %dynamic-update-slice), channel_id=5, replica_groups={{0,4,8,12,16,20,24,28},{2,6,10,14,18,22,26,30},{1,5,9,13,17,21,25,29},{..., use_global_device_ids=true, to_apply=%add.1 | all-reduce | flops 2560 | bytes 20480
  300.0 0.1 reshape.308
  300.1 0.1 reshape.304
  300.2 0.0 reduce-scatter.5.cloned.1.call-done
  300.2 1.2 slice.64
  301.4 1.4 collective-permute-start.2
  302.8 0.1 fusion.26
  303.0 0.6 fusion.36
  303.6 12.5 %collective-permute-done.2 = bf16[128,3584]{1,0:T(8,128)(2,1)S(1)} collective-permute-done((bf16[128,3584]{1,0:T(8,128)(2,1)S(1)}, bf16[128,3584]{1,0:T(8,128)(2,1)S(1)}, u32[]{:S(2)}, u32[]{:S(2)}) %collective-permute-start.2) | collective-permute-done | bytes 917536 | tf_op jit(solution)/shard_map/ppermute | solution.py:131
  316.1 2.3 fusion.8
  318.5 45.3 %reduce-scatter.3.cloned.1.call-done = bf16[1,40,7168]{2,1,0:T(8,128)(2,1)} async-done(((bf16[8,40,7168]{2,1,0:T(8,128)(2,1)}), bf16[1,40,7168]{2,1,0:T(8,128)(2,1)}) %reduce-scatter.3.cloned.1.call-update) | async-done | bytes 573456 | tf_op jit(solution)/shard_map/reduce_scatter | solution.py:110
  363.8 3.0 convolution_convert_fusion.1
  (19 shorter events, 0.2 us)
Async XLA Ops:
  7.2 64.5 %copy-start = (bf16[128,7168]{1,0:T(8,128)(2,1)S(1)}, bf16[128,7168]{1,0:T(8,128)(2,1)}, u32[]{:S(2)}) copy-start(bf16[128,7168]{1,0:T(8,128)(2,1)} %param.7) | copy-start | bytes 5505028
  7.2 72.9 %all-gather.13.cloned.1.call-start = ((), (), s32[]{:S(2)}) async-start(), calls=%async_computation.6 | async-start | bytes 2752512 | tf_op jit(solution)/shard_map/all_gather | solution.py:61
  8.6 24.2 %collective-permute-start = (bf16[128,3584]{1,0:T(8,128)(2,1)S(1)}, bf16[128,3584]{1,0:T(8,128)(2,1)S(1)}, u32[]{:S(2)}, u32[]{:S(2)}) collective-permute-start(bf16[128,3584]{1,0:T(8,128)(2,1)S(1)} %dynamic-slice_bitcast_fusion.2), channel_id=1, source_target_pairs={{0,2},{2,0},{4,6},{6,4},{8,10},{10,8},{12,14},{14,12},{16,18},{18,... | collective-permute-start | bytes 2752520 | tf_op jit(solution)/shard_map/ppermute | solution.py:59
  13.2 58.3 %copy-start.7 = (s32[128,8]{0,1:T(8,128)S(1)}, s32[128,8]{0,1:T(8,128)}, u32[]{:S(2)}) copy-start(s32[128,8]{0,1:T(8,128)} %param.10) | copy-start | bytes 12292
  14.6 58.4 %copy-start.6 = (f32[128,32]{0,1:T(8,128)S(1)}, f32[128,32]{0,1:T(8,128)}, u32[]{:S(2)}) copy-start(f32[128,32]{0,1:T(8,128)} %param.9) | copy-start | bytes 49156
  14.6 56.8 %collective-permute-start.1 = (bf16[3584,256]{1,0:T(8,128)(2,1)}, bf16[3584,256]{1,0:T(8,128)(2,1)}, u32[]{:S(2)}, u32[]{:S(2)}) collective-permute-start(bf16[3584,256]{1,0:T(8,128)(2,1)} %pad_maximum_fusion.3), channel_id=1, source_target_pairs={{0,2},{2,0},{4,6},{6,4},{8,10},{10,8},{12,14},{14,12},{16,18},{18,... | collective-permute-start | bytes 5505032 | tf_op jit(solution)/shard_map/ppermute | solution.py:58
  32.8 0.9 copy-start.5
  33.7 52.2 %all-gather.9.cloned.1.call-start = ((), (), s32[]{:S(2)}) async-start(), calls=%async_computation.2 | async-start | bytes 5505024 | tf_op jit(solution)/shard_map/all_gather | solution.py:60
  71.4 96.2 %all-gather.15.cloned.1.call-start = ((), (), s32[]{:S(2)}) async-start(), calls=%async_computation.7 | async-start | bytes 5160960 | tf_op jit(solution)/shard_map/all_gather | solution.py:82
  73.0 173.2 %all-gather.11.cloned.1.call-start = ((), (), s32[]{:S(2)}) async-start(), calls=%async_computation.5 | async-start | bytes 5160960 | tf_op jit(solution)/shard_map/all_gather | solution.py:82
  76.1 224.1 %reduce-scatter.5.cloned.1.call-start = ((), (), s32[]{:S(2)}) async-start(), calls=%async_computation.4 | async-start | bytes 5505024 | tf_op jit(solution)/shard_map/reduce_scatter | solution.py:128
  167.6 5.0 %copy-start.2 = (bf16[1,7168,128]{2,1,0:T(8,128)(2,1)S(1)}, bf16[1,7168,128]{2,1,0:T(8,128)(2,1)}, u32[]{:S(2)}) copy-start(bf16[1,7168,128]{2,1,0:T(8,128)(2,1)} %param.12) | copy-start | bytes 5505028
  167.6 5.0 %copy-start.3 = (bf16[1,7168,128]{2,1,0:T(8,128)(2,1)S(1)}, bf16[1,7168,128]{2,1,0:T(8,128)(2,1)}, u32[]{:S(2)}) copy-start(bf16[1,7168,128]{2,1,0:T(8,128)(2,1)} %param.11) | copy-start | bytes 5505028
  167.6 5.8 %copy-start.8 = (bf16[320,7168]{1,0:T(8,128)(2,1)S(1)}, bf16[320,7168]{1,0:T(8,128)(2,1)}, u32[]{:S(2)}) copy-start(bf16[320,7168]{1,0:T(8,128)(2,1)} %all-gather.15.cloned.1.call-done) | copy-start | bytes 13762564
  246.1 5.0 %copy-start.1 = (bf16[320,7168]{1,0:T(8,128)(2,1)S(1)}, bf16[320,7168]{1,0:T(8,128)(2,1)}, u32[]{:S(2)}) copy-start(bf16[320,7168]{1,0:T(8,128)(2,1)} %all-gather.11.cloned.1.call-done) | copy-start | bytes 13762564
  255.1 108.7 %reduce-scatter.3.cloned.1.call-start = ((), (), s32[]{:S(2)}) async-start(), calls=%async_computation.3 | async-start | bytes 5160960 | tf_op jit(solution)/shard_map/reduce_scatter | solution.py:110
  255.2 3.6 copy-start.4
  262.3 0.7 copy-start.9
  301.4 14.7 %collective-permute-start.2 = (bf16[128,3584]{1,0:T(8,128)(2,1)S(1)}, bf16[128,3584]{1,0:T(8,128)(2,1)S(1)}, u32[]{:S(2)}, u32[]{:S(2)}) collective-permute-start(bf16[128,3584]{1,0:T(8,128)(2,1)S(1)} %slice.64), channel_id=1, source_target_pairs={{0,2},{2,0},{4,6},{6,4},{8,10},{10,8},{12,14},{14,12},{16,18},{18,... | collective-permute-start | bytes 2752520 | tf_op jit(solution)/shard_map/ppermute | solution.py:131
Sparse Core Ops, SparseCore 0:
  33.9 11.9 all-gather.12
  71.5 14.3 all-gather.8
  88.2 79.4 all-gather.14
  169.7 76.4 all-gather.10
  255.2 9.6 reduce-scatter.4
  268.9 94.9 reduce-scatter.2

commit v2 on v1

v2 whole, which is shorter than its diff:
```python
import jax
import jax.numpy as jnp
from jax import lax
from jax.sharding import PartitionSpec as P

SPLIT = 16
SCALE = 2.5
QUAD = 4
bf16 = jnp.bfloat16
f32 = jnp.float32
CONTRACT0 = (((0,), (0,)), ((), ()))
CONTRACT1 = (((1,), (1,)), ((), ()))


def router(logits, expert_ids):
    experts = logits.shape[1]
    lane = jnp.arange(experts, dtype=jnp.int32)[None, None, :]
    has = jnp.any(expert_ids[:, :, None] == lane, axis=1)
    chosen = jnp.where(has, jax.nn.sigmoid(logits), 0.0)
    total = jnp.sum(chosen, axis=1, keepdims=True)
    return has, chosen, total, SCALE * chosen / total


def select_matrix(has, held, capacity):
    count = has.shape[0]
    live = has[:, :held]
    row = jnp.arange(count, dtype=jnp.int32)
    before = (row[None, :] < row[:, None]).astype(bf16)
    rank = jnp.dot(before, live.astype(bf16), preferred_element_type=f32)
    slot = jnp.arange(capacity, dtype=f32)
    pick = live[:, :, None] & (rank[:, :, None] == slot[None, None, :])
    return pick.astype(bf16)


def per_device(tokens, cotangent, logits, expert_ids, gate_proj, up_proj, down_proj):
    devices = lax.axis_size("expert")
    cores = lax.axis_size("dp")
    core = lax.axis_index("dp")
    index = lax.axis_index("expert")
    held = devices // SPLIT
    tok_count, top = expert_ids.shape
    experts = logits.shape[1]
    width = tokens.shape[1]
    ff = gate_proj.shape[2]
    part = width // cores
    capacity = max(2, 5 * tok_count * top // (4 * experts))
    members = SPLIT // QUAD
    member = (index % SPLIT) // QUAD
    across = [[e * SPLIT + j for e in range(held)] for j in range(SPLIT)]
    within = [
        [e * SPLIT + m * QUAD + q for m in range(members)] for e in range(held) for q in range(QUAD)
    ]
    swap1 = [(i, i ^ 1) for i in range(devices)]
    swap2 = [(i, i ^ 2) for i in range(devices)]
    cross = [(i, i ^ 3) for i in range(devices)]
    sibling = [(c, cores - 1 - c) for c in range(cores)]

    gu0 = jnp.concatenate(
        [
            lax.dynamic_slice_in_dim(gate_proj[0], core * part, part, 0),
            lax.dynamic_slice_in_dim(up_proj[0], core * part, part, 0),
        ],
        axis=1,
    )
    dn0 = lax.dynamic_slice_in_dim(down_proj[0], core * part, part, 1)
    gu0, logits, tokens = lax.optimization_barrier((gu0, logits, tokens))
    gu1 = lax.ppermute(gu0, "expert", swap1)
    gu2 = lax.ppermute(gu0, "expert", swap2)

    has, chosen, total, weight = router(logits, expert_ids)
    weight_b = weight[:, :held].astype(bf16)
    pick = select_matrix(has, held, capacity)
    pick2 = pick.reshape(tok_count, held * capacity)
    slot_w = jnp.sum(pick.astype(f32) * weight_b.astype(f32)[:, :, None], axis=0).reshape(
        held * capacity, 1
    )

    def halves(array):
        mine = lax.dynamic_slice_in_dim(array, core * part, part, 1)
        other = lax.dynamic_slice_in_dim(array, (cores - 1 - core) * part, part, 1)
        return mine, other

    def join(mine, theirs):
        first = jnp.where(core == 0, mine, theirs)
        second = jnp.where(core == 0, theirs, mine)
        return jnp.stack([first, second], axis=1)

    rows = lax.dot_general(pick2, tokens, CONTRACT0, preferred_element_type=f32).astype(bf16)
    cots = lax.dot_general(pick2, cotangent, CONTRACT0, preferred_element_type=f32)
    scaled = (cots * slot_w).astype(bf16)

    def spread(array):
        mine, other = halves(array)
        theirs = lax.ppermute(other, "dp", sibling)
        shape = (held, capacity, part)
        return join(mine.reshape(shape), theirs.reshape(shape))

    def gather(block):
        if held > 1:
            block = lax.all_to_all(block, "expert", 0, 0, axis_index_groups=across, tiled=True)
        block = block.reshape(held * cores * capacity, part)
        return lax.all_gather(block, "expert", axis_index_groups=within, axis=0, tiled=True)

    x_block, s_block = spread(rows), spread(scaled)
    x = gather(x_block)
    sc = gather(s_block)

    dn0, x_block = lax.optimization_barrier((dn0, x_block))
    dn1 = lax.ppermute(dn0, "expert", swap1)
    dn2 = lax.ppermute(dn0, "expert", swap2)
    low, lowf = part // 2, ff // 2
    gu3a = lax.ppermute(gu2[:low], "expert", swap1)
    gu3b = lax.ppermute(gu1[low:], "expert", swap2)
    dn3a = lax.ppermute(dn2[:lowf], "expert", swap1)
    dn3b = lax.ppermute(dn1[lowf:], "expert", swap2)

    def add_sibling(array):
        return array + lax.ppermute(array, "dp", sibling)

    dot = lambda a, b: jnp.dot(a, b, preferred_element_type=f32)
    dot1 = lambda a, b: lax.dot_general(a, b, CONTRACT1, preferred_element_type=f32)
    gu3 = jnp.concatenate([gu3a, gu3b], axis=0)
    dn3 = jnp.concatenate([dn3a, dn3b], axis=0)
    packs = (gu0, gu1, gu2, gu3)
    products = [dot(x, w) for w in packs]
    g_u = add_sibling(
        jnp.concatenate([p[:, :ff] for p in products] + [p[:, ff:] for p in products], axis=1)
    )
    proj = add_sibling(jnp.concatenate([dot1(sc, w) for w in (dn0, dn1, dn2, dn3)], axis=1))
    g, u = g_u[:, : QUAD * ff], g_u[:, QUAD * ff :]
    sig = jax.nn.sigmoid(g)
    active = g * sig
    hidden = (active * u).astype(bf16)
    dots = jnp.sum(hidden.astype(f32) * proj, axis=1)
    dgate = (proj * u * sig * (1.0 + g * (1.0 - sig))).astype(bf16)
    dup = (proj * active).astype(bf16)
    d_gu = jnp.concatenate([dgate, dup], axis=1)
    w_gu = jnp.concatenate([w[:, :ff] for w in packs] + [w[:, ff:] for w in packs], axis=1)
    back = dot1(d_gu, w_gu).astype(bf16)
    back_sum = lax.psum_scatter(
        back.reshape(members, held * cores * capacity, part),
        "expert",
        scatter_dimension=0,
        axis_index_groups=within,
        tiled=True,
    ).reshape(held, cores, capacity, part)

    grads = lax.dot_general(
        hidden, sc, CONTRACT0, preferred_element_type=f32
    ).astype(bf16)
    parts = [grads[:ff]] + [
        lax.ppermute(grads[q * ff : (q + 1) * ff], "expert", route)
        for q, route in ((1, swap1), (2, swap2), (3, cross))
    ]
    down_grad = sum(p.astype(f32) for p in parts).astype(bf16)[None]

    dots = dots.reshape(members, held * cores * capacity)
    dots_mine = lax.dynamic_index_in_dim(dots, member, 0, keepdims=False)
    for shift in range(1, members):
        target = lax.rem(member + shift, members)
        route = [
            (e * SPLIT + m * QUAD + q, e * SPLIT + (m + shift) % members * QUAD + q)
            for e in range(held)
            for m in range(members)
            for q in range(QUAD)
        ]
        sent = lax.dynamic_index_in_dim(dots, target, 0, keepdims=False)
        dots_mine = dots_mine + lax.ppermute(sent, "expert", route)
    dots_mine = dots_mine.reshape(held, cores, capacity)

    if held > 1:
        back_sum = lax.all_to_all(back_sum, "expert", 0, 0, axis_index_groups=across, tiled=True)
        dots_mine = lax.all_to_all(dots_mine, "expert", 0, 0, axis_index_groups=across, tiled=True)
    dots_mine = lax.dynamic_index_in_dim(dots_mine, core, 1, keepdims=False)
    mine = lax.dynamic_index_in_dim(back_sum, core, 1, keepdims=False)
    other = lax.dynamic_index_in_dim(back_sum, cores - 1 - core, 1, keepdims=False)
    theirs = lax.ppermute(other, "dp", sibling)
    shape = (held * capacity, part)
    gm, gt = dot(pick2, mine.reshape(shape)), dot(pick2, theirs.reshape(shape))
    token_grad = jnp.concatenate(
        [jnp.where(core == 0, gm, gt), jnp.where(core == 0, gt, gm)], axis=1
    ).astype(bf16)
    dw = jnp.sum(pick.astype(f32) * dots_mine[None], axis=2)
    live = has[:, :held]
    dw = jnp.where(live, dw / jnp.where(live, weight_b.astype(f32), 1.0), 0.0)
    dw = jnp.pad(dw, ((0, 0), (0, experts - held)))
    inner = jnp.sum(dw * chosen, axis=1, keepdims=True) / total
    dchosen = SCALE / total * (dw - inner)
    logit_grad = jnp.where(has, dchosen * chosen * (1.0 - chosen), 0.0)
    return (token_grad, logit_grad, down_grad)


def solution(mesh):
    in_specs = (
        P(("expert", "dp"), None),
        P(("expert", "dp"), None),
        P(("expert", "dp"), None),
        P(("expert", "dp"), None),
        P("expert", None, None),
        P("expert", None, None),
        P("expert", None, None),
    )
    out_specs = (P(("expert", "dp"), None), P(("expert", "dp"), None), P("expert", None, "dp"))
    return jax.shard_map(
        per_device, mesh=mesh, in_specs=in_specs, out_specs=out_specs, check_vma=False
    )
```

time: 374 us -> 209 us (0.56)
  waiting for transfers between devices: 269 us -> 106 us
  blocking collectives: 35.5 us -> 0 us
  starting transfers between devices: 4.67 us -> 19.4 us
  local copies, waits for them, and re-layouts: 15.6 us -> 30.1 us
  other arithmetic: 4.73 us -> 11.1 us
    all_gather x2, waiting for transfers between devices: 153 us -> 0.01 us  [gather(): lax.all_gather(block, 'expert', axis_index_groups=within, axis=0, tiled=T...]
    unnamed x1 -> x0, blocking collectives: 35.5 us -> none
    ppermute x3 -> x19, starting transfers between devices: 4.43 us -> 19.3 us  [the longest x3 4.67 us: per_device(): dots_mine = dots_mine + lax.ppermute(sent, 'expert', route)]
    unnamed x24 -> x41, local copies, waits for them, and re-layouts: 7.19 us -> 21 us
    reduce_scatter x2 -> x1, waiting for transfers between devices: 45.4 us -> 32.1 us  [per_device(): lax.psum_scatter(back.reshape(members, held * cores * capacity, part), 'e...]
    ppermute x3 -> x19, waiting for transfers between devices: 68.3 us -> 73.8 us  [the longest x1 47.2 us: per_device(): dn1 = lax.ppermute(dn0, 'expert', swap1)]
    transpose x1 -> x0, local copies, waits for them, and re-layouts: 3.99 us -> none  [per_device(): pair_d = jnp.transpose(pair_d, (1, 0, 2)).reshape(down.shape)]
    dot_general x10 -> x15, matrix products: 29.5 us -> 27.9 us  [the longest x5 10.7 us: per_device(): lax.dot_general(a, b, CONTRACT1, preferred_element_type=f32)]
  transfers between devices with their start and end apart: 9 -> 22, of which waited for: 7 -> 5; matrix products, arithmetic and copies ran while one was open for 9% -> 28% of each run, Pallas kernels for 0% -> 0%
where the time goes in v2:
time: 209 us
  waiting for transfers between devices  106 us (51%)
  local copies, waits for them, and re-layouts  30.1 us (14%)
  matrix products  27.9 us (13%)
  starting transfers between devices  19.4 us (9%)
  between operations  14.2 us (7%)
  other arithmetic  11.1 us (5%)
    ppermute x1, waiting for transfers between devices, per_device(): dn1 = lax.ppermute(dn0, 'expert', swap1)  47.2 us
    reduce_scatter x1, waiting for transfers between devices, per_device(): lax.psum_scatter(back.reshape(members, held * cores * capacity, part), 'e...  32.1 us
    unnamed x41, local copies, waits for them, and re-layouts  21 us
    ppermute x1, waiting for transfers between devices, per_device(): gu3a = lax.ppermute(gu2[:low], 'expert', swap1)  20.5 us
    dot_general x5, matrix products, per_device(): lax.dot_general(a, b, CONTRACT1, preferred_element_type=f32)  10.7 us
    dot_general x6, matrix products, per_device(): dot = lambda a, b: jnp.dot(a, b, preferred_element_type=f32)  9.24 us
    ppermute x3, starting transfers between devices, per_device(): dots_mine = dots_mine + lax.ppermute(sent, 'expert', route)  4.67 us
    ppermute x3, waiting for transfers between devices, per_device(): lax.ppermute(grads[q * ff:(q + 1) * ff], 'expert', route)  4.63 us
  transfers between devices with their start and end apart: 22, of which 5 were waited for; matrix products, arithmetic and copies ran while one was open for 28% of the time, Pallas kernels for 0%

profile of v2, /device:TPU:0, one launch (start us, length us, event | category | flops | bytes accessed | tf_op | source)
XLA Modules:
  0.0 208.6 jit_solution(16907107707036415635)
XLA Ops:
  7.2 1.7 dynamic-slice_bitcast_fusion.1
  9.0 1.4 pad_maximum_fusion
  10.4 2.9 %collective-permute-start.7 = (bf16[3584,256]{1,0:T(8,128)(2,1)}, bf16[3584,256]{1,0:T(8,128)(2,1)}, u32[]{:S(2)}, u32[]{:S(2)}) collective-permute-start(bf16[3584,256]{1,0:T(8,128)(2,1)} %pad_maximum_fusion), channel_id=1, source_target_pairs={{0,2},{2,0},{4,6},{6,4},{8,10},{10,8},{12,14},{14,12},{16,18},{18,... | collective-permute-start | bytes 5505032 | tf_op jit(solution)/shard_map/ppermute | solution.py:67
  13.3 1.5 collective-permute-start.8
  15.0 2.0 convolution_convert_fusion
  17.3 1.4 collective-permute-done.1
  18.8 0.9 pad_maximum_fusion.4
  19.7 2.0 fusion
  22.0 2.3 %slice_dynamic-update-slice_fusion.7 = bf16[3584,1024]{1,0:T(8,128)(2,1)} fusion(bf16[3584,256]{1,0:T(8,128)(2,1)} %pad_maximum_fusion), kind=kLoop, calls=%fused_computation.23 | loop fusion | bytes 1835008
  24.3 0.6 collective-permute-start.2
  25.1 0.9 pad_maximum_fusion.3
  26.0 47.2 %collective-permute-done.2 = bf16[128,3584]{1,0:T(8,128)(2,1)S(1)} collective-permute-done((bf16[128,3584]{1,0:T(8,128)(2,1)S(1)}, bf16[128,3584]{1,0:T(8,128)(2,1)S(1)}, u32[]{:S(2)}, u32[]{:S(2)}) %collective-permute-start.2) | collective-permute-done | bytes 917536 | tf_op jit(solution)/shard_map/ppermute | solution.py:109
  73.2 1.8 collective-permute-start.5
  75.1 0.9 slice.119
  76.0 1.5 collective-permute-start.4
  77.4 1.3 slice.124
  78.8 0.6 collective-permute-start.9
  79.4 1.2 slice.125
  80.6 1.2 collective-permute-start.10
  81.8 2.3 %slice_dynamic-update-slice_fusion.5 = bf16[3584,1024]{1,0:T(8,128)(2,1)} fusion(bf16[3584,1024]{1,0:T(8,128)(2,1)} %slice_dynamic-update-slice_fusion.7, bf16[3584,256]{1,0:T(8,128)(2,1)} %collective-permute-done.7), kind=kLoop, calls=%fused_computation.17 | loop fusion | bytes 1835008
  84.1 2.3 %slice_dynamic-update-slice_fusion.4 = bf16[3584,1024]{1,0:T(8,128)(2,1)} fusion(bf16[3584,1024]{1,0:T(8,128)(2,1)} %slice_dynamic-update-slice_fusion.5, bf16[3584,256]{1,0:T(8,128)(2,1)} %collective-permute-done.8), kind=kLoop, calls=%fused_computation.16 | loop fusion | bytes 1835008
  86.4 20.5 %collective-permute-done.9 = bf16[1792,256]{1,0:T(8,128)(2,1)S(1)} collective-permute-done((bf16[1792,256]{1,0:T(8,128)(2,1)S(1)}, bf16[1792,256]{1,0:T(8,128)(2,1)S(1)}, u32[]{:S(2)}, u32[]{:S(2)}) %collective-permute-start.9) | collective-permute-done | bytes 917536 | tf_op jit(solution)/shard_map/ppermute | solution.py:112
  107.1 1.1 slice_dynamic-update-slice_fusion.3
  108.1 2.2 %slice_dynamic-update-slice_fusion.6 = bf16[3584,1024]{1,0:T(8,128)(2,1)} fusion(bf16[3584,1024]{1,0:T(8,128)(2,1)} %slice_dynamic-update-slice_fusion.3, bf16[3584,256]{1,0:T(8,128)(2,1)} %pad_maximum_fusion), kind=kLoop, calls=%fused_computation.22 | loop fusion | bytes 1835008
  110.4 2.2 %slice_dynamic-update-slice_fusion.2 = bf16[3584,1024]{1,0:T(8,128)(2,1)} fusion(bf16[3584,1024]{1,0:T(8,128)(2,1)} %slice_dynamic-update-slice_fusion.6, bf16[3584,256]{1,0:T(8,128)(2,1)} %collective-permute-done.7), kind=kLoop, calls=%fused_computation.14 | loop fusion | bytes 1835008
  112.6 2.2 %slice_dynamic-update-slice_fusion.1 = bf16[3584,1024]{1,0:T(8,128)(2,1)} fusion(bf16[3584,1024]{1,0:T(8,128)(2,1)} %slice_dynamic-update-slice_fusion.2, bf16[3584,256]{1,0:T(8,128)(2,1)} %collective-permute-done.8), kind=kLoop, calls=%fused_computation.13 | loop fusion | bytes 1835008
  114.9 3.1 %fusion.61 = f32[320,256]{1,0:T(8,128)S(1)} fusion(bf16[320,3584]{1,0:T(8,128)(2,1)} %all-gather.5.cloned.1.call-done, bf16[3584,256]{1,0:T(8,128)(2,1)} %pad_maximum_fusion), kind=kOutput, calls=%fused_computation.122 | convolution fusion | flops 587202560 | bytes 4456448 | tf_op jit(solution)/shard_map/dot_general | solution.py:120
  118.0 0.7 slice_dynamic-update-slice_fusion.15
  118.6 2.3 %fusion.62 = f32[320,256]{1,0:T(8,128)S(1)} fusion(bf16[320,3584]{1,0:T(8,128)(2,1)S(1)} %copy-done.10, bf16[3584,256]{1,0:T(8,128)(2,1)} %collective-permute-done.7), kind=kOutput, calls=%fused_computation.123 | convolution fusion | flops 587202560 | bytes 4456448 | tf_op jit(solution)/shard_map/dot_general | solution.py:120
  120.9 0.7 slice_dynamic-update-slice_fusion.14
  121.6 2.2 %fusion.63 = f32[320,256]{1,0:T(8,128)S(1)} fusion(bf16[320,3584]{1,0:T(8,128)(2,1)S(1)} %copy-done.10, bf16[3584,256]{1,0:T(8,128)(2,1)} %collective-permute-done.8), kind=kOutput, calls=%fused_computation.124 | convolution fusion | flops 587202560 | bytes 4456448 | tf_op jit(solution)/shard_map/dot_general | solution.py:120
  123.8 0.7 slice_dynamic-update-slice_fusion.13
  124.5 0.8 fusion.64
  125.3 0.7 slice_dynamic-update-slice_fusion.12
  126.0 0.7 slice_dynamic-update-slice_fusion.11
  126.6 0.7 slice_dynamic-update-slice_fusion.10
  127.3 0.7 slice_dynamic-update-slice_fusion.9
  128.0 0.7 slice_dynamic-update-slice_fusion.8
  128.7 2.8 %fusion.60 = f32[320,128]{1,0:T(8,128)S(1)} fusion(bf16[320,3584]{1,0:T(8,128)(2,1)} %all-gather.3.cloned.1.call-done, bf16[128,3584]{1,0:T(8,128)(2,1)} %copy-done.6), kind=kOutput, calls=%fused_computation.121 | convolution fusion | flops 293601280 | bytes 3375104 | tf_op jit(solution)/shard_map/dot_general | solution.py:121
  131.5 0.7 fusion.59
  132.3 0.7 fusion.58
  133.0 2.5 %fusion.2 = f32[320,128]{1,0:T(8,128)S(1)} fusion(bf16[320,3584]{1,0:T(8,128)(2,1)S(1)} %copy-done.2, bf16[64,3584]{1,0:T(8,128)(2,1)} %collective-permute-done.5, bf16[64,3584]{1,0:T(8,128)(2,1)} %collective-permute-done.4), kind=kOutput, calls=%fused_computation.18 | convolution fusion | flops 295436288 | bytes 3375104 | tf_op jit(solution)/shard_map/dot_general | solution.py:121
  135.6 0.6 collective-permute-start.6
  136.2 0.3 slice_dynamic-update-slice_fusion
  136.5 2.0 add.89
  138.5 0.5 multiply_reduce_fusion
  139.0 4.0 %convolution_convert_fusion.2 = bf16[320,3584]{1,0:T(8,128)(2,1)} fusion(bf16[3584,1024]{1,0:T(8,128)(2,1)S(1)} %slice_dynamic-update-slice_fusion, bf16[320,512]{1,0:T(8,128)(2,1)S(1)} %get-tuple-element.18, bf16[320,512]{1,0:T(8,128)(2,1)S(1)} %get-tuple-element.19), kind=kOutput, calls=%fused_computation.4 | convolution fusion | flops 2351267840 | bytes 10289152 | tf_op jit(solution)/shard_map/dot_general | solution.py:121
  143.2 3.7 %collective-permute-start.15 = (f32[80]{0:T(128)S(1)}, f32[80]{0:T(128)S(1)}, u32[]{:S(2)}, u32[]{:S(2)}) collective-permute-start(f32[80]{0:T(128)S(1)} %get-tuple-element.27), channel_id=1, source_target_pairs={{0,24},{2,26},{4,28},{6,30},{8,0},{10,2},{12,4},{14,6},{16,8},{18,... | collective-permute-start | bytes 968 | tf_op jit(solution)/shard_map/ppermute | solution.py:168
  146.8 1.0 collective-permute-start.13
  147.9 3.8 %convolution_convert_fusion.1 = bf16[512,3584]{1,0:T(8,128)(2,1)S(1)} fusion(bf16[320,512]{1,0:T(8,128)(2,1)S(1)} %get-tuple-element.12, bf16[320,3584]{1,0:T(8,128)(2,1)} %all-gather.3.cloned.1.call-done), kind=kOutput, calls=%fused_computation.3 | convolution fusion | flops 1176240128 | bytes 6291456 | tf_op jit(solution)/shard_map/dot_general | solution.py:148
  151.7 1.6 fusion.57
  153.2 0.8 copy-done.3
  154.0 1.4 collective-permute-start.18
  155.4 1.5 collective-permute-start.17
  156.9 0.6 collective-permute-start.16
  157.8 0.6 fusion.35
  158.4 32.1 %reduce-scatter.2.cloned.1.call-done = bf16[1,80,3584]{2,1,0:T(8,128)(2,1)} async-done(((bf16[4,80,3584]{2,1,0:T(8,128)(2,1)}), bf16[1,80,3584]{2,1,0:T(8,128)(2,1)}) %reduce-scatter.2.cloned.1.call-update) | async-done | bytes 573456 | tf_op jit(solution)/shard_map/reduce_scatter | solution.py:140
  190.5 1.0 dynamic-slice_bitcast_fusion.3
  191.6 4.6 %collective-permute-done.17 = bf16[128,3584]{1,0:T(8,128)(2,1)S(1)} collective-permute-done((bf16[128,3584]{1,0:T(8,128)(2,1)}, bf16[128,3584]{1,0:T(8,128)(2,1)S(1)}, u32[]{:S(2)}, u32[]{:S(2)}) %collective-permute-start.17) | collective-permute-done | bytes 917536 | tf_op jit(solution)/shard_map/ppermute | solution.py:152
  196.2 2.8 %fusion.1 = bf16[1,128,3584]{2,1,0:T(8,128)(2,1)} fusion(bf16[128,3584]{1,0:T(8,128)(2,1)S(1)} %collective-permute-done.18, bf16[128,3584]{1,0:T(8,128)(2,1)S(1)} %collective-permute-done.17, bf16[128,3584]{1,0:T(8,128)(2,1)} %collective-permute-done.16, bf16[512,3584]{1,0:T(8,128)(2,1)} %copy-done.3), kind=kLoop, calls=%fused_computation.11 | loop fusion | flops 3670016 | bytes 4587520 | tf_op jit(solution)/shard_map/broadcast_in_dim | solution.py:155
  199.0 0.4 fusion.12
  199.5 0.5 select_convert_fusion.1
  200.0 1.4 pad_maximum_fusion.1
  201.4 0.7 copy-done.1
  (78 shorter events, 1.9 us)
Async XLA Ops:
  7.2 17.1 %copy-start = (bf16[1,128,7168]{2,1,0:T(8,128)(2,1)S(1)}, bf16[1,128,7168]{2,1,0:T(8,128)(2,1)}, u32[]{:S(2)}) copy-start(bf16[1,128,7168]{2,1,0:T(8,128)(2,1)} %param.13) | copy-start | bytes 5505028
  7.2 107.7 %all-gather.5.cloned.1.call-start = ((), (), s32[]{:S(2)}) async-start(), calls=%async_computation.2 | async-start | bytes 2867200 | tf_op jit(solution)/shard_map/all_gather | solution.py:102
  8.9 5.9 %copy-start.9 = (s32[128,8]{0,1:T(8,128)S(1)}, s32[128,8]{0,1:T(8,128)}, u32[]{:S(2)}) copy-start(s32[128,8]{0,1:T(8,128)} %param.10) | copy-start | bytes 12292
  10.4 6.8 %copy-start.8 = (f32[128,32]{0,1:T(8,128)S(1)}, f32[128,32]{0,1:T(8,128)}, u32[]{:S(2)}) copy-start(f32[128,32]{0,1:T(8,128)} %param.9) | copy-start | bytes 49156
  10.4 69.0 %collective-permute-start.7 = (bf16[3584,256]{1,0:T(8,128)(2,1)}, bf16[3584,256]{1,0:T(8,128)(2,1)}, u32[]{:S(2)}, u32[]{:S(2)}) collective-permute-start(bf16[3584,256]{1,0:T(8,128)(2,1)} %pad_maximum_fusion), channel_id=1, source_target_pairs={{0,2},{2,0},{4,6},{6,4},{8,10},{10,8},{12,14},{14,12},{16,18},{18,... | collective-permute-start | bytes 5505032 | tf_op jit(solution)/shard_map/ppermute | solution.py:67
  13.3 64.1 %collective-permute-start.8 = (bf16[3584,256]{1,0:T(8,128)(2,1)}, bf16[3584,256]{1,0:T(8,128)(2,1)}, u32[]{:S(2)}, u32[]{:S(2)}) collective-permute-start(bf16[3584,256]{1,0:T(8,128)(2,1)} %pad_maximum_fusion), channel_id=1, source_target_pairs={{0,4},{2,6},{4,0},{6,2},{8,12},{10,14},{12,8},{14,10},{16,20},{18,... | collective-permute-start | bytes 5505032 | tf_op jit(solution)/shard_map/ppermute | solution.py:68
  17.1 1.6 collective-permute-start.1
  19.7 109.0 %all-gather.3.cloned.1.call-start = ((), (), s32[]{:S(2)}) async-start(), calls=%async_computation.1 | async-start | bytes 2867200 | tf_op jit(solution)/shard_map/all_gather | solution.py:102
  21.8 3.2 %collective-permute-start = (bf16[40,3584]{1,0:T(8,128)(2,1)S(1)}, bf16[40,3584]{1,0:T(8,128)(2,1)S(1)}, u32[]{:S(2)}, u32[]{:S(2)}) collective-permute-start(bf16[40,3584]{1,0:T(8,128)(2,1)S(1)} %constant_dynamic-slice_fusion.6), channel_id=1, source_target_pairs={{0,1},{1,0},{2,3},{3,2},{4,5},{5,4},{6,7},{7,6},{8,9},{9,8},{10,11... | collective-permute-start | bytes 860168 | tf_op jit(solution)/shard_map/ppermute | solution.py:94
  24.3 48.9 %collective-permute-start.2 = (bf16[128,3584]{1,0:T(8,128)(2,1)S(1)}, bf16[128,3584]{1,0:T(8,128)(2,1)S(1)}, u32[]{:S(2)}, u32[]{:S(2)}) collective-permute-start(bf16[128,3584]{1,0:T(8,128)(2,1)S(1)} %dynamic-slice_bitcast_fusion), channel_id=1, source_target_pairs={{0,2},{2,0},{4,6},{6,4},{8,10},{10,8},{12,14},{14,12},{16,18},{18,... | collective-permute-start | bytes 2752520 | tf_op jit(solution)/shard_map/ppermute | solution.py:109
  24.9 50.2 %collective-permute-start.3 = (bf16[128,3584]{1,0:T(8,128)(2,1)S(1)}, bf16[128,3584]{1,0:T(8,128)(2,1)S(1)}, u32[]{:S(2)}, u32[]{:S(2)}) collective-permute-start(bf16[128,3584]{1,0:T(8,128)(2,1)S(1)} %dynamic-slice_bitcast_fusion), channel_id=1, source_target_pairs={{0,4},{2,6},{4,0},{6,2},{8,12},{10,14},{12,8},{14,10},{16,20},{18,... | collective-permute-start | bytes 2752520 | tf_op jit(solution)/shard_map/ppermute | solution.py:110
  26.0 164.5 %reduce-scatter.2.cloned.1.call-start = ((), (), s32[]{:S(2)}) async-start(), calls=%async_computation.3 | async-start | bytes 2867200 | tf_op jit(solution)/shard_map/reduce_scatter | solution.py:140
  73.2 5.6 %copy-start.4 = (bf16[128,3584]{1,0:T(8,128)(2,1)}, bf16[128,3584]{1,0:T(8,128)(2,1)S(1)}, u32[]{:S(2)}) copy-start(bf16[128,3584]{1,0:T(8,128)(2,1)S(1)} %collective-permute-done.2) | copy-start | bytes 2752516
  73.2 59.8 %collective-permute-start.5 = (bf16[64,3584]{1,0:T(8,128)(2,1)S(1)}, bf16[64,3584]{1,0:T(8,128)(2,1)}, u32[]{:S(2)}, u32[]{:S(2)}) collective-permute-start(bf16[64,3584]{1,0:T(8,128)(2,1)S(1)} %slice.120), channel_id=1, source_target_pairs={{0,4},{2,6},{4,0},{6,2},{8,12},{10,14},{12,8},{14,10},{16,20},{18,... | collective-permute-start | bytes 1376264 | tf_op jit(solution)/shard_map/ppermute | solution.py:115
  75.1 5.5 %copy-start.6 = (bf16[128,3584]{1,0:T(8,128)(2,1)}, bf16[128,3584]{1,0:T(8,128)(2,1)S(1)}, u32[]{:S(2)}) copy-start(bf16[128,3584]{1,0:T(8,128)(2,1)S(1)} %collective-permute-done.3) | copy-start | bytes 2752516
  76.0 57.1 %collective-permute-start.4 = (bf16[64,3584]{1,0:T(8,128)(2,1)}, bf16[64,3584]{1,0:T(8,128)(2,1)}, u32[]{:S(2)}, u32[]{:S(2)}) collective-permute-start(bf16[64,3584]{1,0:T(8,128)(2,1)} %slice.119), channel_id=1, source_target_pairs={{0,2},{2,0},{4,6},{6,4},{8,10},{10,8},{12,14},{14,12},{16,18},{18,... | collective-permute-start | bytes 1376264 | tf_op jit(solution)/shard_map/ppermute | solution.py:114
  78.8 28.2 %collective-permute-start.9 = (bf16[1792,256]{1,0:T(8,128)(2,1)S(1)}, bf16[1792,256]{1,0:T(8,128)(2,1)S(1)}, u32[]{:S(2)}, u32[]{:S(2)}) collective-permute-start(bf16[1792,256]{1,0:T(8,128)(2,1)S(1)} %slice.124), channel_id=1, source_target_pairs={{0,2},{2,0},{4,6},{6,4},{8,10},{10,8},{12,14},{14,12},{16,18},{18,... | collective-permute-start | bytes 2752520 | tf_op jit(solution)/shard_map/ppermute | solution.py:112
  80.6 26.4 %collective-permute-start.10 = (bf16[1792,256]{1,0:T(8,128)(2,1)S(1)}, bf16[1792,256]{1,0:T(8,128)(2,1)S(1)}, u32[]{:S(2)}, u32[]{:S(2)}) collective-permute-start(bf16[1792,256]{1,0:T(8,128)(2,1)S(1)} %slice.125), channel_id=1, source_target_pairs={{0,4},{2,6},{4,0},{6,2},{8,12},{10,14},{12,8},{14,10},{16,20},{18,... | collective-permute-start | bytes 2752520 | tf_op jit(solution)/shard_map/ppermute | solution.py:113
  114.9 3.8 %copy-start.10 = (bf16[320,3584]{1,0:T(8,128)(2,1)S(1)}, bf16[320,3584]{1,0:T(8,128)(2,1)}, u32[]{:S(2)}) copy-start(bf16[320,3584]{1,0:T(8,128)(2,1)} %all-gather.5.cloned.1.call-done) | copy-start | bytes 6881284
  128.7 7.9 %collective-permute-start.11 = (f32[320,1024]{1,0:T(8,128)}, f32[320,1024]{1,0:T(8,128)}, u32[]{:S(2)}, u32[]{:S(2)}) collective-permute-start(f32[320,1024]{1,0:T(8,128)} %slice_dynamic-update-slice_fusion.8), channel_id=1, source_target_pairs={{0,1},{1,0},{2,3},{3,2},{4,5},{5,4},{6,7},{7,6},{8,9},{9,8},{10,11... | collective-permute-start | bytes 3932168 | tf_op jit(solution)/shard_map/ppermute | solution.py:118
  128.7 2.8 %copy-start.2 = (bf16[320,3584]{1,0:T(8,128)(2,1)S(1)}, bf16[320,3584]{1,0:T(8,128)(2,1)}, u32[]{:S(2)}) copy-start(bf16[320,3584]{1,0:T(8,128)(2,1)} %all-gather.3.cloned.1.call-done) | copy-start | bytes 6881284
  128.7 2.8 %copy-start.5 = (bf16[128,3584]{1,0:T(8,128)(2,1)S(1)}, bf16[128,3584]{1,0:T(8,128)(2,1)}, u32[]{:S(2)}) copy-start(bf16[128,3584]{1,0:T(8,128)(2,1)} %copy-done.4) | copy-start | bytes 2752516
  131.5 4.7 %slice-start = ((s8[7340032]{0:T(1024)(128)(4,1)}), s8[4194304]{0:T(1024)(128)(4,1)S(1)}, s32[]{:S(2)}) async-start(s8[7340032]{0:T(1024)(128)(4,1)} %bitcast.86), calls=%async_computation.4 | async-start | bytes 8388608
  132.3 3.9 %slice-start.1 = ((s8[7340032]{0:T(1024)(128)(4,1)}), s8[3145728]{0:T(1024)(128)(4,1)S(1)}, s32[]{:S(2)}) async-start(s8[7340032]{0:T(1024)(128)(4,1)} %bitcast.86), calls=%async_computation.5 | async-start | bytes 6291456
  135.6 2.9 %collective-permute-start.6 = (f32[320,512]{1,0:T(8,128)S(1)}, f32[320,512]{1,0:T(8,128)S(1)}, u32[]{:S(2)}, u32[]{:S(2)}) collective-permute-start(f32[320,512]{1,0:T(8,128)S(1)} %pad_maximum_fusion.2), channel_id=1, source_target_pairs={{0,1},{1,0},{2,3},{3,2},{4,5},{5,4},{6,7},{7,6},{8,9},{9,8},{10,11... | collective-permute-start | bytes 1966088 | tf_op jit(solution)/shard_map/ppermute | solution.py:118
  143.2 13.7 %collective-permute-start.15 = (f32[80]{0:T(128)S(1)}, f32[80]{0:T(128)S(1)}, u32[]{:S(2)}, u32[]{:S(2)}) collective-permute-start(f32[80]{0:T(128)S(1)} %get-tuple-element.27), channel_id=1, source_target_pairs={{0,24},{2,26},{4,28},{6,30},{8,0},{10,2},{12,4},{14,6},{16,8},{18,... | collective-permute-start | bytes 968 | tf_op jit(solution)/shard_map/ppermute | solution.py:168
  146.8 10.7 %collective-permute-start.14 = (f32[80]{0:T(128)S(1)}, f32[80]{0:T(128)S(1)}, u32[]{:S(2)}, u32[]{:S(2)}) collective-permute-start(f32[80]{0:T(128)S(1)} %get-tuple-element.28), channel_id=1, source_target_pairs={{0,16},{2,18},{4,20},{6,22},{8,24},{10,26},{12,28},{14,30},{16,0},... | collective-permute-start | bytes 968 | tf_op jit(solution)/shard_map/ppermute | solution.py:168
  146.8 10.7 %collective-permute-start.13 = (f32[80]{0:T(128)S(1)}, f32[80]{0:T(128)S(1)}, u32[]{:S(2)}, u32[]{:S(2)}) collective-permute-start(f32[80]{0:T(128)S(1)} %get-tuple-element.26), channel_id=1, source_target_pairs={{0,8},{2,10},{4,12},{6,14},{8,16},{10,18},{12,20},{14,22},{16,24},... | collective-permute-start | bytes 968 | tf_op jit(solution)/shard_map/ppermute | solution.py:168
  151.7 2.4 %copy-start.3 = (bf16[512,3584]{1,0:T(8,128)(2,1)}, bf16[512,3584]{1,0:T(8,128)(2,1)S(1)}, u32[]{:S(2)}) copy-start(bf16[512,3584]{1,0:T(8,128)(2,1)S(1)} %convolution_convert_fusion.1) | copy-start | bytes 11010052
  154.0 37.5 %collective-permute-start.18 = (bf16[128,3584]{1,0:T(8,128)(2,1)}, bf16[128,3584]{1,0:T(8,128)(2,1)S(1)}, u32[]{:S(2)}, u32[]{:S(2)}) collective-permute-start(bf16[128,3584]{1,0:T(8,128)(2,1)} %get-tuple-element.16), channel_id=1, source_target_pairs={{0,6},{2,4},{4,2},{6,0},{8,14},{10,12},{12,10},{14,8},{16,22},{18,... | collective-permute-start | bytes 2752520 | tf_op jit(solution)/shard_map/ppermute | solution.py:152
  155.4 40.8 %collective-permute-start.17 = (bf16[128,3584]{1,0:T(8,128)(2,1)}, bf16[128,3584]{1,0:T(8,128)(2,1)S(1)}, u32[]{:S(2)}, u32[]{:S(2)}) collective-permute-start(bf16[128,3584]{1,0:T(8,128)(2,1)} %get-tuple-element.17), channel_id=1, source_target_pairs={{0,4},{2,6},{4,0},{6,2},{8,12},{10,14},{12,8},{14,10},{16,20},{18,... | collective-permute-start | bytes 2752520 | tf_op jit(solution)/shard_map/ppermute | solution.py:152
  156.9 39.3 %collective-permute-start.16 = (bf16[128,3584]{1,0:T(8,128)(2,1)S(1)}, bf16[128,3584]{1,0:T(8,128)(2,1)}, u32[]{:S(2)}, u32[]{:S(2)}) collective-permute-start(bf16[128,3584]{1,0:T(8,128)(2,1)S(1)} %get-tuple-element.15), channel_id=1, source_target_pairs={{0,2},{2,0},{4,6},{6,4},{8,10},{10,8},{12,14},{14,12},{16,18},{18,... | collective-permute-start | bytes 2752520 | tf_op jit(solution)/shard_map/ppermute | solution.py:152
  191.5 7.6 %copy-start.7 = (bf16[1,80,3584]{2,1,0:T(8,128)(2,1)S(1)}, bf16[1,80,3584]{2,1,0:T(8,128)(2,1)}, u32[]{:S(2)}) copy-start(bf16[1,80,3584]{2,1,0:T(8,128)(2,1)} %reduce-scatter.2.cloned.1.call-done) | copy-start | bytes 1720324
  191.5 8.0 %collective-permute-start.12 = (bf16[1,40,3584]{2,1,0:T(8,128)(2,1)S(1)}, bf16[1,40,3584]{2,1,0:T(8,128)(2,1)S(1)}, u32[]{:S(2)}, u32[]{:S(2)}) collective-permute-start(bf16[1,40,3584]{2,1,0:T(8,128)(2,1)S(1)} %dynamic-slice_bitcast_fusion.3), channel_id=1, source_target_pairs={{0,1},{1,0},{2,3},{3,2},{4,5},{5,4},{6,7},{7,6},{8,9},{9,8},{10,11... | collective-permute-start | bytes 860168 | tf_op jit(solution)/shard_map/ppermute | solution.py:177
  199.9 2.2 %copy-start.1 = (bf16[1,128,7168]{2,1,0:T(8,128)(2,1)S(1)}, bf16[1,128,7168]{2,1,0:T(8,128)(2,1)}, u32[]{:S(2)}) copy-start(bf16[1,128,7168]{2,1,0:T(8,128)(2,1)} %param.13) | copy-start | bytes 5505028
Sparse Core Ops, SparseCore 0:
  19.8 48.7 all-gather.4
  70.2 48.2 all-gather.2
  143.1 47.3 reduce-scatter.1

commit v3 on v1

v3 whole, which is shorter than its diff:
```python
import jax
import jax.numpy as jnp
from jax import lax
from jax.experimental import pallas as pl
from jax.experimental.pallas import tpu as pltpu
from jax.sharding import PartitionSpec as P

SPLIT = 16
SCALE = 2.5
QUAD = 4
bf16 = jnp.bfloat16
f32 = jnp.float32
CONTRACT0 = (((0,), (0,)), ((), ()))
CONTRACT1 = (((1,), (1,)), ((), ()))
VMEM = pl.BlockSpec(memory_space=pltpu.VMEM)


def chunk_of(size, limit):
    best = 128
    for step in range(128, limit + 1, 128):
        if size % step == 0:
            best = step
    return best


def slot_rows(blocks, first, count, columns):
    member = lax.rem(lax.axis_index("expert"), SPLIT) // QUAD
    own, far, up, down, end = [b[first : first + count, columns] for b in blocks]
    below = jnp.where(member == 0, end, up)
    above = jnp.where(member == SPLIT // QUAD - 1, end, down)
    return jnp.concatenate([own, far, below, above], axis=0)


def prep_kernel(held, capacity, *refs):
    gate, up, down, tokens, cotangent, logits, ids = refs[:7]
    gu_top, gu_low, dn_top, dn_low, mine, other, pick_out = refs[7:14]
    chosen_out, inv_w_out, inv_total_out, sems = refs[14:]
    half, wide = gu_top.shape
    ff = wide // 2
    rows, part = dn_top.shape
    core = lax.axis_index("dp")
    start = pl.multiple_of(core * part, 128)
    away = pl.multiple_of((1 - core) * part, 128)
    copies = []
    for side, (gu, dn) in enumerate(((gu_top, dn_top), (gu_low, dn_low))):
        at = pl.ds(pl.multiple_of(start + side * half, 128), half)
        pairs = (
            (gate.at[0, at, :], gu.at[:, :ff]),
            (up.at[0, at, :], gu.at[:, ff:]),
            (down.at[0, side * rows : (side + 1) * rows, pl.ds(start, part)], dn),
        )
        for i, (src, dst) in enumerate(pairs):
            copies.append(pltpu.make_async_copy(src, dst, sems.at[3 * side + i]))
    for copy in copies:
        copy.start()

    experts, count = logits.shape
    expert = lax.broadcasted_iota(jnp.int32, (experts, count), 0)
    has = expert == ids[0:1, :]
    for k in range(1, ids.shape[0]):
        has = has | (expert == ids[k : k + 1, :])
    chosen = jnp.where(has, jax.nn.sigmoid(logits[...]), 0.0)
    total = jnp.sum(chosen, axis=0, keepdims=True)
    weight = (SCALE * chosen / total).astype(bf16).astype(f32)
    before = lax.broadcasted_iota(jnp.int32, (count, count), 0)
    after = lax.broadcasted_iota(jnp.int32, (count, count), 1)
    earlier = jnp.where(before < after, 1.0, 0.0).astype(bf16)
    named = jnp.where(has, 1.0, 0.0)
    rank = jnp.dot(named.astype(bf16), earlier, preferred_element_type=f32)
    slots = held * capacity
    slot = lax.broadcasted_iota(jnp.int32, (slots, count), 0)
    pick = jnp.zeros((slots, count), f32)
    value = jnp.zeros((slots, count), f32)
    for e in range(held):
        place = rank[e : e + 1, :].astype(jnp.int32) + e * capacity
        hit = jnp.where(slot == place, named[e : e + 1, :], 0.0)
        pick = pick + hit
        value = value + hit * weight[e : e + 1, :]
    value = jnp.sum(value, axis=1, keepdims=True)
    pick = pick.astype(bf16)
    pick_out[...] = pick
    chosen_out[...] = chosen
    inv_w_out[...] = jnp.where(has & (expert < held), 1.0 / weight, 0.0)
    inv_total_out[...] = jnp.broadcast_to(1.0 / total, chosen.shape)

    step = chunk_of(part, 512)

    def body(k, carry):
        at = pl.multiple_of(k * step, 128)
        for base, out in ((start, mine), (away, other)):
            columns = pl.ds(pl.multiple_of(base + at, 128), step)
            x = jnp.dot(pick, tokens[:, columns], preferred_element_type=f32)
            c = jnp.dot(pick, cotangent[:, columns], preferred_element_type=f32)
            out[0, :, pl.ds(at, step)] = x.astype(bf16)
            out[1, :, pl.ds(at, step)] = (c * value).astype(bf16)
        return carry

    lax.fori_loop(0, part // step, body, 0)
    for copy in copies:
        copy.wait()


def sum_kernel(own, above, below, far, mine, other, tail):
    first = lax.axis_index("dp") == 0
    rows, part = mine.shape
    step = chunk_of(part, 512)

    def total(columns):
        value = own[:, columns].astype(f32) + above[:, columns].astype(f32)
        value = value + below[:, columns].astype(f32) + far[:, columns].astype(f32)
        top, low = value[:rows], value[rows:]
        return jnp.where(first, top, low), jnp.where(first, low, top)

    def body(k, carry):
        columns = pl.ds(pl.multiple_of(k * step, 128), step)
        here, there = total(columns)
        mine[:, columns] = here.astype(bf16)
        other[:, columns] = there.astype(bf16)
        return carry

    lax.fori_loop(0, part // step, body, 0)
    tail[...] = total(slice(part, part + 128))[0]


def gate_up_kernel(*refs):
    blocks, packs, out = refs[:5], refs[5:-1], refs[-1]
    half, wide = packs[0].shape
    count = out.shape[0] // (SPLIT // QUAD)
    step = chunk_of(half, 1024)
    out[...] = jnp.zeros_like(out)
    for side in range(2):

        def body(k, carry):
            at = pl.multiple_of(k * step, 128)
            columns = pl.ds(pl.multiple_of(side * half + k * step, 128), step)
            x = slot_rows(blocks, 0, count, columns)
            for q in range(QUAD):
                w = packs[2 * q + side][pl.ds(at, step), :]
                out[:, q * wide : (q + 1) * wide] += jnp.dot(x, w, preferred_element_type=f32)
            return carry

        lax.fori_loop(0, half // step, body, 0)


def proj_kernel(*refs):
    blocks, packs, out = refs[:5], refs[5:-1], refs[-1]
    part = packs[0].shape[1]
    count = out.shape[0] // (SPLIT // QUAD)
    step = chunk_of(part, 1024)
    out[...] = jnp.zeros_like(out)

    def body(k, carry):
        columns = pl.ds(pl.multiple_of(k * step, 128), step)
        rows = slot_rows(blocks, count, count, columns)
        w = jnp.concatenate([p[:, columns] for p in packs], axis=0)
        out[...] += lax.dot_general(rows, w, CONTRACT1, preferred_element_type=f32)
        return carry

    lax.fori_loop(0, part // step, body, 0)


def activations(mine, theirs, q, ff):
    base = 2 * q * ff
    g = mine[:, base : base + ff] + theirs[:, base : base + ff]
    u = mine[:, base + ff : base + 2 * ff] + theirs[:, base + ff : base + 2 * ff]
    sig = jax.nn.sigmoid(g)
    return g, u, sig, g * sig


def down_kernel(mine, theirs, *refs):
    blocks, outs, scratch = refs[:5], refs[5:-1], refs[-1]
    ff, part = outs[0].shape
    count = scratch.shape[1] // (SPLIT // QUAD)
    step = chunk_of(part, 512)
    for q in range(QUAD):
        g, u, sig, active = activations(mine, theirs, q, ff)
        hidden = (active * u).astype(bf16).astype(f32)
        scratch[q * ff : (q + 1) * ff, :] = hidden.T.astype(bf16)

    def body(k, carry):
        columns = pl.ds(pl.multiple_of(k * step, 128), step)
        rows = slot_rows(blocks, count, count, columns)
        grads = jnp.dot(scratch[...], rows, preferred_element_type=f32).astype(bf16)
        at = 0
        for out in outs:
            out[:, columns] = grads[at : at + out.shape[0]]
            at += out.shape[0]
        return carry

    lax.fori_loop(0, part // step, body, 0)


def back_kernel(mine, theirs, proj_mine, proj_theirs, *refs):
    packs, outs, scratch = refs[: 2 * QUAD], refs[2 * QUAD : -1], refs[-1]
    half, wide = packs[0].shape
    ff = wide // 2
    rows = outs[0].shape[0]
    step = chunk_of(half, 256)
    dots = 0.0
    for q in range(QUAD):
        g, u, sig, active = activations(mine, theirs, q, ff)
        proj = proj_mine[:, q * ff : (q + 1) * ff] + proj_theirs[:, q * ff : (q + 1) * ff]
        hidden = (active * u).astype(bf16).astype(f32)
        dots = dots + jnp.sum(hidden * proj, axis=1, keepdims=True)
        base = 2 * q * ff
        scratch[:, base : base + ff] = (proj * u * sig * (1.0 + g * (1.0 - sig))).astype(bf16)
        scratch[:, base + ff : base + 2 * ff] = (proj * active).astype(bf16)

    def write(values, columns):
        for i, out in enumerate(outs):
            out[:, columns] = values[i * rows : (i + 1) * rows].astype(bf16)

    high = dots.astype(bf16).astype(f32)
    rest = dots - high
    lane = lax.broadcasted_iota(jnp.int32, (dots.shape[0], 128), 1)
    tail = slice(2 * half, 2 * half + 128)
    write(jnp.where(lane == 0, high, jnp.where(lane == 1, rest, 0.0)), tail)
    for side in range(2):

        def body(k, carry):
            at = pl.multiple_of(k * step, 128)
            columns = pl.ds(pl.multiple_of(side * half + k * step, 128), step)
            w = jnp.concatenate(
                [packs[2 * q + side][pl.ds(at, step), :] for q in range(QUAD)], axis=1
            )
            grads = lax.dot_general(scratch[...], w, CONTRACT1, preferred_element_type=f32)
            write(grads, columns)
            return carry

        lax.fori_loop(0, half // step, body, 0)


def final_kernel(held, pick, mine, theirs, tail, chosen, inv_w, inv_total, tok_out, logit_out):
    core = lax.axis_index("dp")
    slots, part = mine.shape
    step = chunk_of(part, 512)
    pick_t = pick[...]

    def body(k, carry):
        at = pl.multiple_of(k * step, 128)
        for source, side in ((mine, core), (theirs, 1 - core)):
            block = lax.dot_general(
                pick_t, source[:, pl.ds(at, step)], CONTRACT0, preferred_element_type=f32
            )
            tok_out[:, pl.ds(pl.multiple_of(side * part + at, 128), step)] = block.astype(bf16)
        return carry

    lax.fori_loop(0, part // step, body, 0)
    values = jnp.sum(tail[...], axis=1, keepdims=True)
    entries = pick_t.astype(f32) * values
    full = chosen.shape
    expert = lax.broadcasted_iota(jnp.int32, full, 0)
    slot = lax.broadcasted_iota(jnp.int32, entries.shape, 0)
    capacity = slots // held
    dw = jnp.zeros(full, f32)
    for e in range(held):
        inside = (slot >= e * capacity) & (slot < (e + 1) * capacity)
        found = jnp.sum(jnp.where(inside, entries, 0.0), axis=0, keepdims=True)
        dw = jnp.where(expert == e, jnp.broadcast_to(found, full), dw)
    dw = dw * inv_w[...]
    share = chosen[...]
    inner = jnp.sum(dw * share, axis=0, keepdims=True) * inv_total[...]
    logit_out[...] = SCALE * inv_total[...] * (dw - inner) * share * (1.0 - share)


def call(kernel, outs, in_specs, scratch, flops, moved, limit=40):
    return pl.pallas_call(
        kernel,
        out_shape=outs,
        in_specs=in_specs,
        out_specs=[VMEM] * len(outs),
        scratch_shapes=scratch,
        compiler_params=pltpu.CompilerParams(vmem_limit_bytes=limit * 1024 * 1024),
        cost_estimate=pl.CostEstimate(flops=flops, bytes_accessed=moved, transcendentals=0),
    )


def per_device(tokens, cotangent, logits, expert_ids, gate_proj, up_proj, down_proj):
    devices = lax.axis_size("expert")
    cores = lax.axis_size("dp")
    core = lax.axis_index("dp")
    held = devices // SPLIT
    tok_count, top = expert_ids.shape
    experts = logits.shape[1]
    width = tokens.shape[1]
    ff = gate_proj.shape[2]
    part = width // cores
    capacity = max(2, 5 * tok_count * top // (4 * experts))
    members = SPLIT // QUAD
    last = members - 1
    rows_dev = held * capacity
    rows_chip = cores * rows_dev
    slots = members * rows_chip
    across = [[e * SPLIT + j for e in range(held)] for j in range(SPLIT)]
    swap1 = [(i, i ^ 1) for i in range(devices)]
    swap2 = [(i, i ^ 2) for i in range(devices)]
    sibling = [(c, cores - 1 - c) for c in range(cores)]
    barrier = lax.optimization_barrier

    def send(array, route):
        return lax.ppermute(array, "expert", route)

    def line(pairs):
        return [
            (e * SPLIT + a * QUAD + q, e * SPLIT + b * QUAD + q)
            for e in range(held)
            for a, b in pairs
            for q in range(QUAD)
        ]

    upward = line([(m, m + 1) for m in range(last)])
    downward = line([(m + 1, m) for m in range(last)])
    distant = line([(m, m ^ 2) for m in range(members)])

    low, lowf = part // 2, ff // 2
    shape = jax.ShapeDtypeStruct
    gu_t, gu_b, dn_t, dn_b, mine, other, pick, chosen, inv_w, inv_total = call(
        lambda *refs: prep_kernel(held, capacity, *refs),
        [shape((low, 2 * ff), bf16)] * 2
        + [shape((lowf, part), bf16)] * 2
        + [shape((2, rows_dev, part), bf16)] * 2
        + [shape((rows_dev, tok_count), bf16)]
        + [shape((experts, tok_count), f32)] * 3,
        [pl.BlockSpec(memory_space=pltpu.HBM)] * 3 + [VMEM] * 4,
        [pltpu.SemaphoreType.DMA((6,))],
        4 * rows_dev * tok_count * width,
        12 * part * ff + 4 * tok_count * width,
        limit=58,
    )(gate_proj, up_proj, down_proj, tokens, cotangent, logits.T, expert_ids.T)
    gu1b = send(gu_b, swap1)
    gu2t = send(gu_t, swap2)

    theirs = lax.ppermute(other, "dp", sibling)
    own = jnp.concatenate(
        [
            jnp.where(core == (0 if side == 0 else cores - 1), mine[i], theirs[i])
            for i in range(2)
            for side in range(cores)
        ],
        axis=0,
    )
    if held > 1:
        own = own.reshape(2, cores, held, capacity, part)
        own = lax.all_to_all(own, "expert", 2, 2, axis_index_groups=across, tiled=True)
        own = own.reshape(2 * rows_chip, part)
    far = send(own, distant)
    up = send(own, upward)
    down = send(own, downward)

    gu_t, gu_b, gu1b, gu2t, own = barrier((gu_t, gu_b, gu1b, gu2t, own))
    gu1t = send(gu_t, swap1)
    gu2b = send(gu_b, swap2)
    gu1b, gu2t, gu1t, gu2b = barrier((gu1b, gu2t, gu1t, gu2b))
    gu3t = send(gu2t, swap1)
    gu3b = send(gu1b, swap2)
    end = send(far, line([(2, 3), (1, 0)]))
    dn_t, dn_b, gu3t, gu3b = barrier((dn_t, dn_b, gu3t, gu3b))
    dn1b = send(dn_b, swap1)
    dn2t = send(dn_t, swap2)
    dn_t, dn_b, dn1b, dn2t = barrier((dn_t, dn_b, dn1b, dn2t))
    dn1t = send(dn_t, swap1)
    dn2b = send(dn_b, swap2)
    dn3t = send(dn2t, swap1)
    dn3b = send(dn1b, swap2)
    gu = [gu_t, gu_b, gu1t, gu1b, gu2t, gu2b, gu3t, gu3b]
    dn = [dn_t, dn_b, dn1t, dn1b, dn2t, dn2b, dn3t, dn3b]
    blocks = [own, far, up, down, end]

    matmul = 2 * slots * part * QUAD * ff
    (g_u,) = call(
        gate_up_kernel,
        [shape((slots, QUAD * 2 * ff), f32)],
        [VMEM] * 13,
        [],
        2 * matmul,
        2 * part * (slots + QUAD * 2 * ff),
    )(*blocks, *gu)
    g_u_sib = lax.ppermute(g_u, "dp", sibling)
    (proj,) = call(
        proj_kernel,
        [shape((slots, QUAD * ff), f32)],
        [VMEM] * 13,
        [],
        matmul,
        2 * part * (slots + QUAD * ff),
    )(*blocks, *dn)
    proj_sib = lax.ppermute(proj, "dp", sibling)
    g0, g1, g2, g3a, g3b = call(
        down_kernel,
        [shape((ff, part), bf16)] * 3
        + [shape((lowf, part), bf16)] * 2,
        [VMEM] * 7,
        [pltpu.VMEM((QUAD * ff, slots), bf16)],
        matmul,
        2 * part * (slots + QUAD * ff),
    )(g_u, g_u_sib, *blocks)
    g0, g3a, g3b, proj, proj_sib = barrier((g0, g3a, g3b, proj, proj_sib))
    r3a = send(g3a, swap1)
    r3b = send(g3b, swap2)
    b0, b1, b2, b3 = call(
        back_kernel,
        [shape((rows_chip, part + 128), bf16)] * members,
        [VMEM] * 12,
        [pltpu.VMEM((slots, QUAD * 2 * ff), bf16)],
        2 * matmul,
        2 * part * (slots + QUAD * 2 * ff),
    )(g_u, g_u_sib, proj, proj_sib, *gu)

    from_above = send(b2, line([(m, (m - 1) % members) for m in range(members)]))
    from_below = send(b3, line([(m, (m + 1) % members) for m in range(members)]))
    from_far = send(b1, distant)

    from_above, r3a, r3b = barrier((from_above, r3a, r3b))
    r1 = send(jnp.concatenate([g1[:lowf], g1[lowf:] + r3b], axis=0), swap1)
    r2 = send(jnp.concatenate([g2[:lowf] + r3a, g2[lowf:]], axis=0), swap2)
    down_grad = (g0.astype(f32) + r1.astype(f32) + r2.astype(f32)).astype(bf16)[None]

    mine, other, tail = call(
        sum_kernel,
        [shape((rows_dev, part), bf16)] * 2 + [shape((rows_dev, 128), f32)],
        [VMEM] * 4,
        [],
        4 * rows_chip * part,
        12 * rows_chip * part,
    )(b0, from_above, from_below, from_far)
    if held > 1:
        mine, other, tail = [
            lax.all_to_all(
                array.reshape(held, capacity, array.shape[1]),
                "expert",
                0,
                0,
                axis_index_groups=across,
                tiled=True,
            ).reshape(array.shape)
            for array in (mine, other, tail)
        ]
    theirs = lax.ppermute(other, "dp", sibling)
    token_grad, logit_grad = call(
        lambda *refs: final_kernel(held, *refs),
        [
            shape((tok_count, width), bf16),
            shape((experts, tok_count), f32),
        ],
        [VMEM] * 7,
        [],
        2 * tok_count * rows_dev * width,
        2 * width * (tok_count + rows_dev),
    )(pick, mine, theirs, tail, chosen, inv_w, inv_total)
    return (token_grad, logit_grad.T, down_grad)


def solution(mesh):
    in_specs = (
        P(("expert", "dp"), None),
        P(("expert", "dp"), None),
        P(("expert", "dp"), None),
        P(("expert", "dp"), None),
        P("expert", None, None),
        P("expert", None, None),
        P("expert", None, None),
    )
    out_specs = (P(("expert", "dp"), None), P(("expert", "dp"), None), P("expert", None, "dp"))
    return jax.shard_map(
        per_device, mesh=mesh, in_specs=in_specs, out_specs=out_specs, check_vma=False
    )
```

time: 374 us -> 221 us (0.59)
  waiting for transfers between devices: 269 us -> 151 us
  starting transfers between devices: 4.67 us -> 41.9 us
  blocking collectives: 35.5 us -> 0 us
  matrix products: 29.5 us -> 0 us
  Pallas kernels: 0 us -> 23.8 us
  local copies, waits for them, and re-layouts: 15.6 us -> 0.03 us
  between operations: 15 us -> 0.83 us
    all_gather x4 -> x0, waiting for transfers between devices: 155 us -> none  [the longest x2 153 us: gather(): lax.all_gather(block, 'expert', axis_index_groups=within, axis=0, tiled=T...]
    ppermute x3 -> x27, waiting for transfers between devices: 68.3 us -> 151 us  [the longest x23 149 us: send(): return lax.ppermute(array, 'expert', route)]
    reduce_scatter x2 -> x0, waiting for transfers between devices: 45.4 us -> none  [the longest x1 45.3 us: per_device(): lax.psum_scatter(back.reshape(members * held, capacity, width), 'expert',...]
    ppermute x3 -> x27, starting transfers between devices: 4.43 us -> 41.9 us  [the longest x23 41.2 us: send(): return lax.ppermute(array, 'expert', route)]
    unnamed x1 -> x0, blocking collectives: 35.5 us -> none
    dot_general x10 -> x0, matrix products: 29.5 us -> none  [the longest x1 5.01 us: per_device(): proj = lax.dot_general(sc, dn, contract, preferred_element_type=jnp.float32)]
    pallas_call x0 -> x7, Pallas kernels: none -> 23.8 us  [the longest x1 5.78 us: per_device(): call(lambda *refs: prep_kernel(held, capacity, *refs), [shape((low, 2 * f...]
    unnamed x24 -> x16, local copies, waits for them, and re-layouts: 7.19 us -> 0.03 us
  transfers between devices with their start and end apart: 9 -> 27, of which waited for: 7 -> 14; matrix products, arithmetic and copies ran while one was open for 9% -> 1% of each run, Pallas kernels for 0% -> 6%
where the time goes in v3:
time: 221 us; the launch traced here: 220 us
  waiting for transfers between devices  151 us (68%)
  starting transfers between devices  41.9 us (19%)
  Pallas kernels  23.8 us (11%)
  other arithmetic  3 us (1%)
    ppermute x23, waiting for transfers between devices, send(): return lax.ppermute(array, 'expert', route)  149 us
    ppermute x23, starting transfers between devices, send(): return lax.ppermute(array, 'expert', route)  41.2 us
    pallas_call x1, Pallas kernels, per_device(): call(lambda *refs: prep_kernel(held, capacity, *refs), [shape((low, 2 * f...  5.78 us
    pallas_call x1, Pallas kernels, per_device(): call(back_kernel, [shape((rows_chip, part + 128), bf16)] * members, [VMEM...  5.69 us
  transfers between devices with their start and end apart: 27, of which 14 were waited for; matrix products, arithmetic and copies ran while one was open for 1% of the time, Pallas kernels for 6%

profile of v3, /device:TPU:0, one launch (start us, length us, event | category | flops | bytes accessed | tf_op | source)
XLA Modules:
  0.0 220.3 jit_solution(13218571048069531455)
XLA Ops:
  0.6 5.8 %shard_map.94 = (bf16[1792,256]{1,0:T(8,128)(2,1)}, bf16[1792,256]{1,0:T(8,128)(2,1)}, bf16[64,3584]{1,0:T(8,128)(2,1)}, bf16[64,3584]{1,0:T(8,128)(2,1)}, bf16[...) custom-call(bf16[1,7168,128]{2,1,0:T(8,128)(2,1)} %refs_0_.1, ...), custom_call_target="tpu_custom_call" | custom-call | flops 146800640 | bytes 9175040 | tf_op jit(solution)/shard_map/pallas_call | solution.py:317
  6.4 0.5 collective-permute-start.2
  6.9 2.6 %collective-permute-start.1 = (bf16[1792,256]{1,0:T(8,128)(2,1)}, bf16[1792,256]{1,0:T(8,128)(2,1)S(1)}, u32[]{:S(2)}, u32[]{:S(2)}) collective-permute-start(bf16[1792,256]{1,0:T(8,128)(2,1)} %get-tuple-element.58.refs_5_.refs_0_), channel_id=1, source_target_pairs={{0,4},{2,6},{4,0},{6,2},{8,12},{10,14},{12,8},{14,10},{16,20},{18,... | collective-permute-start | bytes 2752520 | tf_op jit(solution)/shard_map/ppermute | solution.py:301
  9.5 1.5 collective-permute-start
  11.0 0.0 collective-permute-done.2
  11.1 1.3 select_bitcast_fusion.3
  12.3 0.1 pad_maximum_fusion.refs_0_
  12.4 2.7 %collective-permute-start.3 = (bf16[160,3584]{1,0:T(8,128)(2,1)S(1)}, bf16[160,3584]{1,0:T(8,128)(2,1)S(1)}, u32[]{:S(2)}, u32[]{:S(2)}) collective-permute-start(bf16[160,3584]{1,0:T(8,128)(2,1)S(1)} %pad_maximum_fusion.refs_0_), channel_id=1, source_target_pairs={{0,16},{2,18},{4,20},{6,22},{8,24},{10,26},{12,28},{14,30},{16,0},... | collective-permute-start | bytes 3440648 | tf_op jit(solution)/shard_map/ppermute | solution.py:301
  15.1 15.6 %collective-permute-done.1.refs_9_.refs_4_ = bf16[1792,256]{1,0:T(8,128)(2,1)S(1)} collective-permute-done((bf16[1792,256]{1,0:T(8,128)(2,1)}, bf16[1792,256]{1,0:T(8,128)(2,1)S(1)}, u32[]{:S(2)}, u32[]{:S(2)}) %collective-permute-start.1) | collective-permute-done | bytes 917536 | tf_op jit(solution)/shard_map/ppermute | solution.py:301
  30.7 1.5 collective-permute-done.refs_8_.refs_3_
  32.2 1.5 collective-permute-start.7
  33.7 0.5 collective-permute-start.8
  34.2 1.3 collective-permute-start.5
  35.5 4.6 %collective-permute-start.4 = (bf16[160,3584]{1,0:T(8,128)(2,1)S(1)}, bf16[160,3584]{1,0:T(8,128)(2,1)S(1)}, u32[]{:S(2)}, u32[]{:S(2)}) collective-permute-start(bf16[160,3584]{1,0:T(8,128)(2,1)S(1)} %pad_maximum_fusion.refs_0_), channel_id=1, source_target_pairs={{0,8},{2,10},{4,12},{6,14},{8,16},{10,18},{12,20},{14,22},{16,24},... | collective-permute-start | bytes 3440648 | tf_op jit(solution)/shard_map/ppermute | solution.py:301
  40.1 26.1 %collective-permute-done.3.refs_1_ = bf16[160,3584]{1,0:T(8,128)(2,1)S(1)} collective-permute-done((bf16[160,3584]{1,0:T(8,128)(2,1)S(1)}, bf16[160,3584]{1,0:T(8,128)(2,1)S(1)}, u32[]{:S(2)}, u32[]{:S(2)}) %collective-permute-start.3) | collective-permute-done | bytes 1146912 | tf_op jit(solution)/shard_map/ppermute | solution.py:301
  66.2 1.3 collective-permute-start.6
  67.4 0.0 collective-permute-done.7.refs_7_.refs_2_
  67.5 0.0 collective-permute-done.8.refs_10_.refs_5_
  67.5 0.6 collective-permute-start.10
  68.1 1.5 collective-permute-start.9
  69.6 18.1 %collective-permute-done.10.refs_12_.refs_7_ = bf16[1792,256]{1,0:T(8,128)(2,1)S(1)} collective-permute-done((bf16[1792,256]{1,0:T(8,128)(2,1)S(1)}, bf16[1792,256]{1,0:T(8,128)(2,1)S(1)}, u32[]{:S(2)}, u32[]{:S(2)}) %collective-permute-start.10) | collective-permute-done | bytes 917536 | tf_op jit(solution)/shard_map/ppermute | solution.py:301
  87.7 0.8 collective-permute-done.9.refs_11_.refs_6_
  88.6 0.9 collective-permute-start.13
  89.5 1.1 collective-permute-start.12
  90.6 0.0 collective-permute-done.5.refs_3_
  90.6 0.0 collective-permute-done.4.refs_2_
  90.6 19.6 %collective-permute-done.6.refs_4_ = bf16[160,3584]{1,0:T(8,128)(2,1)S(1)} collective-permute-done((bf16[160,3584]{1,0:T(8,128)(2,1)S(1)}, bf16[160,3584]{1,0:T(8,128)(2,1)S(1)}, u32[]{:S(2)}, u32[]{:S(2)}) %collective-permute-start.6) | collective-permute-done | bytes 1146912 | tf_op jit(solution)/shard_map/ppermute | solution.py:301
  110.2 3.5 %shard_map.95.mine = f32[320,1024]{1,0:T(8,128)S(1)} custom-call(bf16[160,3584]{1,0:T(8,128)(2,1)S(1)} %pad_maximum_fusion.refs_0_, bf16[160,3584]{1,0:T(8,128)(2,1)S(1)} %collective-permute-done.3.refs_1_, bf16[160,3584]{1,0:T(8,128)(2,1)S(1)} %collective-permute-done.4.refs_2_, bf16[160,3584]{1,0:T(8,128)(2,1)S(1)} %collective-permute-done.5.refs_3_, ...), custom_call_target="tpu_custom_call" | custom-call | flops 2348810240 | bytes 9633792 | tf_op jit(solution)/shard_map/pallas_call | solution.py:370
  113.7 0.1 collective-permute-start.11
  113.8 0.0 collective-permute-done.13.refs_9_
  113.8 0.0 collective-permute-done.12.refs_8_
  113.8 0.6 collective-permute-start.14
  114.4 1.4 collective-permute-start.15
  115.8 0.6 collective-permute-start.17
  116.4 1.5 collective-permute-start.16
  117.9 9.3 %collective-permute-done.14.refs_7_ = bf16[64,3584]{1,0:T(8,128)(2,1)S(1)} collective-permute-done((bf16[64,3584]{1,0:T(8,128)(2,1)S(1)}, bf16[64,3584]{1,0:T(8,128)(2,1)S(1)}, u32[]{:S(2)}, u32[]{:S(2)}) %collective-permute-start.14) | collective-permute-done | bytes 458784 | tf_op jit(solution)/shard_map/ppermute | solution.py:301
  127.2 0.6 collective-permute-done.15.refs_10_
  127.7 9.0 %collective-permute-done.17.refs_12_ = bf16[64,3584]{1,0:T(8,128)(2,1)S(1)} collective-permute-done((bf16[64,3584]{1,0:T(8,128)(2,1)S(1)}, bf16[64,3584]{1,0:T(8,128)(2,1)S(1)}, u32[]{:S(2)}, u32[]{:S(2)}) %collective-permute-start.17) | collective-permute-done | bytes 458784 | tf_op jit(solution)/shard_map/ppermute | solution.py:301
  136.8 0.0 collective-permute-done.16.refs_11_
  136.8 2.2 shard_map.97.proj_mine
  139.0 0.1 collective-permute-start.18
  139.1 0.0 collective-permute-done.11.theirs
  139.1 3.2 %shard_map.96 = (bf16[128,3584]{1,0:T(8,128)(2,1)S(1)}, bf16[128,3584]{1,0:T(8,128)(2,1)S(1)}, bf16[128,3584]{1,0:T(8,128)(2,1)S(1)}, bf16[64,3584]{1,0:T(8,128)(2,1)S(1)}, bf16[64,3584]{1,0:T(8,128)(2,1)S(1)}) custom-call(f32[320,1024]{1,0:T(8,128)S(1)} %shard_map.95.mine, f32[320,1024]{1,0:T(8,128)S(1)} %collective-permute-done.11.theirs, ...), custom_call_target="tpu_custom_call" | custom-call | flops 1174405120 | bytes 5963776 | tf_op jit(solution)/shard_map/pallas_call | solution.py:388
  142.3 5.7 %shard_map.98 = (bf16[80,3712]{1,0:T(8,128)(2,1)S(1)}, bf16[80,3712]{1,0:T(8,128)(2,1)S(1)}, bf16[80,3712]{1,0:T(8,128)(2,1)S(1)}, bf16[80,3712]{1,0:T(8,128)(2,1)S(1)}) custom-call(f32[320,1024]{1,0:T(8,128)S(1)} %shard_map.95.mine, f32[320,1024]{1,0:T(8,128)S(1)} %collective-permute-done.11.theirs, f32[320,512]{1,0:T(8,128)S(1)} %shard_map.97.proj_mine, ...), custom_call_target="tpu_custom_call" | custom-call | flops 2348810240 | bytes 9633792 | tf_op jit(solution)/shard_map/pallas_call | solution.py:400
  148.0 6.9 %collective-permute-start.19 = (bf16[80,3712]{1,0:T(8,128)(2,1)S(1)}, bf16[80,3712]{1,0:T(8,128)(2,1)S(1)}, u32[]{:S(2)}, u32[]{:S(2)}) collective-permute-start(bf16[80,3712]{1,0:T(8,128)(2,1)S(1)} %get-tuple-element.82), channel_id=1, source_target_pairs={{0,24},{2,26},{4,28},{6,30},{8,0},{10,2},{12,4},{14,6},{16,8},{18,... | collective-permute-start | bytes 1781768 | tf_op jit(solution)/shard_map/ppermute | solution.py:301
  154.9 1.4 collective-permute-start.20
  156.3 1.4 collective-permute-start.21
  157.7 9.8 %collective-permute-done.20 = bf16[64,3584]{1,0:T(8,128)(2,1)S(1)} collective-permute-done((bf16[64,3584]{1,0:T(8,128)(2,1)S(1)}, bf16[64,3584]{1,0:T(8,128)(2,1)S(1)}, u32[]{:S(2)}, u32[]{:S(2)}) %collective-permute-start.20) | collective-permute-done | bytes 458784 | tf_op jit(solution)/shard_map/ppermute | solution.py:301
  167.5 1.2 collective-permute-done.21
  168.7 0.1 slice_add_fusion
  168.8 0.1 pad_maximum_fusion.1
  168.9 1.0 collective-permute-start.25
  169.9 0.1 pad_maximum_fusion.2
  170.0 1.5 collective-permute-start.26
  171.5 0.0 collective-permute-start.22
  171.5 4.8 %collective-permute-start.23 = (bf16[80,3712]{1,0:T(8,128)(2,1)S(1)}, bf16[80,3712]{1,0:T(8,128)(2,1)S(1)}, u32[]{:S(2)}, u32[]{:S(2)}) collective-permute-start(bf16[80,3712]{1,0:T(8,128)(2,1)S(1)} %get-tuple-element.87), channel_id=1, source_target_pairs={{0,16},{2,18},{4,20},{6,22},{8,24},{10,26},{12,28},{14,30},{16,0},... | collective-permute-start | bytes 1781768 | tf_op jit(solution)/shard_map/ppermute | solution.py:301
  176.3 13.9 %collective-permute-done.22.below = bf16[80,3712]{1,0:T(8,128)(2,1)S(1)} collective-permute-done((bf16[80,3712]{1,0:T(8,128)(2,1)S(1)}, bf16[80,3712]{1,0:T(8,128)(2,1)S(1)}, u32[]{:S(2)}, u32[]{:S(2)}) %collective-permute-start.22) | collective-permute-done | bytes 593952 | tf_op jit(solution)/shard_map/ppermute | solution.py:301
  190.2 23.8 %collective-permute-done.23.far = bf16[80,3712]{1,0:T(8,128)(2,1)S(1)} collective-permute-done((bf16[80,3712]{1,0:T(8,128)(2,1)S(1)}, bf16[80,3712]{1,0:T(8,128)(2,1)S(1)}, u32[]{:S(2)}, u32[]{:S(2)}) %collective-permute-start.23) | collective-permute-done | bytes 593952 | tf_op jit(solution)/shard_map/ppermute | solution.py:301
  214.0 0.4 shard_map.99
  214.3 0.1 collective-permute-start.24
  214.4 1.6 collective-permute-done.24.refs_2_
  216.0 3.0 %shard_map.100 = (bf16[128,7168]{1,0:T(8,128)(2,1)}, f32[32,128]{1,0:T(8,128)}) custom-call(bf16[40,128]{1,0:T(8,128)(2,1)S(1)} %copy-done.7, bf16[40,3584]{1,0:T(8,128)(2,1)S(1)} %get-tuple-element.88.refs_1_, bf16[40,3584]{1,0:T(8,128)(2,1)S(1)} %collective-permute-done.24.refs_2_, f32[40,128]{1,0:T(8,128)S(1)} %get-tuple-element.90.refs_3_, ...), custom_call_target="tpu_custom_call" | custom-call | flops 73400320 | bytes 2408448 | tf_op jit(solution)/shard_map/pallas_call | solution.py:439
  219.0 0.0 collective-permute-done.25
  219.0 1.3 fusion
  (19 shorter events, 0.0 us)
Async XLA Ops:
  6.4 4.6 %collective-permute-start.2 = (bf16[2,40,3584]{2,1,0:T(8,128)(2,1)}, bf16[2,40,3584]{2,1,0:T(8,128)(2,1)S(1)}, u32[]{:S(2)}, u32[]{:S(2)}) collective-permute-start(bf16[2,40,3584]{2,1,0:T(8,128)(2,1)} %get-tuple-element.56), channel_id=1, source_target_pairs={{0,1},{1,0},{2,3},{3,2},{4,5},{5,4},{6,7},{7,6},{8,9},{9,8},{10,11... | collective-permute-start | bytes 1720328 | tf_op jit(solution)/shard_map/ppermute | solution.py:333
  6.9 23.7 %collective-permute-start.1 = (bf16[1792,256]{1,0:T(8,128)(2,1)}, bf16[1792,256]{1,0:T(8,128)(2,1)S(1)}, u32[]{:S(2)}, u32[]{:S(2)}) collective-permute-start(bf16[1792,256]{1,0:T(8,128)(2,1)} %get-tuple-element.58.refs_5_.refs_0_), channel_id=1, source_target_pairs={{0,4},{2,6},{4,0},{6,2},{8,12},{10,14},{12,8},{14,10},{16,20},{18,... | collective-permute-start | bytes 2752520 | tf_op jit(solution)/shard_map/ppermute | solution.py:301
  9.5 22.6 %collective-permute-start = (bf16[1792,256]{1,0:T(8,128)(2,1)}, bf16[1792,256]{1,0:T(8,128)(2,1)S(1)}, u32[]{:S(2)}, u32[]{:S(2)}) collective-permute-start(bf16[1792,256]{1,0:T(8,128)(2,1)} %get-tuple-element.59.refs_6_.refs_1_), channel_id=1, source_target_pairs={{0,2},{2,0},{4,6},{6,4},{8,10},{10,8},{12,14},{14,12},{16,18},{18,... | collective-permute-start | bytes 2752520 | tf_op jit(solution)/shard_map/ppermute | solution.py:301
  11.0 21.1 %copy-start = (bf16[1792,256]{1,0:T(8,128)(2,1)S(1)}, bf16[1792,256]{1,0:T(8,128)(2,1)}, u32[]{:S(2)}) copy-start(bf16[1792,256]{1,0:T(8,128)(2,1)} %get-tuple-element.58.refs_5_.refs_0_) | copy-start | bytes 2752516
  11.0 22.6 %copy-start.1 = (bf16[1792,256]{1,0:T(8,128)(2,1)S(1)}, bf16[1792,256]{1,0:T(8,128)(2,1)}, u32[]{:S(2)}) copy-start(bf16[1792,256]{1,0:T(8,128)(2,1)} %get-tuple-element.59.refs_6_.refs_1_) | copy-start | bytes 2752516
  11.0 77.5 %copy-start.2 = (bf16[64,3584]{1,0:T(8,128)(2,1)S(1)}, bf16[64,3584]{1,0:T(8,128)(2,1)}, u32[]{:S(2)}) copy-start(bf16[64,3584]{1,0:T(8,128)(2,1)} %get-tuple-element.75.refs_5_) | copy-start | bytes 1376260
  11.0 78.4 %copy-start.3 = (bf16[64,3584]{1,0:T(8,128)(2,1)S(1)}, bf16[64,3584]{1,0:T(8,128)(2,1)}, u32[]{:S(2)}) copy-start(bf16[64,3584]{1,0:T(8,128)(2,1)} %get-tuple-element.76.refs_6_) | copy-start | bytes 1376260
  12.4 53.7 %collective-permute-start.3 = (bf16[160,3584]{1,0:T(8,128)(2,1)S(1)}, bf16[160,3584]{1,0:T(8,128)(2,1)S(1)}, u32[]{:S(2)}, u32[]{:S(2)}) collective-permute-start(bf16[160,3584]{1,0:T(8,128)(2,1)S(1)} %pad_maximum_fusion.refs_0_), channel_id=1, source_target_pairs={{0,16},{2,18},{4,20},{6,22},{8,24},{10,26},{12,28},{14,30},{16,0},... | collective-permute-start | bytes 3440648 | tf_op jit(solution)/shard_map/ppermute | solution.py:301
  32.2 35.3 %collective-permute-start.7 = (bf16[1792,256]{1,0:T(8,128)(2,1)S(1)}, bf16[1792,256]{1,0:T(8,128)(2,1)S(1)}, u32[]{:S(2)}, u32[]{:S(2)}) collective-permute-start(bf16[1792,256]{1,0:T(8,128)(2,1)S(1)} %copy-done), channel_id=1, source_target_pairs={{0,2},{2,0},{4,6},{6,4},{8,10},{10,8},{12,14},{14,12},{16,18},{18,... | collective-permute-start | bytes 2752520 | tf_op jit(solution)/shard_map/ppermute | solution.py:301
  33.7 33.8 %collective-permute-start.8 = (bf16[1792,256]{1,0:T(8,128)(2,1)S(1)}, bf16[1792,256]{1,0:T(8,128)(2,1)S(1)}, u32[]{:S(2)}, u32[]{:S(2)}) collective-permute-start(bf16[1792,256]{1,0:T(8,128)(2,1)S(1)} %copy-done.1), channel_id=1, source_target_pairs={{0,4},{2,6},{4,0},{6,2},{8,12},{10,14},{12,8},{14,10},{16,20},{18,... | collective-permute-start | bytes 2752520 | tf_op jit(solution)/shard_map/ppermute | solution.py:301
  34.2 56.4 %collective-permute-start.5 = (bf16[160,3584]{1,0:T(8,128)(2,1)S(1)}, bf16[160,3584]{1,0:T(8,128)(2,1)S(1)}, u32[]{:S(2)}, u32[]{:S(2)}) collective-permute-start(bf16[160,3584]{1,0:T(8,128)(2,1)S(1)} %pad_maximum_fusion.refs_0_), channel_id=1, source_target_pairs={{8,0},{10,2},{12,4},{14,6},{16,8},{18,10},{20,12},{22,14},{24,16},... | collective-permute-start | bytes 3440648 | tf_op jit(solution)/shard_map/ppermute | solution.py:301
  35.5 55.1 %collective-permute-start.4 = (bf16[160,3584]{1,0:T(8,128)(2,1)S(1)}, bf16[160,3584]{1,0:T(8,128)(2,1)S(1)}, u32[]{:S(2)}, u32[]{:S(2)}) collective-permute-start(bf16[160,3584]{1,0:T(8,128)(2,1)S(1)} %pad_maximum_fusion.refs_0_), channel_id=1, source_target_pairs={{0,8},{2,10},{4,12},{6,14},{8,16},{10,18},{12,20},{14,22},{16,24},... | collective-permute-start | bytes 3440648 | tf_op jit(solution)/shard_map/ppermute | solution.py:301
  66.2 44.0 %collective-permute-start.6 = (bf16[160,3584]{1,0:T(8,128)(2,1)S(1)}, bf16[160,3584]{1,0:T(8,128)(2,1)S(1)}, u32[]{:S(2)}, u32[]{:S(2)}) collective-permute-start(bf16[160,3584]{1,0:T(8,128)(2,1)S(1)} %collective-permute-done.3.refs_1_), channel_id=1, source_target_pairs={{16,24},{18,26},{20,28},{22,30},{8,0},{10,2},{12,4},{14,6},{17,25}... | collective-permute-start | bytes 3440648 | tf_op jit(solution)/shard_map/ppermute | solution.py:301
  67.5 20.3 %collective-permute-start.10 = (bf16[1792,256]{1,0:T(8,128)(2,1)S(1)}, bf16[1792,256]{1,0:T(8,128)(2,1)S(1)}, u32[]{:S(2)}, u32[]{:S(2)}) collective-permute-start(bf16[1792,256]{1,0:T(8,128)(2,1)S(1)} %collective-permute-done.refs_8_.refs_3_), channel_id=1, source_target_pairs={{0,4},{2,6},{4,0},{6,2},{8,12},{10,14},{12,8},{14,10},{16,20},{18,... | collective-permute-start | bytes 2752520 | tf_op jit(solution)/shard_map/ppermute | solution.py:301
  68.1 20.5 %collective-permute-start.9 = (bf16[1792,256]{1,0:T(8,128)(2,1)S(1)}, bf16[1792,256]{1,0:T(8,128)(2,1)S(1)}, u32[]{:S(2)}, u32[]{:S(2)}) collective-permute-start(bf16[1792,256]{1,0:T(8,128)(2,1)S(1)} %collective-permute-done.1.refs_9_.refs_4_), channel_id=1, source_target_pairs={{0,2},{2,0},{4,6},{6,4},{8,10},{10,8},{12,14},{14,12},{16,18},{18,... | collective-permute-start | bytes 2752520 | tf_op jit(solution)/shard_map/ppermute | solution.py:301
  88.6 25.2 %collective-permute-start.13 = (bf16[64,3584]{1,0:T(8,128)(2,1)S(1)}, bf16[64,3584]{1,0:T(8,128)(2,1)S(1)}, u32[]{:S(2)}, u32[]{:S(2)}) collective-permute-start(bf16[64,3584]{1,0:T(8,128)(2,1)S(1)} %copy-done.2), channel_id=1, source_target_pairs={{0,4},{2,6},{4,0},{6,2},{8,12},{10,14},{12,8},{14,10},{16,20},{18,... | collective-permute-start | bytes 1376264 | tf_op jit(solution)/shard_map/ppermute | solution.py:301
  89.5 24.3 %collective-permute-start.12 = (bf16[64,3584]{1,0:T(8,128)(2,1)S(1)}, bf16[64,3584]{1,0:T(8,128)(2,1)S(1)}, u32[]{:S(2)}, u32[]{:S(2)}) collective-permute-start(bf16[64,3584]{1,0:T(8,128)(2,1)S(1)} %copy-done.3), channel_id=1, source_target_pairs={{0,2},{2,0},{4,6},{6,4},{8,10},{10,8},{12,14},{14,12},{16,18},{18,... | collective-permute-start | bytes 1376264 | tf_op jit(solution)/shard_map/ppermute | solution.py:301
  113.7 25.4 %collective-permute-start.11 = (f32[320,1024]{1,0:T(8,128)S(1)}, f32[320,1024]{1,0:T(8,128)S(1)}, u32[]{:S(2)}, u32[]{:S(2)}) collective-permute-start(f32[320,1024]{1,0:T(8,128)S(1)} %shard_map.95.mine), channel_id=1, source_target_pairs={{0,1},{1,0},{2,3},{3,2},{4,5},{5,4},{6,7},{7,6},{8,9},{9,8},{10,11... | collective-permute-start | bytes 3932168 | tf_op jit(solution)/shard_map/ppermute | solution.py:378
  113.8 13.4 %collective-permute-start.14 = (bf16[64,3584]{1,0:T(8,128)(2,1)S(1)}, bf16[64,3584]{1,0:T(8,128)(2,1)S(1)}, u32[]{:S(2)}, u32[]{:S(2)}) collective-permute-start(bf16[64,3584]{1,0:T(8,128)(2,1)S(1)} %copy-done.2), channel_id=1, source_target_pairs={{0,2},{2,0},{4,6},{6,4},{8,10},{10,8},{12,14},{14,12},{16,18},{18,... | collective-permute-start | bytes 1376264 | tf_op jit(solution)/shard_map/ppermute | solution.py:301
  114.4 13.4 %collective-permute-start.15 = (bf16[64,3584]{1,0:T(8,128)(2,1)S(1)}, bf16[64,3584]{1,0:T(8,128)(2,1)S(1)}, u32[]{:S(2)}, u32[]{:S(2)}) collective-permute-start(bf16[64,3584]{1,0:T(8,128)(2,1)S(1)} %copy-done.3), channel_id=1, source_target_pairs={{0,4},{2,6},{4,0},{6,2},{8,12},{10,14},{12,8},{14,10},{16,20},{18,... | collective-permute-start | bytes 1376264 | tf_op jit(solution)/shard_map/ppermute | solution.py:301
  115.8 21.0 %collective-permute-start.17 = (bf16[64,3584]{1,0:T(8,128)(2,1)S(1)}, bf16[64,3584]{1,0:T(8,128)(2,1)S(1)}, u32[]{:S(2)}, u32[]{:S(2)}) collective-permute-start(bf16[64,3584]{1,0:T(8,128)(2,1)S(1)} %collective-permute-done.12.refs_8_), channel_id=1, source_target_pairs={{0,4},{2,6},{4,0},{6,2},{8,12},{10,14},{12,8},{14,10},{16,20},{18,... | collective-permute-start | bytes 1376264 | tf_op jit(solution)/shard_map/ppermute | solution.py:301
  116.4 20.4 %collective-permute-start.16 = (bf16[64,3584]{1,0:T(8,128)(2,1)S(1)}, bf16[64,3584]{1,0:T(8,128)(2,1)S(1)}, u32[]{:S(2)}, u32[]{:S(2)}) collective-permute-start(bf16[64,3584]{1,0:T(8,128)(2,1)S(1)} %collective-permute-done.13.refs_9_), channel_id=1, source_target_pairs={{0,2},{2,0},{4,6},{6,4},{8,10},{10,8},{12,14},{14,12},{16,18},{18,... | collective-permute-start | bytes 1376264 | tf_op jit(solution)/shard_map/ppermute | solution.py:301
  139.0 3.3 %collective-permute-start.18 = (f32[320,512]{1,0:T(8,128)S(1)}, f32[320,512]{1,0:T(8,128)S(1)}, u32[]{:S(2)}, u32[]{:S(2)}) collective-permute-start(f32[320,512]{1,0:T(8,128)S(1)} %shard_map.97.proj_mine), channel_id=1, source_target_pairs={{0,1},{1,0},{2,3},{3,2},{4,5},{5,4},{6,7},{7,6},{8,9},{9,8},{10,11... | collective-permute-start | bytes 1966088 | tf_op jit(solution)/shard_map/ppermute | solution.py:387
  148.0 20.6 %collective-permute-start.19 = (bf16[80,3712]{1,0:T(8,128)(2,1)S(1)}, bf16[80,3712]{1,0:T(8,128)(2,1)S(1)}, u32[]{:S(2)}, u32[]{:S(2)}) collective-permute-start(bf16[80,3712]{1,0:T(8,128)(2,1)S(1)} %get-tuple-element.82), channel_id=1, source_target_pairs={{0,24},{2,26},{4,28},{6,30},{8,0},{10,2},{12,4},{14,6},{16,8},{18,... | collective-permute-start | bytes 1781768 | tf_op jit(solution)/shard_map/ppermute | solution.py:301
  154.9 12.6 %collective-permute-start.20 = (bf16[64,3584]{1,0:T(8,128)(2,1)S(1)}, bf16[64,3584]{1,0:T(8,128)(2,1)S(1)}, u32[]{:S(2)}, u32[]{:S(2)}) collective-permute-start(bf16[64,3584]{1,0:T(8,128)(2,1)S(1)} %get-tuple-element.83), channel_id=1, source_target_pairs={{0,2},{2,0},{4,6},{6,4},{8,10},{10,8},{12,14},{14,12},{16,18},{18,... | collective-permute-start | bytes 1376264 | tf_op jit(solution)/shard_map/ppermute | solution.py:301
  156.3 12.4 %collective-permute-start.21 = (bf16[64,3584]{1,0:T(8,128)(2,1)S(1)}, bf16[64,3584]{1,0:T(8,128)(2,1)S(1)}, u32[]{:S(2)}, u32[]{:S(2)}) collective-permute-start(bf16[64,3584]{1,0:T(8,128)(2,1)S(1)} %get-tuple-element.84), channel_id=1, source_target_pairs={{0,4},{2,6},{4,0},{6,2},{8,12},{10,14},{12,8},{14,10},{16,20},{18,... | collective-permute-start | bytes 1376264 | tf_op jit(solution)/shard_map/ppermute | solution.py:301
  168.9 50.1 %collective-permute-start.25 = (bf16[128,3584]{1,0:T(8,128)(2,1)S(1)}, bf16[128,3584]{1,0:T(8,128)(2,1)S(1)}, u32[]{:S(2)}, u32[]{:S(2)}) collective-permute-start(bf16[128,3584]{1,0:T(8,128)(2,1)S(1)} %pad_maximum_fusion.1), channel_id=1, source_target_pairs={{0,2},{2,0},{4,6},{6,4},{8,10},{10,8},{12,14},{14,12},{16,18},{18,... | collective-permute-start | bytes 2752520 | tf_op jit(solution)/shard_map/ppermute | solution.py:301
  169.9 46.0 %copy-start.4 = (f32[32,128]{1,0:T(8,128)S(1)}, f32[32,128]{1,0:T(8,128)}, u32[]{:S(2)}) copy-start(f32[32,128]{1,0:T(8,128)} %get-tuple-element.91.refs_4_) | copy-start | bytes 49156
  169.9 46.0 %copy-start.5 = (f32[32,128]{1,0:T(8,128)S(1)}, f32[32,128]{1,0:T(8,128)}, u32[]{:S(2)}) copy-start(f32[32,128]{1,0:T(8,128)} %get-tuple-element.92.refs_5_) | copy-start | bytes 49156
  169.9 46.0 %copy-start.6 = (f32[32,128]{1,0:T(8,128)S(1)}, f32[32,128]{1,0:T(8,128)}, u32[]{:S(2)}) copy-start(f32[32,128]{1,0:T(8,128)} %get-tuple-element.93.refs_6_) | copy-start | bytes 49156
  169.9 46.0 %copy-start.7 = (bf16[40,128]{1,0:T(8,128)(2,1)S(1)}, bf16[40,128]{1,0:T(8,128)(2,1)}, u32[]{:S(2)}) copy-start(bf16[40,128]{1,0:T(8,128)(2,1)} %get-tuple-element.52.refs_0_) | copy-start | bytes 30724
  170.0 49.0 %collective-permute-start.26 = (bf16[128,3584]{1,0:T(8,128)(2,1)S(1)}, bf16[128,3584]{1,0:T(8,128)(2,1)S(1)}, u32[]{:S(2)}, u32[]{:S(2)}) collective-permute-start(bf16[128,3584]{1,0:T(8,128)(2,1)S(1)} %pad_maximum_fusion.2), channel_id=1, source_target_pairs={{0,4},{2,6},{4,0},{6,2},{8,12},{10,14},{12,8},{14,10},{16,20},{18,... | collective-permute-start | bytes 2752520 | tf_op jit(solution)/shard_map/ppermute | solution.py:301
  171.5 18.7 %collective-permute-start.22 = (bf16[80,3712]{1,0:T(8,128)(2,1)S(1)}, bf16[80,3712]{1,0:T(8,128)(2,1)S(1)}, u32[]{:S(2)}, u32[]{:S(2)}) collective-permute-start(bf16[80,3712]{1,0:T(8,128)(2,1)S(1)} %get-tuple-element.86), channel_id=1, source_target_pairs={{0,8},{2,10},{4,12},{6,14},{8,16},{10,18},{12,20},{14,22},{16,24},... | collective-permute-start | bytes 1781768 | tf_op jit(solution)/shard_map/ppermute | solution.py:301
  171.5 42.5 %collective-permute-start.23 = (bf16[80,3712]{1,0:T(8,128)(2,1)S(1)}, bf16[80,3712]{1,0:T(8,128)(2,1)S(1)}, u32[]{:S(2)}, u32[]{:S(2)}) collective-permute-start(bf16[80,3712]{1,0:T(8,128)(2,1)S(1)} %get-tuple-element.87), channel_id=1, source_target_pairs={{0,16},{2,18},{4,20},{6,22},{8,24},{10,26},{12,28},{14,30},{16,0},... | collective-permute-start | bytes 1781768 | tf_op jit(solution)/shard_map/ppermute | solution.py:301
  214.3 1.6 collective-permute-start.24

commit v4 on v3

--- a/solution.py
+++ b/solution.py
@@ -23,34 +23,49 @@
     return best
 
 
+def inner_chip():
+    member = lax.rem(lax.axis_index("expert"), SPLIT) // QUAD
+    return (member > 0) & (member < SPLIT // QUAD - 1)
+
+
 def slot_rows(blocks, first, count, columns):
-    member = lax.rem(lax.axis_index("expert"), SPLIT) // QUAD
-    own, far, up, down, end = [b[first : first + count, columns] for b in blocks]
-    below = jnp.where(member == 0, end, up)
-    above = jnp.where(member == SPLIT // QUAD - 1, end, down)
-    return jnp.concatenate([own, far, below, above], axis=0)
+    own, far, ends, outer, middle = [b[first : first + count, columns] for b in blocks]
+    return jnp.concatenate([own, far, ends, jnp.where(inner_chip(), middle, outer)], axis=0)
+
+
+def split_of(total):
+    return total // 2 // 256 * 256
 
 
 def prep_kernel(held, capacity, *refs):
     gate, up, down, tokens, cotangent, logits, ids = refs[:7]
-    gu_top, gu_low, dn_top, dn_low, mine, other, pick_out = refs[7:14]
-    chosen_out, inv_w_out, inv_total_out, sems = refs[14:]
-    half, wide = gu_top.shape
-    ff = wide // 2
-    rows, part = dn_top.shape
+    weights, top, low, mine, other, pick_out = refs[7:13]
+    chosen_out, inv_w_out, inv_total_out, sems = refs[13:]
+    ff = gate.shape[2]
+    part = mine.shape[2]
+    wide = 2 * ff
     core = lax.axis_index("dp")
     start = pl.multiple_of(core * part, 128)
     away = pl.multiple_of((1 - core) * part, 128)
-    copies = []
-    for side, (gu, dn) in enumerate(((gu_top, dn_top), (gu_low, dn_low))):
-        at = pl.ds(pl.multiple_of(start + side * half, 128), half)
-        pairs = (
-            (gate.at[0, at, :], gu.at[:, :ff]),
-            (up.at[0, at, :], gu.at[:, ff:]),
-            (down.at[0, side * rows : (side + 1) * rows, pl.ds(start, part)], dn),
-        )
-        for i, (src, dst) in enumerate(pairs):
-            copies.append(pltpu.make_async_copy(src, dst, sems.at[3 * side + i]))
+    split = top.shape[0]
+    rest = part - split
+    pairs = []
+    for out, at, first, size in (
+        (weights, 0, 0, part),
+        (top, 0, 0, split),
+        (low, 0, split, rest),
+    ):
+        rows = pl.ds(pl.multiple_of(start + first, 128), size)
+        pairs.append((gate.at[0, rows, :], out.at[at : at + size, :ff]))
+        pairs.append((up.at[0, rows, :], out.at[at : at + size, ff:]))
+    for c in range(part // wide):
+        columns = pl.ds(pl.multiple_of(start + c * wide, 128), wide)
+        for out, at in ((weights, part), (low, rest)):
+            rows = slice(at + c * ff, at + (c + 1) * ff)
+            pairs.append((down.at[0, :, columns], out.at[rows, :]))
+    copies = [
+        pltpu.make_async_copy(src, dst, sems.at[i]) for i, (src, dst) in enumerate(pairs)
+    ]
     for copy in copies:
         copy.start()
 
@@ -100,14 +115,16 @@
         copy.wait()
 
 
-def sum_kernel(own, above, below, far, mine, other, tail):
+def sum_kernel(own, far, ends, outer, middle, mine, other, tail):
     first = lax.axis_index("dp") == 0
+    inner = inner_chip()
     rows, part = mine.shape
     step = chunk_of(part, 512)
 
     def total(columns):
-        value = own[:, columns].astype(f32) + above[:, columns].astype(f32)
-        value = value + below[:, columns].astype(f32) + far[:, columns].astype(f32)
+        near = jnp.where(inner, 0.0, ends[:, columns].astype(f32))
+        value = own[:, columns].astype(f32) + far[:, columns].astype(f32) + near
+        value = value + outer[:, columns].astype(f32) + middle[:, columns].astype(f32)
         top, low = value[:rows], value[rows:]
         return jnp.where(first, top, low), jnp.where(first, low, top)
 
@@ -122,41 +139,57 @@
     tail[...] = total(slice(part, part + 128))[0]
 
 
+def piece_sides(pieces):
+    split = pieces[2].shape[0]
+    upper = [(pieces[0], 0), (pieces[1], 0), (pieces[2], 0), (pieces[4], 0)]
+    lower = [(pieces[0], split), (pieces[1], split), (pieces[3], 0), (pieces[5], 0)]
+    return split, upper, lower
+
+
 def gate_up_kernel(*refs):
-    blocks, packs, out = refs[:5], refs[5:-1], refs[-1]
-    half, wide = packs[0].shape
+    blocks, pieces, out = refs[:5], refs[5:-1], refs[-1]
+    wide = pieces[0].shape[1]
+    part = blocks[0].shape[1]
     count = out.shape[0] // (SPLIT // QUAD)
-    step = chunk_of(half, 1024)
+    split, upper, lower = piece_sides(pieces)
     out[...] = jnp.zeros_like(out)
-    for side in range(2):
+    for side, first, size in ((upper, 0, split), (lower, split, part - split)):
+        step = chunk_of(size, 1024)
 
         def body(k, carry):
-            at = pl.multiple_of(k * step, 128)
-            columns = pl.ds(pl.multiple_of(side * half + k * step, 128), step)
+            columns = pl.ds(pl.multiple_of(first + k * step, 128), step)
             x = slot_rows(blocks, 0, count, columns)
-            for q in range(QUAD):
-                w = packs[2 * q + side][pl.ds(at, step), :]
+            for q, (ref, base) in enumerate(side):
+                w = ref[pl.ds(pl.multiple_of(base + k * step, 128), step), :]
                 out[:, q * wide : (q + 1) * wide] += jnp.dot(x, w, preferred_element_type=f32)
             return carry
 
-        lax.fori_loop(0, half // step, body, 0)
+        lax.fori_loop(0, size // step, body, 0)
 
 
 def proj_kernel(*refs):
-    blocks, packs, out = refs[:5], refs[5:-1], refs[-1]
-    part = packs[0].shape[1]
+    blocks, pieces, out = refs[:5], refs[5:-1], refs[-1]
+    wide = pieces[0].shape[1]
+    ff = wide // 2
+    part = blocks[0].shape[1]
     count = out.shape[0] // (SPLIT // QUAD)
-    step = chunk_of(part, 1024)
+    split, upper, lower = piece_sides(pieces)
     out[...] = jnp.zeros_like(out)
 
     def body(k, carry):
-        columns = pl.ds(pl.multiple_of(k * step, 128), step)
+        columns = pl.ds(pl.multiple_of(k * wide, 128), wide)
         rows = slot_rows(blocks, count, count, columns)
-        w = jnp.concatenate([p[:, columns] for p in packs], axis=0)
+        w = jnp.concatenate(
+            [
+                ref[pl.ds(pl.multiple_of(base + part - split + k * ff, 128), ff), :]
+                for ref, base in lower
+            ],
+            axis=0,
+        )
         out[...] += lax.dot_general(rows, w, CONTRACT1, preferred_element_type=f32)
         return carry
 
-    lax.fori_loop(0, part // step, body, 0)
+    lax.fori_loop(0, part // wide, body, 0)
 
 
 def activations(mine, theirs, q, ff):
@@ -169,7 +202,9 @@
 
 def down_kernel(mine, theirs, *refs):
     blocks, outs, scratch = refs[:5], refs[5:-1], refs[-1]
-    ff, part = outs[0].shape
+    own, sent1, sent2, kept1, kept2 = outs
+    ff, part = own.shape
+    half = ff // 2
     count = scratch.shape[1] // (SPLIT // QUAD)
     step = chunk_of(part, 512)
     for q in range(QUAD):
@@ -181,21 +216,25 @@
         columns = pl.ds(pl.multiple_of(k * step, 128), step)
         rows = slot_rows(blocks, count, count, columns)
         grads = jnp.dot(scratch[...], rows, preferred_element_type=f32).astype(bf16)
-        at = 0
-        for out in outs:
-            out[:, columns] = grads[at : at + out.shape[0]]
-            at += out.shape[0]
+        g0, g1, g2, g3 = [grads[q * ff : (q + 1) * ff] for q in range(QUAD)]
+        own[:, columns] = g0
+        sent1[:, columns] = jnp.concatenate([g3[:half], g1[:half]], axis=0)
+        sent2[:, columns] = jnp.concatenate([g3[half:], g2[half:]], axis=0)
+        kept1[:, columns] = g1[half:]
+        kept2[:, columns] = g2[:half]
         return carry
 
     lax.fori_loop(0, part // step, body, 0)
 
 
 def back_kernel(mine, theirs, proj_mine, proj_theirs, *refs):
-    packs, outs, scratch = refs[: 2 * QUAD], refs[2 * QUAD : -1], refs[-1]
-    half, wide = packs[0].shape
+    members = SPLIT // QUAD
+    pieces, outs, scratch = refs[: -members - 1], refs[-members - 1 : -1], refs[-1]
+    wide = pieces[0].shape[1]
     ff = wide // 2
     rows = outs[0].shape[0]
-    step = chunk_of(half, 256)
+    part = outs[0].shape[1] - 128
+    split, upper, lower = piece_sides(pieces)
     dots = 0.0
     for q in range(QUAD):
         g, u, sig, active = activations(mine, theirs, q, ff)
@@ -206,28 +245,30 @@
         scratch[:, base : base + ff] = (proj * u * sig * (1.0 + g * (1.0 - sig))).astype(bf16)
         scratch[:, base + ff : base + 2 * ff] = (proj * active).astype(bf16)
 
-    def write(values, columns):
-        for i, out in enumerate(outs):
-            out[:, columns] = values[i * rows : (i + 1) * rows].astype(bf16)
-
     high = dots.astype(bf16).astype(f32)
     rest = dots - high
-    lane = lax.broadcasted_iota(jnp.int32, (dots.shape[0], 128), 1)
-    tail = slice(2 * half, 2 * half + 128)
-    write(jnp.where(lane == 0, high, jnp.where(lane == 1, rest, 0.0)), tail)
-    for side in range(2):
+    lane = lax.broadcasted_iota(jnp.int32, (rows, 128), 1)
+    for i, out in enumerate(outs):
+        at = 2 if i == 2 else 0
+        top, low = high[i * rows : (i + 1) * rows], rest[i * rows : (i + 1) * rows]
+        out[:, part : part + 128] = jnp.where(
+            lane == at, top, jnp.where(lane == at + 1, low, 0.0)
+        ).astype(bf16)
+    for side, first, size in ((upper, 0, split), (lower, split, part - split)):
+        step = chunk_of(size, 256)
 
         def body(k, carry):
-            at = pl.multiple_of(k * step, 128)
-            columns = pl.ds(pl.multiple_of(side * half + k * step, 128), step)
+            columns = pl.ds(pl.multiple_of(first + k * step, 128), step)
             w = jnp.concatenate(
-                [packs[2 * q + side][pl.ds(at, step), :] for q in range(QUAD)], axis=1
+                [ref[pl.ds(pl.multiple_of(base + k * step, 128), step), :] for ref, base in side],
+                axis=1,
             )
             grads = lax.dot_general(scratch[...], w, CONTRACT1, preferred_element_type=f32)
-            write(grads, columns)
+            for i, out in enumerate(outs):
+                out[:, columns] = grads[i * rows : (i + 1) * rows].astype(bf16)
             return carry
 
-        lax.fori_loop(0, half // step, body, 0)
+        lax.fori_loop(0, size // step, body, 0)
 
 
 def final_kernel(held, pick, mine, theirs, tail, chosen, inv_w, inv_total, tok_out, logit_out):
@@ -263,12 +304,12 @@
     logit_out[...] = SCALE * inv_total[...] * (dw - inner) * share * (1.0 - share)
 
 
-def call(kernel, outs, in_specs, scratch, flops, moved, limit=40):
+def call(kernel, outs, in_specs, scratch, flops, moved, limit=40, out_specs=None):
     return pl.pallas_call(
         kernel,
         out_shape=outs,
         in_specs=in_specs,
-        out_specs=[VMEM] * len(outs),
+        out_specs=out_specs or [VMEM] * len(outs),
         scratch_shapes=scratch,
         compiler_params=pltpu.CompilerParams(vmem_limit_bytes=limit * 1024 * 1024),
         cost_estimate=pl.CostEstimate(flops=flops, bytes_accessed=moved, transcendentals=0),
@@ -287,7 +328,6 @@
     part = width // cores
     capacity = max(2, 5 * tok_count * top // (4 * experts))
     members = SPLIT // QUAD
-    last = members - 1
     rows_dev = held * capacity
     rows_chip = cores * rows_dev
     slots = members * rows_chip
@@ -308,27 +348,33 @@
             for q in range(QUAD)
         ]
 
-    upward = line([(m, m + 1) for m in range(last)])
-    downward = line([(m + 1, m) for m in range(last)])
     distant = line([(m, m ^ 2) for m in range(members)])
-
-    low, lowf = part // 2, ff // 2
+    outward = line([(1, 0), (2, 3)])
+    inward = line([(0, 1), (3, 2)])
+    middle_swap = line([(1, 2), (2, 1)])
+    inner = inner_chip()
+
+    lowf = ff // 2
+    packed = part + part // 2
+    split = split_of(packed)
     shape = jax.ShapeDtypeStruct
-    gu_t, gu_b, dn_t, dn_b, mine, other, pick, chosen, inv_w, inv_total = call(
+    hbm = pl.BlockSpec(memory_space=pltpu.HBM)
+    weights, w_top, w_low, mine, other, pick, chosen, inv_w, inv_total = call(
         lambda *refs: prep_kernel(held, capacity, *refs),
-        [shape((low, 2 * ff), bf16)] * 2
-        + [shape((lowf, part), bf16)] * 2
+        [shape((size, 2 * ff), bf16) for size in (packed, split, packed - split)]
         + [shape((2, rows_dev, part), bf16)] * 2
         + [shape((rows_dev, tok_count), bf16)]
         + [shape((experts, tok_count), f32)] * 3,
-        [pl.BlockSpec(memory_space=pltpu.HBM)] * 3 + [VMEM] * 4,
-        [pltpu.SemaphoreType.DMA((6,))],
+        [hbm] * 3 + [VMEM] * 4,
+        [pltpu.SemaphoreType.DMA((6 + part // ff,))],
         4 * rows_dev * tok_count * width,
         12 * part * ff + 4 * tok_count * width,
         limit=58,
+        out_specs=[hbm] * 3 + [VMEM] * 6,
     )(gate_proj, up_proj, down_proj, tokens, cotangent, logits.T, expert_ids.T)
-    gu1b = send(gu_b, swap1)
-    gu2t = send(gu_t, swap2)
+    w1 = send(weights, swap1)
+    w2_top = send(w_top, swap2)
+    w2_low = send(w_low, swap2)
 
     theirs = lax.ppermute(other, "dp", sibling)
     own = jnp.concatenate(
@@ -344,85 +390,76 @@
         own = lax.all_to_all(own, "expert", 2, 2, axis_index_groups=across, tiled=True)
         own = own.reshape(2 * rows_chip, part)
     far = send(own, distant)
-    up = send(own, upward)
-    down = send(own, downward)
-
-    gu_t, gu_b, gu1b, gu2t, own = barrier((gu_t, gu_b, gu1b, gu2t, own))
-    gu1t = send(gu_t, swap1)
-    gu2b = send(gu_b, swap2)
-    gu1b, gu2t, gu1t, gu2b = barrier((gu1b, gu2t, gu1t, gu2b))
-    gu3t = send(gu2t, swap1)
-    gu3b = send(gu1b, swap2)
-    end = send(far, line([(2, 3), (1, 0)]))
-    dn_t, dn_b, gu3t, gu3b = barrier((dn_t, dn_b, gu3t, gu3b))
-    dn1b = send(dn_b, swap1)
-    dn2t = send(dn_t, swap2)
-    dn_t, dn_b, dn1b, dn2t = barrier((dn_t, dn_b, dn1b, dn2t))
-    dn1t = send(dn_t, swap1)
-    dn2b = send(dn_b, swap2)
-    dn3t = send(dn2t, swap1)
-    dn3b = send(dn1b, swap2)
-    gu = [gu_t, gu_b, gu1t, gu1b, gu2t, gu2b, gu3t, gu3b]
-    dn = [dn_t, dn_b, dn1t, dn1b, dn2t, dn2b, dn3t, dn3b]
-    blocks = [own, far, up, down, end]
+    outer = send(own, outward)
+    w1, w2_top, w2_low, own, far, outer = barrier((w1, w2_top, w2_low, own, far, outer))
+    w3_top = send(w2_top, swap1)
+    w3_low = send(w1[split:], swap2)
+    ends = send(jnp.where(inner, far, own), outward + inward)
+    middle = send(own, middle_swap)
+    w = [weights, w1, w2_top, w2_low, w3_top, w3_low]
+    blocks = [own, far, ends, outer, middle]
 
     matmul = 2 * slots * part * QUAD * ff
     (g_u,) = call(
         gate_up_kernel,
         [shape((slots, QUAD * 2 * ff), f32)],
-        [VMEM] * 13,
+        [VMEM] * 11,
         [],
         2 * matmul,
         2 * part * (slots + QUAD * 2 * ff),
-    )(*blocks, *gu)
+    )(*blocks, *w)
     g_u_sib = lax.ppermute(g_u, "dp", sibling)
     (proj,) = call(
         proj_kernel,
         [shape((slots, QUAD * ff), f32)],
-        [VMEM] * 13,
+        [VMEM] * 11,
         [],
         matmul,
         2 * part * (slots + QUAD * ff),
-    )(*blocks, *dn)
+    )(*blocks, *w)
     proj_sib = lax.ppermute(proj, "dp", sibling)
-    g0, g1, g2, g3a, g3b = call(
+    g0, sent1, sent2, kept1, kept2 = call(
         down_kernel,
-        [shape((ff, part), bf16)] * 3
-        + [shape((lowf, part), bf16)] * 2,
+        [shape((ff, part), bf16)] * 3 + [shape((lowf, part), bf16)] * 2,
         [VMEM] * 7,
         [pltpu.VMEM((QUAD * ff, slots), bf16)],
         matmul,
         2 * part * (slots + QUAD * ff),
     )(g_u, g_u_sib, *blocks)
-    g0, g3a, g3b, proj, proj_sib = barrier((g0, g3a, g3b, proj, proj_sib))
-    r3a = send(g3a, swap1)
-    r3b = send(g3b, swap2)
+    g0, sent1, sent2, proj, proj_sib = barrier((g0, sent1, sent2, proj, proj_sib))
+    got1 = send(sent1, swap1)
+    got2 = send(sent2, swap2)
     b0, b1, b2, b3 = call(
         back_kernel,
         [shape((rows_chip, part + 128), bf16)] * members,
-        [VMEM] * 12,
+        [VMEM] * 10,
         [pltpu.VMEM((slots, QUAD * 2 * ff), bf16)],
         2 * matmul,
         2 * part * (slots + QUAD * 2 * ff),
-    )(g_u, g_u_sib, proj, proj_sib, *gu)
-
-    from_above = send(b2, line([(m, (m - 1) % members) for m in range(members)]))
-    from_below = send(b3, line([(m, (m + 1) % members) for m in range(members)]))
-    from_far = send(b1, distant)
-
-    from_above, r3a, r3b = barrier((from_above, r3a, r3b))
-    r1 = send(jnp.concatenate([g1[:lowf], g1[lowf:] + r3b], axis=0), swap1)
-    r2 = send(jnp.concatenate([g2[:lowf] + r3a, g2[lowf:]], axis=0), swap2)
-    down_grad = (g0.astype(f32) + r1.astype(f32) + r2.astype(f32)).astype(bf16)[None]
-
+    )(g_u, g_u_sib, proj, proj_sib, *w)
+
+    ends = send(b2, outward + inward)
+    middle = send(b3, middle_swap)
+    ends, middle, got1, got2, b1, b3 = barrier((ends, middle, got1, got2, b1, b3))
+    joined = b1 + jnp.where(inner, ends, jnp.zeros((), bf16))
+    joined, got1, got2 = barrier((joined, got1, got2))
+    far = send(joined, distant)
+    outer = send(b3, inward)
+    got3 = send(kept1 + got2[:lowf], swap1)
+    got4 = send(kept2 + got1[:lowf], swap2)
     mine, other, tail = call(
         sum_kernel,
         [shape((rows_dev, part), bf16)] * 2 + [shape((rows_dev, 128), f32)],
-        [VMEM] * 4,
+        [VMEM] * 5,
         [],
-        4 * rows_chip * part,
+        matmul,
         12 * rows_chip * part,
-    )(b0, from_above, from_below, from_far)
+    )(b0, far, ends, outer, middle)
+    other, got3, got4 = barrier((other, got3, got4))
+    add = lambda a, b, c: (a.astype(f32) + b.astype(f32) + c.astype(f32)).astype(bf16)
+    down_grad = jnp.concatenate(
+        [add(g0[:lowf], got1[lowf:], got4), add(g0[lowf:], got2[lowf:], got3)], axis=0
+    )[None]
     if held > 1:
         mine, other, tail = [
             lax.all_to_all(

time: 221 us -> 353 us (1.60)
  Pallas kernels: 23.8 us -> 201 us
  waiting for transfers between devices: 151 us -> 118 us
  starting transfers between devices: 41.9 us -> 28.1 us
    pallas_call x3, Pallas kernels: 11.5 us -> 186 us  [the longest x1 171 us: per_device(): call(lambda *refs: prep_kernel(held, capacity, *refs), [shape((size, 2 *...]
    ppermute x23 -> x17, waiting for transfers between devices: 149 us -> 118 us  [send(): return lax.ppermute(array, 'expert', route)]
    ppermute x23 -> x17, starting transfers between devices: 41.2 us -> 26.9 us  [send(): return lax.ppermute(array, 'expert', route)]
  transfers between devices with their start and end apart: 27 -> 21, of which waited for: 14 -> 8; matrix products, arithmetic and copies ran while one was open for 1% -> 1% of each run, Pallas kernels for 6% -> 5%
where the time goes in v4:
time: 353 us
  Pallas kernels  201 us (57%)
  waiting for transfers between devices  118 us (33%)
  starting transfers between devices  28.1 us (8%)
    pallas_call x1, Pallas kernels, per_device(): call(lambda *refs: prep_kernel(held, capacity, *refs), [shape((size, 2 *...  171 us
    ppermute x17, waiting for transfers between devices, send(): return lax.ppermute(array, 'expert', route)  118 us
    ppermute x17, starting transfers between devices, send(): return lax.ppermute(array, 'expert', route)  26.9 us
    pallas_call x1, Pallas kernels, per_device(): call(back_kernel, [shape((rows_chip, part + 128), bf16)] * members, [VMEM...  8.3 us
    pallas_call x1, Pallas kernels, per_device(): call(proj_kernel, [shape((slots, QUAD * ff), f32)], [VMEM] * 11, [], matm...  7.31 us
  transfers between devices with their start and end apart: 21, of which 8 were waited for; matrix products, arithmetic and copies ran while one was open for 1% of the time, Pallas kernels for 5%

profile of v4, /device:TPU:0, one launch (start us, length us, event | category | flops | bytes accessed | tf_op | source)
XLA Modules:
  0.0 352.9 jit_solution(1782643491932133935)
XLA Ops:
  0.6 171.2 %shard_map.94 = (bf16[5376,256]{1,0:T(8,128)(2,1)}, bf16[2560,256]{1,0:T(8,128)(2,1)}, bf16[2816,256]{1,0:T(8,128)(2,1)}, bf16[2,40,3584]{2,1,0:T(8,128)(2,1)}, ...) custom-call(bf16[1,7168,128]{2,1,0:T(8,128)(2,1)} %refs_0_.1, ...), custom_call_target="tpu_custom_call" | custom-call | flops 146800640 | bytes 9175040 | tf_op jit(solution)/shard_map/pallas_call | solution.py:362
  171.9 0.5 collective-permute-start.3
  172.4 2.6 collective-permute-start
  175.0 1.6 collective-permute-start.1
  176.5 0.5 collective-permute-start.2
  177.0 0.0 collective-permute-done.3
  177.0 1.1 select_bitcast_fusion.3
  178.1 0.1 pad_maximum_fusion.refs_0_
  178.2 2.7 collective-permute-start.4
  180.9 1.3 collective-permute-start.5
  182.2 24.7 %collective-permute-done.1.refs_7_.refs_2_ = bf16[2560,256]{1,0:T(8,128)(2,1)} collective-permute-done((bf16[2560,256]{1,0:T(8,128)(2,1)}, bf16[2560,256]{1,0:T(8,128)(2,1)}, u32[]{:S(2)}, u32[]{:S(2)}) %collective-permute-start.1) | collective-permute-done | bytes 1310752 | tf_op jit(solution)/shard_map/ppermute | solution.py:341
  206.9 30.1 %collective-permute-done.2.refs_8_.refs_3_ = bf16[2816,256]{1,0:T(8,128)(2,1)} collective-permute-done((bf16[2816,256]{1,0:T(8,128)(2,1)}, bf16[2816,256]{1,0:T(8,128)(2,1)}, u32[]{:S(2)}, u32[]{:S(2)}) %collective-permute-start.2) | collective-permute-done | bytes 1441824 | tf_op jit(solution)/shard_map/ppermute | solution.py:341
  237.0 0.0 collective-permute-done.4.refs_1_
  237.0 0.0 collective-permute-done.5.refs_3_
  237.0 0.0 collective-permute-done.refs_6_.refs_1_
  237.0 0.4 collective-permute-start.8
  237.4 1.5 slice.41
  238.9 1.8 collective-permute-start.9
  240.7 0.1 broadcast_select_fusion
  240.8 1.6 collective-permute-start.6
  242.4 0.7 collective-permute-start.7
  243.2 23.6 %collective-permute-done.6.refs_2_ = bf16[160,3584]{1,0:T(8,128)(2,1)S(1)} collective-permute-done((bf16[160,3584]{1,0:T(8,128)(2,1)S(1)}, bf16[160,3584]{1,0:T(8,128)(2,1)S(1)}, u32[]{:S(2)}, u32[]{:S(2)}) %collective-permute-start.6) | collective-permute-done | bytes 1146912 | tf_op jit(solution)/shard_map/ppermute | solution.py:341
  266.8 0.0 collective-permute-done.7.refs_4_
  266.8 0.5 collective-permute-done.8.refs_9_.refs_4_
  267.3 4.4 %collective-permute-done.9.refs_10_.refs_5_ = bf16[2816,256]{1,0:T(8,128)(2,1)S(1)} collective-permute-done((bf16[2816,256]{1,0:T(8,128)(2,1)S(1)}, bf16[2816,256]{1,0:T(8,128)(2,1)S(1)}, u32[]{:S(2)}, u32[]{:S(2)}) %collective-permute-start.9) | collective-permute-done | bytes 1441824 | tf_op jit(solution)/shard_map/ppermute | solution.py:341
  271.8 7.0 %shard_map.95.mine = f32[320,1024]{1,0:T(8,128)S(1)} custom-call(bf16[160,3584]{1,0:T(8,128)(2,1)S(1)} %pad_maximum_fusion.refs_0_, bf16[160,3584]{1,0:T(8,128)(2,1)S(1)} %collective-permute-done.4.refs_1_, bf16[160,3584]{1,0:T(8,128)(2,1)S(1)} %collective-permute-done.6.refs_2_, bf16[160,3584]{1,0:T(8,128)(2,1)S(1)} %collective-permute-done.5.refs_3_, ...), custom_call_target="tpu_custom_call" | custom-call | flops 2348810240 | bytes 9633792 | tf_op jit(solution)/shard_map/pallas_call | solution.py:403
  278.8 0.1 collective-permute-start.10
  278.9 7.3 %shard_map.97.proj_mine = f32[320,512]{1,0:T(8,128)S(1)} custom-call(bf16[160,3584]{1,0:T(8,128)(2,1)S(1)} %pad_maximum_fusion.refs_0_, bf16[160,3584]{1,0:T(8,128)(2,1)S(1)} %collective-permute-done.4.refs_1_, bf16[160,3584]{1,0:T(8,128)(2,1)S(1)} %collective-permute-done.6.refs_2_, bf16[160,3584]{1,0:T(8,128)(2,1)S(1)} %collective-permute-done.5.refs_3_, ...), custom_call_target="tpu_custom_call" | custom-call | flops 1174405120 | bytes 5963776 | tf_op jit(solution)/shard_map/pallas_call | solution.py:412
  286.2 0.0 copy-start.1
  286.2 0.6 collective-permute-start.11
  286.8 0.0 collective-permute-done.10.theirs
  286.8 3.3 shard_map.96
  290.1 0.0 copy-done.1
  290.1 0.0 collective-permute-done.11.proj_theirs
  290.1 1.5 collective-permute-start.14
  291.5 1.5 collective-permute-start.15
  293.1 0.0 copy-done
  293.1 1.1 copy-done.2
  294.2 8.3 %shard_map.98 = (bf16[80,3712]{1,0:T(8,128)(2,1)S(1)}, bf16[80,3712]{1,0:T(8,128)(2,1)S(1)}, bf16[80,3712]{1,0:T(8,128)(2,1)S(1)}, bf16[80,3712]{1,0:T(8,128)(2,1)S(1)}) custom-call(f32[320,1024]{1,0:T(8,128)S(1)} %shard_map.95.mine, f32[320,1024]{1,0:T(8,128)S(1)} %collective-permute-done.10.theirs, f32[320,512]{1,0:T(8,128)S(1)} %copy-done.2, ...), custom_call_target="tpu_custom_call" | custom-call | flops 2348810240 | bytes 9633792 | tf_op jit(solution)/shard_map/pallas_call | solution.py:432
  302.5 1.6 collective-permute-start.12
  304.1 0.7 collective-permute-start.13
  304.8 12.5 %collective-permute-done.12.ends = bf16[80,3712]{1,0:T(8,128)(2,1)S(1)} collective-permute-done((bf16[80,3712]{1,0:T(8,128)(2,1)S(1)}, bf16[80,3712]{1,0:T(8,128)(2,1)S(1)}, u32[]{:S(2)}, u32[]{:S(2)}) %collective-permute-start.12) | collective-permute-done | bytes 593952 | tf_op jit(solution)/shard_map/ppermute | solution.py:341
  317.3 0.0 collective-permute-done.13.middle
  317.3 0.0 collective-permute-done.14
  317.3 0.0 collective-permute-done.15
  317.3 0.1 select_add_fusion
  317.4 6.0 %collective-permute-start.16 = (bf16[80,3712]{1,0:T(8,128)(2,1)S(1)}, bf16[80,3712]{1,0:T(8,128)(2,1)S(1)}, u32[]{:S(2)}, u32[]{:S(2)}) collective-permute-start(bf16[80,3712]{1,0:T(8,128)(2,1)S(1)} %select_add_fusion), channel_id=1, source_target_pairs={{0,16},{2,18},{4,20},{6,22},{8,24},{10,26},{12,28},{14,30},{16,0},... | collective-permute-start | bytes 1781768 | tf_op jit(solution)/shard_map/ppermute | solution.py:341
  323.4 1.3 collective-permute-start.17
  324.7 0.1 slice_add_fusion.1
  324.7 0.6 collective-permute-start.18
  325.4 0.6 collective-permute-start.19
  326.0 21.7 %collective-permute-done.16.far = bf16[80,3712]{1,0:T(8,128)(2,1)S(1)} collective-permute-done((bf16[80,3712]{1,0:T(8,128)(2,1)S(1)}, bf16[80,3712]{1,0:T(8,128)(2,1)S(1)}, u32[]{:S(2)}, u32[]{:S(2)}) %collective-permute-start.16) | collective-permute-done | bytes 593952 | tf_op jit(solution)/shard_map/ppermute | solution.py:341
  347.7 0.0 collective-permute-done.17.outer
  347.7 0.5 shard_map.99
  348.2 0.0 collective-permute-done.18
  348.2 0.0 collective-permute-done.19
  348.2 0.1 collective-permute-start.20
  348.3 0.3 add_convert_fusion.1
  348.6 0.0 copy-start.3
  348.6 0.0 copy-start.4
  348.7 1.0 maximum_bitcast_fusion
  349.7 0.2 collective-permute-done.20.refs_2_
  349.9 0.0 copy-done.6
  349.9 3.0 shard_map.100
  (8 shorter events, 0.1 us)
Async XLA Ops:
  171.9 5.1 %collective-permute-start.3 = (bf16[2,40,3584]{2,1,0:T(8,128)(2,1)}, bf16[2,40,3584]{2,1,0:T(8,128)(2,1)S(1)}, u32[]{:S(2)}, u32[]{:S(2)}) collective-permute-start(bf16[2,40,3584]{2,1,0:T(8,128)(2,1)} %get-tuple-element.54), channel_id=1, source_target_pairs={{0,1},{1,0},{2,3},{3,2},{4,5},{5,4},{6,7},{7,6},{8,9},{9,8},{10,11... | collective-permute-start | bytes 1720328 | tf_op jit(solution)/shard_map/ppermute | solution.py:379
  172.4 64.6 %collective-permute-start = (bf16[5376,256]{1,0:T(8,128)(2,1)}, bf16[5376,256]{1,0:T(8,128)(2,1)}, u32[]{:S(2)}, u32[]{:S(2)}) collective-permute-start(bf16[5376,256]{1,0:T(8,128)(2,1)} %get-tuple-element.50.refs_5_.refs_0_), channel_id=1, source_target_pairs={{0,2},{2,0},{4,6},{6,4},{8,10},{10,8},{12,14},{14,12},{16,18},{18,... | collective-permute-start | bytes 8257544 | tf_op jit(solution)/shard_map/ppermute | solution.py:341
  175.0 31.9 %collective-permute-start.1 = (bf16[2560,256]{1,0:T(8,128)(2,1)}, bf16[2560,256]{1,0:T(8,128)(2,1)}, u32[]{:S(2)}, u32[]{:S(2)}) collective-permute-start(bf16[2560,256]{1,0:T(8,128)(2,1)} %get-tuple-element.51), channel_id=1, source_target_pairs={{0,4},{2,6},{4,0},{6,2},{8,12},{10,14},{12,8},{14,10},{16,20},{18,... | collective-permute-start | bytes 3932168 | tf_op jit(solution)/shard_map/ppermute | solution.py:341
  176.5 60.5 %collective-permute-start.2 = (bf16[2816,256]{1,0:T(8,128)(2,1)}, bf16[2816,256]{1,0:T(8,128)(2,1)}, u32[]{:S(2)}, u32[]{:S(2)}) collective-permute-start(bf16[2816,256]{1,0:T(8,128)(2,1)} %get-tuple-element.52), channel_id=1, source_target_pairs={{0,4},{2,6},{4,0},{6,2},{8,12},{10,14},{12,8},{14,10},{16,20},{18,... | collective-permute-start | bytes 4325384 | tf_op jit(solution)/shard_map/ppermute | solution.py:341
  178.2 58.8 %collective-permute-start.4 = (bf16[160,3584]{1,0:T(8,128)(2,1)S(1)}, bf16[160,3584]{1,0:T(8,128)(2,1)S(1)}, u32[]{:S(2)}, u32[]{:S(2)}) collective-permute-start(bf16[160,3584]{1,0:T(8,128)(2,1)S(1)} %pad_maximum_fusion.refs_0_), channel_id=1, source_target_pairs={{0,16},{2,18},{4,20},{6,22},{8,24},{10,26},{12,28},{14,30},{16,0},... | collective-permute-start | bytes 3440648 | tf_op jit(solution)/shard_map/ppermute | solution.py:341
  180.9 56.2 %collective-permute-start.5 = (bf16[160,3584]{1,0:T(8,128)(2,1)S(1)}, bf16[160,3584]{1,0:T(8,128)(2,1)S(1)}, u32[]{:S(2)}, u32[]{:S(2)}) collective-permute-start(bf16[160,3584]{1,0:T(8,128)(2,1)S(1)} %pad_maximum_fusion.refs_0_), channel_id=1, source_target_pairs={{8,0},{10,2},{12,4},{14,6},{16,24},{18,26},{20,28},{22,30},{9,1},{... | collective-permute-start | bytes 3440648 | tf_op jit(solution)/shard_map/ppermute | solution.py:341
  237.0 30.3 %collective-permute-start.8 = (bf16[2560,256]{1,0:T(8,128)(2,1)}, bf16[2560,256]{1,0:T(8,128)(2,1)S(1)}, u32[]{:S(2)}, u32[]{:S(2)}) collective-permute-start(bf16[2560,256]{1,0:T(8,128)(2,1)} %collective-permute-done.1.refs_7_.refs_2_), channel_id=1, source_target_pairs={{0,2},{2,0},{4,6},{6,4},{8,10},{10,8},{12,14},{14,12},{16,18},{18,... | collective-permute-start | bytes 3932168 | tf_op jit(solution)/shard_map/ppermute | solution.py:341
  238.9 32.9 %collective-permute-start.9 = (bf16[2816,256]{1,0:T(8,128)(2,1)S(1)}, bf16[2816,256]{1,0:T(8,128)(2,1)S(1)}, u32[]{:S(2)}, u32[]{:S(2)}) collective-permute-start(bf16[2816,256]{1,0:T(8,128)(2,1)S(1)} %slice.41), channel_id=1, source_target_pairs={{0,4},{2,6},{4,0},{6,2},{8,12},{10,14},{12,8},{14,10},{16,20},{18,... | collective-permute-start | bytes 4325384 | tf_op jit(solution)/shard_map/ppermute | solution.py:341
  240.8 26.0 %collective-permute-start.6 = (bf16[160,3584]{1,0:T(8,128)(2,1)S(1)}, bf16[160,3584]{1,0:T(8,128)(2,1)S(1)}, u32[]{:S(2)}, u32[]{:S(2)}) collective-permute-start(bf16[160,3584]{1,0:T(8,128)(2,1)S(1)} %broadcast_select_fusion), channel_id=1, source_target_pairs={{8,0},{10,2},{12,4},{14,6},{16,24},{18,26},{20,28},{22,30},{0,8},{... | collective-permute-start | bytes 3440648 | tf_op jit(solution)/shard_map/ppermute | solution.py:341
  242.4 24.4 %collective-permute-start.7 = (bf16[160,3584]{1,0:T(8,128)(2,1)S(1)}, bf16[160,3584]{1,0:T(8,128)(2,1)S(1)}, u32[]{:S(2)}, u32[]{:S(2)}) collective-permute-start(bf16[160,3584]{1,0:T(8,128)(2,1)S(1)} %pad_maximum_fusion.refs_0_), channel_id=1, source_target_pairs={{8,16},{10,18},{12,20},{14,22},{16,8},{18,10},{20,12},{22,14},{9,1... | collective-permute-start | bytes 3440648 | tf_op jit(solution)/shard_map/ppermute | solution.py:341
  278.8 8.0 %collective-permute-start.10 = (f32[320,1024]{1,0:T(8,128)S(1)}, f32[320,1024]{1,0:T(8,128)S(1)}, u32[]{:S(2)}, u32[]{:S(2)}) collective-permute-start(f32[320,1024]{1,0:T(8,128)S(1)} %shard_map.95.mine), channel_id=1, source_target_pairs={{0,1},{1,0},{2,3},{3,2},{4,5},{5,4},{6,7},{7,6},{8,9},{9,8},{10,11... | collective-permute-start | bytes 3932168 | tf_op jit(solution)/shard_map/ppermute | solution.py:411
  286.2 3.9 %copy-start.1 = (f32[320,512]{1,0:T(8,128)}, f32[320,512]{1,0:T(8,128)S(1)}, u32[]{:S(2)}) copy-start(f32[320,512]{1,0:T(8,128)S(1)} %shard_map.97.proj_mine) | copy-start | bytes 1966084
  286.2 3.9 %collective-permute-start.11 = (f32[320,512]{1,0:T(8,128)S(1)}, f32[320,512]{1,0:T(8,128)S(1)}, u32[]{:S(2)}, u32[]{:S(2)}) collective-permute-start(f32[320,512]{1,0:T(8,128)S(1)} %shard_map.97.proj_mine), channel_id=1, source_target_pairs={{0,1},{1,0},{2,3},{3,2},{4,5},{5,4},{6,7},{7,6},{8,9},{9,8},{10,11... | collective-permute-start | bytes 1966088 | tf_op jit(solution)/shard_map/ppermute | solution.py:420
  286.8 6.3 %copy-start = (bf16[5376,256]{1,0:T(8,128)(2,1)S(1)}, bf16[5376,256]{1,0:T(8,128)(2,1)}, u32[]{:S(2)}) copy-start(bf16[5376,256]{1,0:T(8,128)(2,1)} %get-tuple-element.50.refs_5_.refs_0_) | copy-start | bytes 8257540
  290.1 27.2 %collective-permute-start.14 = (bf16[128,3584]{1,0:T(8,128)(2,1)S(1)}, bf16[128,3584]{1,0:T(8,128)(2,1)S(1)}, u32[]{:S(2)}, u32[]{:S(2)}) collective-permute-start(bf16[128,3584]{1,0:T(8,128)(2,1)S(1)} %get-tuple-element.69), channel_id=1, source_target_pairs={{0,2},{2,0},{4,6},{6,4},{8,10},{10,8},{12,14},{14,12},{16,18},{18,... | collective-permute-start | bytes 2752520 | tf_op jit(solution)/shard_map/ppermute | solution.py:341
  291.5 25.7 %collective-permute-start.15 = (bf16[128,3584]{1,0:T(8,128)(2,1)S(1)}, bf16[128,3584]{1,0:T(8,128)(2,1)S(1)}, u32[]{:S(2)}, u32[]{:S(2)}) collective-permute-start(bf16[128,3584]{1,0:T(8,128)(2,1)S(1)} %get-tuple-element.70), channel_id=1, source_target_pairs={{0,4},{2,6},{4,0},{6,2},{8,12},{10,14},{12,8},{14,10},{16,20},{18,... | collective-permute-start | bytes 2752520 | tf_op jit(solution)/shard_map/ppermute | solution.py:341
  293.1 1.1 copy-start.2
  302.5 14.8 %collective-permute-start.12 = (bf16[80,3712]{1,0:T(8,128)(2,1)S(1)}, bf16[80,3712]{1,0:T(8,128)(2,1)S(1)}, u32[]{:S(2)}, u32[]{:S(2)}) collective-permute-start(bf16[80,3712]{1,0:T(8,128)(2,1)S(1)} %get-tuple-element.67), channel_id=1, source_target_pairs={{8,0},{10,2},{12,4},{14,6},{16,24},{18,26},{20,28},{22,30},{0,8},{... | collective-permute-start | bytes 1781768 | tf_op jit(solution)/shard_map/ppermute | solution.py:341
  304.1 13.2 %collective-permute-start.13 = (bf16[80,3712]{1,0:T(8,128)(2,1)S(1)}, bf16[80,3712]{1,0:T(8,128)(2,1)S(1)}, u32[]{:S(2)}, u32[]{:S(2)}) collective-permute-start(bf16[80,3712]{1,0:T(8,128)(2,1)S(1)} %get-tuple-element.77), channel_id=1, source_target_pairs={{8,16},{10,18},{12,20},{14,22},{16,8},{18,10},{20,12},{22,14},{9,1... | collective-permute-start | bytes 1781768 | tf_op jit(solution)/shard_map/ppermute | solution.py:341
  317.4 30.3 %collective-permute-start.16 = (bf16[80,3712]{1,0:T(8,128)(2,1)S(1)}, bf16[80,3712]{1,0:T(8,128)(2,1)S(1)}, u32[]{:S(2)}, u32[]{:S(2)}) collective-permute-start(bf16[80,3712]{1,0:T(8,128)(2,1)S(1)} %select_add_fusion), channel_id=1, source_target_pairs={{0,16},{2,18},{4,20},{6,22},{8,24},{10,26},{12,28},{14,30},{16,0},... | collective-permute-start | bytes 1781768 | tf_op jit(solution)/shard_map/ppermute | solution.py:341
  323.4 24.4 %collective-permute-start.17 = (bf16[80,3712]{1,0:T(8,128)(2,1)S(1)}, bf16[80,3712]{1,0:T(8,128)(2,1)S(1)}, u32[]{:S(2)}, u32[]{:S(2)}) collective-permute-start(bf16[80,3712]{1,0:T(8,128)(2,1)S(1)} %get-tuple-element.77), channel_id=1, source_target_pairs={{0,8},{2,10},{4,12},{6,14},{24,16},{26,18},{28,20},{30,22},{1,9},{... | collective-permute-start | bytes 1781768 | tf_op jit(solution)/shard_map/ppermute | solution.py:341
  324.7 23.5 %collective-permute-start.18 = (bf16[64,3584]{1,0:T(8,128)(2,1)S(1)}, bf16[64,3584]{1,0:T(8,128)(2,1)S(1)}, u32[]{:S(2)}, u32[]{:S(2)}) collective-permute-start(bf16[64,3584]{1,0:T(8,128)(2,1)S(1)} %slice_add_fusion.1), channel_id=1, source_target_pairs={{0,2},{2,0},{4,6},{6,4},{8,10},{10,8},{12,14},{14,12},{16,18},{18,... | collective-permute-start | bytes 1376264 | tf_op jit(solution)/shard_map/ppermute | solution.py:341
  325.4 22.8 %collective-permute-start.19 = (bf16[64,3584]{1,0:T(8,128)(2,1)S(1)}, bf16[64,3584]{1,0:T(8,128)(2,1)S(1)}, u32[]{:S(2)}, u32[]{:S(2)}) collective-permute-start(bf16[64,3584]{1,0:T(8,128)(2,1)S(1)} %slice_add_fusion), channel_id=1, source_target_pairs={{0,4},{2,6},{4,0},{6,2},{8,12},{10,14},{12,8},{14,10},{16,20},{18,... | collective-permute-start | bytes 1376264 | tf_op jit(solution)/shard_map/ppermute | solution.py:341
  348.2 1.6 collective-permute-start.20
  348.6 1.2 copy-start.3
  348.6 1.2 copy-start.4
  348.7 1.2 copy-start.5
  348.7 1.2 copy-start.6

commit v5 on v4

--- a/solution.py
+++ b/solution.py
@@ -40,7 +40,7 @@
 def prep_kernel(held, capacity, *refs):
     gate, up, down, tokens, cotangent, logits, ids = refs[:7]
     weights, top, low, mine, other, pick_out = refs[7:13]
-    chosen_out, inv_w_out, inv_total_out, sems = refs[13:]
+    chosen_out, inv_w_out, inv_total_out, packed, sems = refs[13:]
     ff = gate.shape[2]
     part = mine.shape[2]
     wide = 2 * ff
@@ -48,25 +48,20 @@
     start = pl.multiple_of(core * part, 128)
     away = pl.multiple_of((1 - core) * part, 128)
     split = top.shape[0]
-    rest = part - split
-    pairs = []
-    for out, at, first, size in (
-        (weights, 0, 0, part),
-        (top, 0, 0, split),
-        (low, 0, split, rest),
-    ):
-        rows = pl.ds(pl.multiple_of(start + first, 128), size)
-        pairs.append((gate.at[0, rows, :], out.at[at : at + size, :ff]))
-        pairs.append((up.at[0, rows, :], out.at[at : at + size, ff:]))
+    half = pl.ds(start, part)
+    pairs = [
+        (gate.at[0, half, :], packed.at[:part, :ff]),
+        (up.at[0, half, :], packed.at[:part, ff:]),
+    ]
     for c in range(part // wide):
         columns = pl.ds(pl.multiple_of(start + c * wide, 128), wide)
-        for out, at in ((weights, part), (low, rest)):
-            rows = slice(at + c * ff, at + (c + 1) * ff)
-            pairs.append((down.at[0, :, columns], out.at[rows, :]))
+        pairs.append((down.at[0, :, columns], packed.at[part + c * ff : part + (c + 1) * ff, :]))
+    reads = len(pairs)
+    pairs += [(packed, weights), (packed.at[:split, :], top), (packed.at[split:, :], low)]
     copies = [
         pltpu.make_async_copy(src, dst, sems.at[i]) for i, (src, dst) in enumerate(pairs)
     ]
-    for copy in copies:
+    for copy in copies[:reads]:
         copy.start()
 
     experts, count = logits.shape
@@ -110,8 +105,12 @@
             out[1, :, pl.ds(at, step)] = (c * value).astype(bf16)
         return carry
 
+    for copy in copies[:reads]:
+        copy.wait()
+    for copy in copies[reads:]:
+        copy.start()
     lax.fori_loop(0, part // step, body, 0)
-    for copy in copies:
+    for copy in copies[reads:]:
         copy.wait()
 
 
@@ -176,12 +175,21 @@
     split, upper, lower = piece_sides(pieces)
     out[...] = jnp.zeros_like(out)
 
+    pair = 2 if part // wide % 2 == 0 else 1
+    step = pair * wide
+
     def body(k, carry):
-        columns = pl.ds(pl.multiple_of(k * wide, 128), wide)
+        columns = pl.ds(pl.multiple_of(k * step, 128), step)
         rows = slot_rows(blocks, count, count, columns)
         w = jnp.concatenate(
             [
-                ref[pl.ds(pl.multiple_of(base + part - split + k * ff, 128), ff), :]
+                jnp.concatenate(
+                    [
+                        ref[pl.ds(pl.multiple_of(base + part - split + (pair * k + i) * ff, 128), ff), :]
+                        for i in range(pair)
+                    ],
+                    axis=1,
+                )
                 for ref, base in lower
             ],
             axis=0,
@@ -189,7 +197,7 @@
         out[...] += lax.dot_general(rows, w, CONTRACT1, preferred_element_type=f32)
         return carry
 
-    lax.fori_loop(0, part // wide, body, 0)
+    lax.fori_loop(0, part // step, body, 0)
 
 
 def activations(mine, theirs, q, ff):
@@ -304,7 +312,7 @@
     logit_out[...] = SCALE * inv_total[...] * (dw - inner) * share * (1.0 - share)
 
 
-def call(kernel, outs, in_specs, scratch, flops, moved, limit=40, out_specs=None):
+def call(kernel, outs, in_specs, scratch, flops, moved, limit=20, out_specs=None):
     return pl.pallas_call(
         kernel,
         out_shape=outs,
@@ -366,7 +374,7 @@
         + [shape((rows_dev, tok_count), bf16)]
         + [shape((experts, tok_count), f32)] * 3,
         [hbm] * 3 + [VMEM] * 4,
-        [pltpu.SemaphoreType.DMA((6 + part // ff,))],
+        [pltpu.VMEM((packed, 2 * ff), bf16), pltpu.SemaphoreType.DMA((5 + part // (2 * ff),))],
         4 * rows_dev * tok_count * width,
         12 * part * ff + 4 * tok_count * width,
         limit=58,

time: 353 us -> 186 us (0.53)
  Pallas kernels: 201 us -> 35.4 us
    pallas_call x1, Pallas kernels: 171 us -> 7.34 us  [per_device(): call(lambda *refs: prep_kernel(held, capacity, *refs), [shape((size, 2 *...]
  transfers between devices with their start and end apart: 21 -> 21, of which waited for: 8 -> 8; matrix products, arithmetic and copies ran while one was open for 1% -> 3% of each run, Pallas kernels for 5% -> 10%
where the time goes in v5:
time: 186 us; the launch traced here: 185 us
  waiting for transfers between devices  116 us (62%)
  Pallas kernels  35.4 us (19%)
  starting transfers between devices  27.9 us (15%)
  other arithmetic  5.16 us (3%)
    ppermute x17, waiting for transfers between devices, send(): return lax.ppermute(array, 'expert', route)  116 us
    ppermute x17, starting transfers between devices, send(): return lax.ppermute(array, 'expert', route)  26.7 us
    pallas_call x1, Pallas kernels, per_device(): call(back_kernel, [shape((rows_chip, part + 128), bf16)] * members, [VMEM...  7.46 us
    pallas_call x1, Pallas kernels, per_device(): call(lambda *refs: prep_kernel(held, capacity, *refs), [shape((size, 2 *...  7.34 us
    pallas_call x1, Pallas kernels, per_device(): call(gate_up_kernel, [shape((slots, QUAD * 2 * ff), f32)], [VMEM] * 11, [...  6.46 us
    pallas_call x1, Pallas kernels, per_device(): call(proj_kernel, [shape((slots, QUAD * ff), f32)], [VMEM] * 11, [], matm...  5.44 us
    pallas_call x1, Pallas kernels, per_device(): call(down_kernel, [shape((ff, part), bf16)] * 3 + [shape((lowf, part), bf...  5.19 us
  transfers between devices with their start and end apart: 21, of which 8 were waited for; matrix products, arithmetic and copies ran while one was open for 3% of the time, Pallas kernels for 10%

profile of v5, /device:TPU:0, one launch (start us, length us, event | category | flops | bytes accessed | tf_op | source)
XLA Modules:
  0.0 185.4 jit_solution(14349773302955662757)
XLA Ops:
  0.6 7.3 %shard_map.94 = (bf16[5376,256]{1,0:T(8,128)(2,1)}, bf16[2560,256]{1,0:T(8,128)(2,1)}, bf16[2816,256]{1,0:T(8,128)(2,1)}, bf16[2,40,3584]{2,1,0:T(8,128)(2,1)}, ...) custom-call(bf16[1,7168,128]{2,1,0:T(8,128)(2,1)} %refs_0_.1, ...), custom_call_target="tpu_custom_call" | custom-call | flops 146800640 | bytes 9175040 | tf_op jit(solution)/shard_map/pallas_call | solution.py:370
  8.0 0.5 collective-permute-start.3
  8.5 2.6 %collective-permute-start = (bf16[5376,256]{1,0:T(8,128)(2,1)}, bf16[5376,256]{1,0:T(8,128)(2,1)S(1)}, u32[]{:S(2)}, u32[]{:S(2)}) collective-permute-start(bf16[5376,256]{1,0:T(8,128)(2,1)} %get-tuple-element.50.refs_5_.refs_0_), channel_id=1, source_target_pairs={{0,2},{2,0},{4,6},{6,4},{8,10},{10,8},{12,14},{14,12},{16,18},{18,... | collective-permute-start | bytes 8257544 | tf_op jit(solution)/shard_map/ppermute | solution.py:349
  11.1 1.6 collective-permute-start.1
  12.6 0.5 collective-permute-start.2
  13.1 0.0 collective-permute-done.3
  13.1 1.1 select_bitcast_fusion.3
  14.2 1.1 pad_maximum_fusion.refs_0_
  15.4 2.6 %collective-permute-start.4 = (bf16[160,3584]{1,0:T(8,128)(2,1)}, bf16[160,3584]{1,0:T(8,128)(2,1)}, u32[]{:S(2)}, u32[]{:S(2)}) collective-permute-start(bf16[160,3584]{1,0:T(8,128)(2,1)} %pad_maximum_fusion.refs_0_), channel_id=1, source_target_pairs={{0,16},{2,18},{4,20},{6,22},{8,24},{10,26},{12,28},{14,30},{16,0},... | collective-permute-start | bytes 3440648 | tf_op jit(solution)/shard_map/ppermute | solution.py:349
  18.0 1.3 collective-permute-start.5
  19.3 23.7 %collective-permute-done.1.refs_7_.refs_2_ = bf16[2560,256]{1,0:T(8,128)(2,1)} collective-permute-done((bf16[2560,256]{1,0:T(8,128)(2,1)}, bf16[2560,256]{1,0:T(8,128)(2,1)}, u32[]{:S(2)}, u32[]{:S(2)}) %collective-permute-start.1) | collective-permute-done | bytes 1310752 | tf_op jit(solution)/shard_map/ppermute | solution.py:349
  43.0 30.1 %collective-permute-done.2.refs_8_.refs_3_ = bf16[2816,256]{1,0:T(8,128)(2,1)} collective-permute-done((bf16[2816,256]{1,0:T(8,128)(2,1)}, bf16[2816,256]{1,0:T(8,128)(2,1)}, u32[]{:S(2)}, u32[]{:S(2)}) %collective-permute-start.2) | collective-permute-done | bytes 1441824 | tf_op jit(solution)/shard_map/ppermute | solution.py:349
  73.1 0.0 collective-permute-done.4.refs_1_
  73.1 0.0 collective-permute-done.5.refs_3_
  73.1 0.0 collective-permute-done.refs_6_.refs_1_
  73.1 0.4 collective-permute-start.8
  73.5 0.1 slice.41
  73.6 0.0 copy-start
  73.6 1.8 collective-permute-start.9
  75.4 1.4 broadcast_select_fusion
  76.8 1.6 collective-permute-start.6
  78.5 0.7 collective-permute-start.7
  79.2 23.6 %collective-permute-done.6.refs_2_ = bf16[160,3584]{1,0:T(8,128)(2,1)S(1)} collective-permute-done((bf16[160,3584]{1,0:T(8,128)(2,1)S(1)}, bf16[160,3584]{1,0:T(8,128)(2,1)S(1)}, u32[]{:S(2)}, u32[]{:S(2)}) %collective-permute-start.6) | collective-permute-done | bytes 1146912 | tf_op jit(solution)/shard_map/ppermute | solution.py:349
  102.8 0.0 collective-permute-done.7.refs_4_
  102.8 0.6 collective-permute-done.8.refs_9_.refs_4_
  103.4 3.1 %collective-permute-done.9.refs_10_.refs_5_ = bf16[2816,256]{1,0:T(8,128)(2,1)S(1)} collective-permute-done((bf16[2816,256]{1,0:T(8,128)(2,1)S(1)}, bf16[2816,256]{1,0:T(8,128)(2,1)S(1)}, u32[]{:S(2)}, u32[]{:S(2)}) %collective-permute-start.9) | collective-permute-done | bytes 1441824 | tf_op jit(solution)/shard_map/ppermute | solution.py:349
  106.5 0.0 copy-done
  106.5 6.5 %shard_map.95.mine = f32[320,1024]{1,0:T(8,128)S(1)} custom-call(bf16[160,3584]{1,0:T(8,128)(2,1)} %pad_maximum_fusion.refs_0_, bf16[160,3584]{1,0:T(8,128)(2,1)} %collective-permute-done.4.refs_1_, bf16[160,3584]{1,0:T(8,128)(2,1)S(1)} %collective-permute-done.6.refs_2_, bf16[160,3584]{1,0:T(8,128)(2,1)} %collective-permute-done.5.refs_3_, ...), custom_call_target="tpu_custom_call" | custom-call | flops 2348810240 | bytes 9633792 | tf_op jit(solution)/shard_map/pallas_call | solution.py:411
  113.0 0.1 collective-permute-start.10
  113.0 5.4 %shard_map.97.proj_mine = f32[320,512]{1,0:T(8,128)S(1)} custom-call(bf16[160,3584]{1,0:T(8,128)(2,1)} %pad_maximum_fusion.refs_0_, bf16[160,3584]{1,0:T(8,128)(2,1)} %collective-permute-done.4.refs_1_, bf16[160,3584]{1,0:T(8,128)(2,1)S(1)} %collective-permute-done.6.refs_2_, bf16[160,3584]{1,0:T(8,128)(2,1)} %collective-permute-done.5.refs_3_, ...), custom_call_target="tpu_custom_call" | custom-call | flops 1174405120 | bytes 5963776 | tf_op jit(solution)/shard_map/pallas_call | solution.py:420
  118.5 0.6 collective-permute-start.11
  119.0 0.0 collective-permute-done.10.theirs
  119.0 5.2 %shard_map.96 = (bf16[128,3584]{1,0:T(8,128)(2,1)S(1)}, bf16[128,3584]{1,0:T(8,128)(2,1)S(1)}, bf16[128,3584]{1,0:T(8,128)(2,1)S(1)}, bf16[64,3584]{1,0:T(8,128)(2,1)S(1)}, bf16[64,3584]{1,0:T(8,128)(2,1)S(1)}) custom-call(f32[320,1024]{1,0:T(8,128)S(1)} %shard_map.95.mine, f32[320,1024]{1,0:T(8,128)S(1)} %collective-permute-done.10.theirs, ...), custom_call_target="tpu_custom_call" | custom-call | flops 1174405120 | bytes 5963776 | tf_op jit(solution)/shard_map/pallas_call | solution.py:429
  124.2 0.0 collective-permute-done.11.proj_theirs
  124.3 1.5 collective-permute-start.14
  125.8 1.5 collective-permute-start.15
  127.3 7.5 %shard_map.98 = (bf16[80,3712]{1,0:T(8,128)(2,1)S(1)}, bf16[80,3712]{1,0:T(8,128)(2,1)S(1)}, bf16[80,3712]{1,0:T(8,128)(2,1)S(1)}, bf16[80,3712]{1,0:T(8,128)(2,1)S(1)}) custom-call(f32[320,1024]{1,0:T(8,128)S(1)} %shard_map.95.mine, f32[320,1024]{1,0:T(8,128)S(1)} %collective-permute-done.10.theirs, f32[320,512]{1,0:T(8,128)S(1)} %shard_map.97.proj_mine, ...), custom_call_target="tpu_custom_call" | custom-call | flops 2348810240 | bytes 9633792 | tf_op jit(solution)/shard_map/pallas_call | solution.py:440
  134.7 1.6 collective-permute-start.12
  136.4 0.7 collective-permute-start.13
  137.1 12.6 %collective-permute-done.12.ends = bf16[80,3712]{1,0:T(8,128)(2,1)S(1)} collective-permute-done((bf16[80,3712]{1,0:T(8,128)(2,1)S(1)}, bf16[80,3712]{1,0:T(8,128)(2,1)S(1)}, u32[]{:S(2)}, u32[]{:S(2)}) %collective-permute-start.12) | collective-permute-done | bytes 593952 | tf_op jit(solution)/shard_map/ppermute | solution.py:349
  149.6 0.0 collective-permute-done.13.middle
  149.7 0.0 collective-permute-done.14
  149.7 0.0 collective-permute-done.15
  149.7 0.1 select_add_fusion
  149.8 5.8 %collective-permute-start.16 = (bf16[80,3712]{1,0:T(8,128)(2,1)S(1)}, bf16[80,3712]{1,0:T(8,128)(2,1)S(1)}, u32[]{:S(2)}, u32[]{:S(2)}) collective-permute-start(bf16[80,3712]{1,0:T(8,128)(2,1)S(1)} %select_add_fusion), channel_id=1, source_target_pairs={{0,16},{2,18},{4,20},{6,22},{8,24},{10,26},{12,28},{14,30},{16,0},... | collective-permute-start | bytes 1781768 | tf_op jit(solution)/shard_map/ppermute | solution.py:349
  155.6 1.3 collective-permute-start.17
  156.9 0.1 slice_add_fusion.1
  157.0 0.6 collective-permute-start.18
  157.7 0.6 collective-permute-start.19
  158.2 21.9 %collective-permute-done.16.far = bf16[80,3712]{1,0:T(8,128)(2,1)S(1)} collective-permute-done((bf16[80,3712]{1,0:T(8,128)(2,1)S(1)}, bf16[80,3712]{1,0:T(8,128)(2,1)S(1)}, u32[]{:S(2)}, u32[]{:S(2)}) %collective-permute-start.16) | collective-permute-done | bytes 593952 | tf_op jit(solution)/shard_map/ppermute | solution.py:349
  180.2 0.0 collective-permute-done.17.outer
  180.2 0.5 shard_map.99
  180.7 0.0 collective-permute-done.18
  180.7 0.0 collective-permute-done.19
  180.7 0.1 collective-permute-start.20
  180.8 0.3 add_convert_fusion.1
  181.1 0.0 copy-start.1
  181.1 0.0 copy-start.2
  181.2 0.0 copy-start.3
  181.2 0.0 copy-start.4
  181.2 1.0 maximum_bitcast_fusion
  182.2 0.2 collective-permute-done.20.refs_2_
  182.4 0.0 copy-done.2
  182.4 3.0 %shard_map.100 = (bf16[128,7168]{1,0:T(8,128)(2,1)}, f32[32,128]{1,0:T(8,128)}) custom-call(bf16[40,128]{1,0:T(8,128)(2,1)S(1)} %copy-done.4, bf16[40,3584]{1,0:T(8,128)(2,1)S(1)} %get-tuple-element.79.refs_1_, bf16[40,3584]{1,0:T(8,128)(2,1)S(1)} %collective-permute-done.20.refs_2_, f32[40,128]{1,0:T(8,128)S(1)} %get-tuple-element.86.refs_3_, ...), custom_call_target="tpu_custom_call" | custom-call | flops 73400320 | bytes 2408448 | tf_op jit(solution)/shard_map/pallas_call | solution.py:484
  (4 shorter events, 0.1 us)
Async XLA Ops:
  8.0 5.1 %collective-permute-start.3 = (bf16[2,40,3584]{2,1,0:T(8,128)(2,1)}, bf16[2,40,3584]{2,1,0:T(8,128)(2,1)S(1)}, u32[]{:S(2)}, u32[]{:S(2)}) collective-permute-start(bf16[2,40,3584]{2,1,0:T(8,128)(2,1)} %get-tuple-element.54), channel_id=1, source_target_pairs={{0,1},{1,0},{2,3},{3,2},{4,5},{5,4},{6,7},{7,6},{8,9},{9,8},{10,11... | collective-permute-start | bytes 1720328 | tf_op jit(solution)/shard_map/ppermute | solution.py:387
  8.5 64.6 %collective-permute-start = (bf16[5376,256]{1,0:T(8,128)(2,1)}, bf16[5376,256]{1,0:T(8,128)(2,1)S(1)}, u32[]{:S(2)}, u32[]{:S(2)}) collective-permute-start(bf16[5376,256]{1,0:T(8,128)(2,1)} %get-tuple-element.50.refs_5_.refs_0_), channel_id=1, source_target_pairs={{0,2},{2,0},{4,6},{6,4},{8,10},{10,8},{12,14},{14,12},{16,18},{18,... | collective-permute-start | bytes 8257544 | tf_op jit(solution)/shard_map/ppermute | solution.py:349
  11.1 31.9 %collective-permute-start.1 = (bf16[2560,256]{1,0:T(8,128)(2,1)}, bf16[2560,256]{1,0:T(8,128)(2,1)}, u32[]{:S(2)}, u32[]{:S(2)}) collective-permute-start(bf16[2560,256]{1,0:T(8,128)(2,1)} %get-tuple-element.51), channel_id=1, source_target_pairs={{0,4},{2,6},{4,0},{6,2},{8,12},{10,14},{12,8},{14,10},{16,20},{18,... | collective-permute-start | bytes 3932168 | tf_op jit(solution)/shard_map/ppermute | solution.py:349
  12.6 60.5 %collective-permute-start.2 = (bf16[2816,256]{1,0:T(8,128)(2,1)}, bf16[2816,256]{1,0:T(8,128)(2,1)}, u32[]{:S(2)}, u32[]{:S(2)}) collective-permute-start(bf16[2816,256]{1,0:T(8,128)(2,1)} %get-tuple-element.52), channel_id=1, source_target_pairs={{0,4},{2,6},{4,0},{6,2},{8,12},{10,14},{12,8},{14,10},{16,20},{18,... | collective-permute-start | bytes 4325384 | tf_op jit(solution)/shard_map/ppermute | solution.py:349
  15.4 57.8 %collective-permute-start.4 = (bf16[160,3584]{1,0:T(8,128)(2,1)}, bf16[160,3584]{1,0:T(8,128)(2,1)}, u32[]{:S(2)}, u32[]{:S(2)}) collective-permute-start(bf16[160,3584]{1,0:T(8,128)(2,1)} %pad_maximum_fusion.refs_0_), channel_id=1, source_target_pairs={{0,16},{2,18},{4,20},{6,22},{8,24},{10,26},{12,28},{14,30},{16,0},... | collective-permute-start | bytes 3440648 | tf_op jit(solution)/shard_map/ppermute | solution.py:349
  18.0 55.2 %collective-permute-start.5 = (bf16[160,3584]{1,0:T(8,128)(2,1)}, bf16[160,3584]{1,0:T(8,128)(2,1)}, u32[]{:S(2)}, u32[]{:S(2)}) collective-permute-start(bf16[160,3584]{1,0:T(8,128)(2,1)} %pad_maximum_fusion.refs_0_), channel_id=1, source_target_pairs={{8,0},{10,2},{12,4},{14,6},{16,24},{18,26},{20,28},{22,30},{9,1},{... | collective-permute-start | bytes 3440648 | tf_op jit(solution)/shard_map/ppermute | solution.py:349
  73.1 30.3 %collective-permute-start.8 = (bf16[2560,256]{1,0:T(8,128)(2,1)}, bf16[2560,256]{1,0:T(8,128)(2,1)S(1)}, u32[]{:S(2)}, u32[]{:S(2)}) collective-permute-start(bf16[2560,256]{1,0:T(8,128)(2,1)} %collective-permute-done.1.refs_7_.refs_2_), channel_id=1, source_target_pairs={{0,2},{2,0},{4,6},{6,4},{8,10},{10,8},{12,14},{14,12},{16,18},{18,... | collective-permute-start | bytes 3932168 | tf_op jit(solution)/shard_map/ppermute | solution.py:349
  73.6 32.9 %copy-start = (bf16[5376,256]{1,0:T(8,128)(2,1)S(1)}, bf16[5376,256]{1,0:T(8,128)(2,1)}, u32[]{:S(2)}) copy-start(bf16[5376,256]{1,0:T(8,128)(2,1)} %get-tuple-element.50.refs_5_.refs_0_) | copy-start | bytes 8257540
  73.6 32.9 %collective-permute-start.9 = (bf16[2816,256]{1,0:T(8,128)(2,1)S(1)}, bf16[2816,256]{1,0:T(8,128)(2,1)S(1)}, u32[]{:S(2)}, u32[]{:S(2)}) collective-permute-start(bf16[2816,256]{1,0:T(8,128)(2,1)S(1)} %slice.41), channel_id=1, source_target_pairs={{0,4},{2,6},{4,0},{6,2},{8,12},{10,14},{12,8},{14,10},{16,20},{18,... | collective-permute-start | bytes 4325384 | tf_op jit(solution)/shard_map/ppermute | solution.py:349
  76.8 26.0 %collective-permute-start.6 = (bf16[160,3584]{1,0:T(8,128)(2,1)S(1)}, bf16[160,3584]{1,0:T(8,128)(2,1)S(1)}, u32[]{:S(2)}, u32[]{:S(2)}) collective-permute-start(bf16[160,3584]{1,0:T(8,128)(2,1)S(1)} %broadcast_select_fusion), channel_id=1, source_target_pairs={{8,0},{10,2},{12,4},{14,6},{16,24},{18,26},{20,28},{22,30},{0,8},{... | collective-permute-start | bytes 3440648 | tf_op jit(solution)/shard_map/ppermute | solution.py:349
  78.5 24.4 %collective-permute-start.7 = (bf16[160,3584]{1,0:T(8,128)(2,1)}, bf16[160,3584]{1,0:T(8,128)(2,1)S(1)}, u32[]{:S(2)}, u32[]{:S(2)}) collective-permute-start(bf16[160,3584]{1,0:T(8,128)(2,1)} %pad_maximum_fusion.refs_0_), channel_id=1, source_target_pairs={{8,16},{10,18},{12,20},{14,22},{16,8},{18,10},{20,12},{22,14},{9,1... | collective-permute-start | bytes 3440648 | tf_op jit(solution)/shard_map/ppermute | solution.py:349
  113.0 6.1 %collective-permute-start.10 = (f32[320,1024]{1,0:T(8,128)S(1)}, f32[320,1024]{1,0:T(8,128)S(1)}, u32[]{:S(2)}, u32[]{:S(2)}) collective-permute-start(f32[320,1024]{1,0:T(8,128)S(1)} %shard_map.95.mine), channel_id=1, source_target_pairs={{0,1},{1,0},{2,3},{3,2},{4,5},{5,4},{6,7},{7,6},{8,9},{9,8},{10,11... | collective-permute-start | bytes 3932168 | tf_op jit(solution)/shard_map/ppermute | solution.py:419
  118.5 5.8 %collective-permute-start.11 = (f32[320,512]{1,0:T(8,128)S(1)}, f32[320,512]{1,0:T(8,128)S(1)}, u32[]{:S(2)}, u32[]{:S(2)}) collective-permute-start(f32[320,512]{1,0:T(8,128)S(1)} %shard_map.97.proj_mine), channel_id=1, source_target_pairs={{0,1},{1,0},{2,3},{3,2},{4,5},{5,4},{6,7},{7,6},{8,9},{9,8},{10,11... | collective-permute-start | bytes 1966088 | tf_op jit(solution)/shard_map/ppermute | solution.py:428
  124.3 25.4 %collective-permute-start.14 = (bf16[128,3584]{1,0:T(8,128)(2,1)S(1)}, bf16[128,3584]{1,0:T(8,128)(2,1)S(1)}, u32[]{:S(2)}, u32[]{:S(2)}) collective-permute-start(bf16[128,3584]{1,0:T(8,128)(2,1)S(1)} %get-tuple-element.69), channel_id=1, source_target_pairs={{0,2},{2,0},{4,6},{6,4},{8,10},{10,8},{12,14},{14,12},{16,18},{18,... | collective-permute-start | bytes 2752520 | tf_op jit(solution)/shard_map/ppermute | solution.py:349
  125.8 23.9 %collective-permute-start.15 = (bf16[128,3584]{1,0:T(8,128)(2,1)S(1)}, bf16[128,3584]{1,0:T(8,128)(2,1)S(1)}, u32[]{:S(2)}, u32[]{:S(2)}) collective-permute-start(bf16[128,3584]{1,0:T(8,128)(2,1)S(1)} %get-tuple-element.70), channel_id=1, source_target_pairs={{0,4},{2,6},{4,0},{6,2},{8,12},{10,14},{12,8},{14,10},{16,20},{18,... | collective-permute-start | bytes 2752520 | tf_op jit(solution)/shard_map/ppermute | solution.py:349
  134.7 14.9 %collective-permute-start.12 = (bf16[80,3712]{1,0:T(8,128)(2,1)S(1)}, bf16[80,3712]{1,0:T(8,128)(2,1)S(1)}, u32[]{:S(2)}, u32[]{:S(2)}) collective-permute-start(bf16[80,3712]{1,0:T(8,128)(2,1)S(1)} %get-tuple-element.67), channel_id=1, source_target_pairs={{8,0},{10,2},{12,4},{14,6},{16,24},{18,26},{20,28},{22,30},{0,8},{... | collective-permute-start | bytes 1781768 | tf_op jit(solution)/shard_map/ppermute | solution.py:349
  136.4 13.3 %collective-permute-start.13 = (bf16[80,3712]{1,0:T(8,128)(2,1)S(1)}, bf16[80,3712]{1,0:T(8,128)(2,1)S(1)}, u32[]{:S(2)}, u32[]{:S(2)}) collective-permute-start(bf16[80,3712]{1,0:T(8,128)(2,1)S(1)} %get-tuple-element.77), channel_id=1, source_target_pairs={{8,16},{10,18},{12,20},{14,22},{16,8},{18,10},{20,12},{22,14},{9,1... | collective-permute-start | bytes 1781768 | tf_op jit(solution)/shard_map/ppermute | solution.py:349
  149.8 30.4 %collective-permute-start.16 = (bf16[80,3712]{1,0:T(8,128)(2,1)S(1)}, bf16[80,3712]{1,0:T(8,128)(2,1)S(1)}, u32[]{:S(2)}, u32[]{:S(2)}) collective-permute-start(bf16[80,3712]{1,0:T(8,128)(2,1)S(1)} %select_add_fusion), channel_id=1, source_target_pairs={{0,16},{2,18},{4,20},{6,22},{8,24},{10,26},{12,28},{14,30},{16,0},... | collective-permute-start | bytes 1781768 | tf_op jit(solution)/shard_map/ppermute | solution.py:349
  155.6 24.6 %collective-permute-start.17 = (bf16[80,3712]{1,0:T(8,128)(2,1)S(1)}, bf16[80,3712]{1,0:T(8,128)(2,1)S(1)}, u32[]{:S(2)}, u32[]{:S(2)}) collective-permute-start(bf16[80,3712]{1,0:T(8,128)(2,1)S(1)} %get-tuple-element.77), channel_id=1, source_target_pairs={{0,8},{2,10},{4,12},{6,14},{24,16},{26,18},{28,20},{30,22},{1,9},{... | collective-permute-start | bytes 1781768 | tf_op jit(solution)/shard_map/ppermute | solution.py:349
  157.0 23.7 %collective-permute-start.18 = (bf16[64,3584]{1,0:T(8,128)(2,1)S(1)}, bf16[64,3584]{1,0:T(8,128)(2,1)S(1)}, u32[]{:S(2)}, u32[]{:S(2)}) collective-permute-start(bf16[64,3584]{1,0:T(8,128)(2,1)S(1)} %slice_add_fusion.1), channel_id=1, source_target_pairs={{0,2},{2,0},{4,6},{6,4},{8,10},{10,8},{12,14},{14,12},{16,18},{18,... | collective-permute-start | bytes 1376264 | tf_op jit(solution)/shard_map/ppermute | solution.py:349
  157.7 23.0 %collective-permute-start.19 = (bf16[64,3584]{1,0:T(8,128)(2,1)S(1)}, bf16[64,3584]{1,0:T(8,128)(2,1)S(1)}, u32[]{:S(2)}, u32[]{:S(2)}) collective-permute-start(bf16[64,3584]{1,0:T(8,128)(2,1)S(1)} %slice_add_fusion), channel_id=1, source_target_pairs={{0,4},{2,6},{4,0},{6,2},{8,12},{10,14},{12,8},{14,10},{16,20},{18,... | collective-permute-start | bytes 1376264 | tf_op jit(solution)/shard_map/ppermute | solution.py:349
  180.7 1.6 collective-permute-start.20
  181.1 1.2 copy-start.1
  181.1 1.2 copy-start.2
  181.2 1.2 copy-start.3
  181.2 1.2 copy-start.4

commit v6 on v5

--- a/solution.py
+++ b/solution.py
@@ -28,8 +28,8 @@
     return (member > 0) & (member < SPLIT // QUAD - 1)
 
 
-def slot_rows(blocks, first, count, columns):
-    own, far, ends, outer, middle = [b[first : first + count, columns] for b in blocks]
+def slot_rows(blocks):
+    own, far, ends, outer, middle = [b[...] for b in blocks]
     return jnp.concatenate([own, far, ends, jnp.where(inner_chip(), middle, outer)], axis=0)
 
 
@@ -37,17 +37,12 @@
     return total // 2 // 256 * 256
 
 
-def prep_kernel(held, capacity, *refs):
-    gate, up, down, tokens, cotangent, logits, ids = refs[:7]
-    weights, top, low, mine, other, pick_out = refs[7:13]
-    chosen_out, inv_w_out, inv_total_out, packed, sems = refs[13:]
+def pack_kernel(gate, up, down, weights, top, low, packed, sems):
     ff = gate.shape[2]
-    part = mine.shape[2]
     wide = 2 * ff
-    core = lax.axis_index("dp")
-    start = pl.multiple_of(core * part, 128)
-    away = pl.multiple_of((1 - core) * part, 128)
+    part = packed.shape[0] * 2 // 3
     split = top.shape[0]
+    start = pl.multiple_of(lax.axis_index("dp") * part, 128)
     half = pl.ds(start, part)
     pairs = [
         (gate.at[0, half, :], packed.at[:part, :ff]),
@@ -63,6 +58,25 @@
     ]
     for copy in copies[:reads]:
         copy.start()
+    for copy in copies[:reads]:
+        copy.wait()
+    for copy in copies[reads:]:
+        copy.start()
+    for copy in copies[reads:]:
+        copy.wait()
+
+
+def arrived_kernel(w1, w2_top, w2_low, mark):
+    mark[...] = jnp.zeros_like(mark)
+
+
+def prep_kernel(held, capacity, *refs):
+    tokens, cotangent, logits, ids = refs[:4]
+    mine, other, pick_out, chosen_out, inv_w_out, inv_total_out = refs[4:]
+    part = mine.shape[2]
+    core = lax.axis_index("dp")
+    start = pl.multiple_of(core * part, 128)
+    away = pl.multiple_of((1 - core) * part, 128)
 
     experts, count = logits.shape
     expert = lax.broadcasted_iota(jnp.int32, (experts, count), 0)
@@ -105,13 +119,7 @@
             out[1, :, pl.ds(at, step)] = (c * value).astype(bf16)
         return carry
 
-    for copy in copies[:reads]:
-        copy.wait()
-    for copy in copies[reads:]:
-        copy.start()
     lax.fori_loop(0, part // step, body, 0)
-    for copy in copies[reads:]:
-        copy.wait()
 
 
 def sum_kernel(own, far, ends, outer, middle, mine, other, tail):
@@ -138,66 +146,63 @@
     tail[...] = total(slice(part, part + 128))[0]
 
 
-def piece_sides(pieces):
-    split = pieces[2].shape[0]
-    upper = [(pieces[0], 0), (pieces[1], 0), (pieces[2], 0), (pieces[4], 0)]
-    lower = [(pieces[0], split), (pieces[1], split), (pieces[3], 0), (pieces[5], 0)]
-    return split, upper, lower
-
-
-def gate_up_kernel(*refs):
+def step_of(part, split):
+    for step in (512, 256):
+        if part % step == 0 and split % step == 0:
+            return step
+    return 128
+
+
+def row_specs(count, step, half):
+    spec = pl.BlockSpec((count, step), lambda i: (half, i))
+    return [spec] * 5
+
+
+def piece_specs(step, split, wide):
+    upper = split // step
+    whole = pl.BlockSpec((step, wide), lambda i: (i, 0))
+    top = pl.BlockSpec((step, wide), lambda i: (jnp.minimum(i, upper - 1), 0))
+    low = pl.BlockSpec((step, wide), lambda i: (jnp.maximum(i - upper, 0), 0))
+    return [whole, whole, top, low, top, low]
+
+
+def piece_blocks(pieces, upper):
+    here = pl.program_id(0) < upper
+    first, second, top2, low2, top3, low3 = [p[...] for p in pieces]
+    return [first, second, jnp.where(here, top2, low2), jnp.where(here, top3, low3)]
+
+
+def gate_up_kernel(upper, *refs):
     blocks, pieces, out = refs[:5], refs[5:-1], refs[-1]
     wide = pieces[0].shape[1]
-    part = blocks[0].shape[1]
-    count = out.shape[0] // (SPLIT // QUAD)
-    split, upper, lower = piece_sides(pieces)
-    out[...] = jnp.zeros_like(out)
-    for side, first, size in ((upper, 0, split), (lower, split, part - split)):
-        step = chunk_of(size, 1024)
-
-        def body(k, carry):
-            columns = pl.ds(pl.multiple_of(first + k * step, 128), step)
-            x = slot_rows(blocks, 0, count, columns)
-            for q, (ref, base) in enumerate(side):
-                w = ref[pl.ds(pl.multiple_of(base + k * step, 128), step), :]
-                out[:, q * wide : (q + 1) * wide] += jnp.dot(x, w, preferred_element_type=f32)
-            return carry
-
-        lax.fori_loop(0, size // step, body, 0)
+
+    @pl.when(pl.program_id(0) == 0)
+    def _():
+        out[...] = jnp.zeros_like(out)
+
+    x = slot_rows(blocks)
+    for q, w in enumerate(piece_blocks(pieces, upper)):
+        out[:, q * wide : (q + 1) * wide] += jnp.dot(x, w, preferred_element_type=f32)
 
 
 def proj_kernel(*refs):
     blocks, pieces, out = refs[:5], refs[5:-1], refs[-1]
-    wide = pieces[0].shape[1]
+    rows, wide = pieces[0].shape
     ff = wide // 2
-    part = blocks[0].shape[1]
-    count = out.shape[0] // (SPLIT // QUAD)
-    split, upper, lower = piece_sides(pieces)
-    out[...] = jnp.zeros_like(out)
-
-    pair = 2 if part // wide % 2 == 0 else 1
-    step = pair * wide
-
-    def body(k, carry):
-        columns = pl.ds(pl.multiple_of(k * step, 128), step)
-        rows = slot_rows(blocks, count, count, columns)
-        w = jnp.concatenate(
-            [
-                jnp.concatenate(
-                    [
-                        ref[pl.ds(pl.multiple_of(base + part - split + (pair * k + i) * ff, 128), ff), :]
-                        for i in range(pair)
-                    ],
-                    axis=1,
-                )
-                for ref, base in lower
-            ],
-            axis=0,
-        )
-        out[...] += lax.dot_general(rows, w, CONTRACT1, preferred_element_type=f32)
-        return carry
-
-    lax.fori_loop(0, part // step, body, 0)
+
+    @pl.when(pl.program_id(0) == 0)
+    def _():
+        out[...] = jnp.zeros_like(out)
+
+    c = slot_rows(blocks)
+    w = jnp.concatenate(
+        [
+            jnp.concatenate([p[at : at + ff, :] for at in range(0, rows, ff)], axis=1)
+            for p in pieces
+        ],
+        axis=0,
+    )
+    out[...] += lax.dot_general(c, w, CONTRACT1, preferred_element_type=f32)
 
 
 def activations(mine, theirs, q, ff):
@@ -211,75 +216,67 @@
 def down_kernel(mine, theirs, *refs):
     blocks, outs, scratch = refs[:5], refs[5:-1], refs[-1]
     own, sent1, sent2, kept1, kept2 = outs
-    ff, part = own.shape
+    ff = own.shape[0]
     half = ff // 2
-    count = scratch.shape[1] // (SPLIT // QUAD)
-    step = chunk_of(part, 512)
-    for q in range(QUAD):
-        g, u, sig, active = activations(mine, theirs, q, ff)
-        hidden = (active * u).astype(bf16).astype(f32)
-        scratch[q * ff : (q + 1) * ff, :] = hidden.T.astype(bf16)
-
-    def body(k, carry):
-        columns = pl.ds(pl.multiple_of(k * step, 128), step)
-        rows = slot_rows(blocks, count, count, columns)
-        grads = jnp.dot(scratch[...], rows, preferred_element_type=f32).astype(bf16)
-        g0, g1, g2, g3 = [grads[q * ff : (q + 1) * ff] for q in range(QUAD)]
-        own[:, columns] = g0
-        sent1[:, columns] = jnp.concatenate([g3[:half], g1[:half]], axis=0)
-        sent2[:, columns] = jnp.concatenate([g3[half:], g2[half:]], axis=0)
-        kept1[:, columns] = g1[half:]
-        kept2[:, columns] = g2[:half]
-        return carry
-
-    lax.fori_loop(0, part // step, body, 0)
-
-
-def back_kernel(mine, theirs, proj_mine, proj_theirs, *refs):
+    step = blocks[0].shape[1]
+
+    @pl.when(pl.program_id(0) == 0)
+    def _():
+        for q in range(QUAD):
+            g, u, sig, active = activations(mine, theirs, q, ff)
+            hidden = (active * u).astype(bf16).astype(f32)
+            scratch[q * ff : (q + 1) * ff, :] = hidden.T.astype(bf16)
+
+    columns = pl.ds(pl.multiple_of(pl.program_id(0) * step, 128), step)
+    rows = slot_rows(blocks)
+    grads = jnp.dot(scratch[...], rows, preferred_element_type=f32).astype(bf16)
+    g0, g1, g2, g3 = [grads[q * ff : (q + 1) * ff] for q in range(QUAD)]
+    own[:, columns] = g0
+    sent1[:, columns] = jnp.concatenate([g3[:half], g1[:half]], axis=0)
+    sent2[:, columns] = jnp.concatenate([g3[half:], g2[half:]], axis=0)
+    kept1[:, columns] = g1[half:]
+    kept2[:, columns] = g2[:half]
+
+
+def back_kernel(upper, mine, theirs, proj_mine, proj_theirs, *refs):
     members = SPLIT // QUAD
     pieces, outs, scratch = refs[: -members - 1], refs[-members - 1 : -1], refs[-1]
-    wide = pieces[0].shape[1]
+    step, wide = pieces[0].shape
     ff = wide // 2
     rows = outs[0].shape[0]
     part = outs[0].shape[1] - 128
-    split, upper, lower = piece_sides(pieces)
-    dots = 0.0
-    for q in range(QUAD):
-        g, u, sig, active = activations(mine, theirs, q, ff)
-        proj = proj_mine[:, q * ff : (q + 1) * ff] + proj_theirs[:, q * ff : (q + 1) * ff]
-        hidden = (active * u).astype(bf16).astype(f32)
-        dots = dots + jnp.sum(hidden * proj, axis=1, keepdims=True)
-        base = 2 * q * ff
-        scratch[:, base : base + ff] = (proj * u * sig * (1.0 + g * (1.0 - sig))).astype(bf16)
-        scratch[:, base + ff : base + 2 * ff] = (proj * active).astype(bf16)
-
-    high = dots.astype(bf16).astype(f32)
-    rest = dots - high
-    lane = lax.broadcasted_iota(jnp.int32, (rows, 128), 1)
+
+    @pl.when(pl.program_id(0) == 0)
+    def _():
+        dots = 0.0
+        for q in range(QUAD):
+            g, u, sig, active = activations(mine, theirs, q, ff)
+            proj = proj_mine[:, q * ff : (q + 1) * ff] + proj_theirs[:, q * ff : (q + 1) * ff]
+            hidden = (active * u).astype(bf16).astype(f32)
+            dots = dots + jnp.sum(hidden * proj, axis=1, keepdims=True)
+            base = 2 * q * ff
+            dgate = proj * u * sig * (1.0 + g * (1.0 - sig))
+            scratch[:, base : base + ff] = dgate.astype(bf16)
+            scratch[:, base + ff : base + 2 * ff] = (proj * active).astype(bf16)
+
+        high = dots.astype(bf16).astype(f32)
+        rest = dots - high
+        lane = lax.broadcasted_iota(jnp.int32, (rows, 128), 1)
+        for i, out in enumerate(outs):
+            at = 2 if i == 2 else 0
+            top, low = high[i * rows : (i + 1) * rows], rest[i * rows : (i + 1) * rows]
+            out[:, part : part + 128] = jnp.where(
+                lane == at, top, jnp.where(lane == at + 1, low, 0.0)
+            ).astype(bf16)
+
+    columns = pl.ds(pl.multiple_of(pl.program_id(0) * step, 128), step)
+    w = jnp.concatenate(piece_blocks(pieces, upper), axis=1)
+    grads = lax.dot_general(scratch[...], w, CONTRACT1, preferred_element_type=f32)
     for i, out in enumerate(outs):
-        at = 2 if i == 2 else 0
-        top, low = high[i * rows : (i + 1) * rows], rest[i * rows : (i + 1) * rows]
-        out[:, part : part + 128] = jnp.where(
-            lane == at, top, jnp.where(lane == at + 1, low, 0.0)
-        ).astype(bf16)
-    for side, first, size in ((upper, 0, split), (lower, split, part - split)):
-        step = chunk_of(size, 256)
-
-        def body(k, carry):
-            columns = pl.ds(pl.multiple_of(first + k * step, 128), step)
-            w = jnp.concatenate(
-                [ref[pl.ds(pl.multiple_of(base + k * step, 128), step), :] for ref, base in side],
-                axis=1,
-            )
-            grads = lax.dot_general(scratch[...], w, CONTRACT1, preferred_element_type=f32)
-            for i, out in enumerate(outs):
-                out[:, columns] = grads[i * rows : (i + 1) * rows].astype(bf16)
-            return carry
-
-        lax.fori_loop(0, size // step, body, 0)
-
-
-def final_kernel(held, pick, mine, theirs, tail, chosen, inv_w, inv_total, tok_out, logit_out):
+        out[:, columns] = grads[i * rows : (i + 1) * rows].astype(bf16)
+
+
+def final_kernel(held, pick, mine, theirs, tail, chosen, inv_w, inv_total, mark, tok_out, logit_out):
     core = lax.axis_index("dp")
     slots, part = mine.shape
     step = chunk_of(part, 512)
@@ -312,10 +309,11 @@
     logit_out[...] = SCALE * inv_total[...] * (dw - inner) * share * (1.0 - share)
 
 
-def call(kernel, outs, in_specs, scratch, flops, moved, limit=20, out_specs=None):
+def call(kernel, outs, in_specs, scratch, flops, moved, limit=20, out_specs=None, grid=()):
     return pl.pallas_call(
         kernel,
         out_shape=outs,
+        grid=grid,
         in_specs=in_specs,
         out_specs=out_specs or [VMEM] * len(outs),
         scratch_shapes=scratch,
@@ -367,19 +365,28 @@
     split = split_of(packed)
     shape = jax.ShapeDtypeStruct
     hbm = pl.BlockSpec(memory_space=pltpu.HBM)
-    weights, w_top, w_low, mine, other, pick, chosen, inv_w, inv_total = call(
+    weights, w_top, w_low = call(
+        pack_kernel,
+        [shape((size, 2 * ff), bf16) for size in (packed, split, packed - split)],
+        [hbm] * 3,
+        [pltpu.VMEM((packed, 2 * ff), bf16), pltpu.SemaphoreType.DMA((5 + part // (2 * ff),))],
+        0,
+        12 * part * ff,
+        limit=58,
+        out_specs=[hbm] * 3,
+    )(gate_proj, up_proj, down_proj)
+    weights, w_top, w_low, logits, tokens = barrier((weights, w_top, w_low, logits, tokens))
+    mine, other, pick, chosen, inv_w, inv_total = call(
         lambda *refs: prep_kernel(held, capacity, *refs),
-        [shape((size, 2 * ff), bf16) for size in (packed, split, packed - split)]
-        + [shape((2, rows_dev, part), bf16)] * 2
+        [shape((2, rows_dev, part), bf16)] * 2
         + [shape((rows_dev, tok_count), bf16)]
         + [shape((experts, tok_count), f32)] * 3,
-        [hbm] * 3 + [VMEM] * 4,
-        [pltpu.VMEM((packed, 2 * ff), bf16), pltpu.SemaphoreType.DMA((5 + part // (2 * ff),))],
+        [VMEM] * 4,
+        [],
         4 * rows_dev * tok_count * width,
-        12 * part * ff + 4 * tok_count * width,
+        4 * tok_count * width,
         limit=58,
-        out_specs=[hbm] * 3 + [VMEM] * 6,
-    )(gate_proj, up_proj, down_proj, tokens, cotangent, logits.T, expert_ids.T)
+    )(tokens, cotangent, logits.T, expert_ids.T)
     w1 = send(weights, swap1)
     w2_top = send(w_top, swap2)
     w2_low = send(w_low, swap2)
@@ -399,7 +406,17 @@
         own = own.reshape(2 * rows_chip, part)
     far = send(own, distant)
     outer = send(own, outward)
-    w1, w2_top, w2_low, own, far, outer = barrier((w1, w2_top, w2_low, own, far, outer))
+    (mark,) = call(
+        arrived_kernel,
+        [shape((8, 128), f32)],
+        [pl.BlockSpec(memory_space=pl.ANY)] * 3,
+        [],
+        8 * slots * part * QUAD * ff * 8,
+        0,
+    )(w1, w2_top, w2_low)
+    w1, w2_top, w2_low, own, far, outer, mark = barrier(
+        (w1, w2_top, w2_low, own, far, outer, mark)
+    )
     w3_top = send(w2_top, swap1)
     w3_low = send(w1[split:], swap2)
     ends = send(jnp.where(inner, far, own), outward + inward)
@@ -408,42 +425,53 @@
     blocks = [own, far, ends, outer, middle]
 
     matmul = 2 * slots * part * QUAD * ff
+    step = step_of(part, split)
+    upper = split // step
+    grid = (part // step,)
+    w_specs = piece_specs(step, split, 2 * ff)
     (g_u,) = call(
-        gate_up_kernel,
+        lambda *refs: gate_up_kernel(upper, *refs),
         [shape((slots, QUAD * 2 * ff), f32)],
-        [VMEM] * 11,
+        row_specs(rows_chip, step, 0) + w_specs,
         [],
         2 * matmul,
         2 * part * (slots + QUAD * 2 * ff),
+        grid=grid,
     )(*blocks, *w)
     g_u_sib = lax.ppermute(g_u, "dp", sibling)
+    half = step // 2
+    in_whole = pl.BlockSpec((half, 2 * ff), lambda i: (part // half + i, 0))
+    in_low = pl.BlockSpec((half, 2 * ff), lambda i: ((part - split) // half + i, 0))
     (proj,) = call(
         proj_kernel,
         [shape((slots, QUAD * ff), f32)],
-        [VMEM] * 11,
+        row_specs(rows_chip, step, 1) + [in_whole, in_whole, in_low, in_low],
         [],
         matmul,
         2 * part * (slots + QUAD * ff),
-    )(*blocks, *w)
+        grid=grid,
+    )(*blocks, weights, w1, w2_low, w3_low)
     proj_sib = lax.ppermute(proj, "dp", sibling)
     g0, sent1, sent2, kept1, kept2 = call(
         down_kernel,
         [shape((ff, part), bf16)] * 3 + [shape((lowf, part), bf16)] * 2,
-        [VMEM] * 7,
+        [VMEM] * 2 + row_specs(rows_chip, step, 1),
         [pltpu.VMEM((QUAD * ff, slots), bf16)],
         matmul,
         2 * part * (slots + QUAD * ff),
+        grid=grid,
     )(g_u, g_u_sib, *blocks)
     g0, sent1, sent2, proj, proj_sib = barrier((g0, sent1, sent2, proj, proj_sib))
     got1 = send(sent1, swap1)
     got2 = send(sent2, swap2)
     b0, b1, b2, b3 = call(
-        back_kernel,
+        lambda *refs: back_kernel(upper, *refs),
         [shape((rows_chip, part + 128), bf16)] * members,
-        [VMEM] * 10,
+        [VMEM] * 4 + w_specs,
         [pltpu.VMEM((slots, QUAD * 2 * ff), bf16)],
         2 * matmul,
         2 * part * (slots + QUAD * 2 * ff),
+        grid=grid,
     )(g_u, g_u_sib, proj, proj_sib, *w)
 
     ends = send(b2, outward + inward)
@@ -487,11 +515,11 @@
             shape((tok_count, width), bf16),
             shape((experts, tok_count), f32),
         ],
-        [VMEM] * 7,
+        [VMEM] * 8,
         [],
         2 * tok_count * rows_dev * width,
         2 * width * (tok_count + rows_dev),
-    )(pick, mine, theirs, tail, chosen, inv_w, inv_total)
+    )(pick, mine, theirs, tail, chosen, inv_w, inv_total, mark)
     return (token_grad, logit_grad.T, down_grad)
 
 

time: 186 us -> 186 us (level)
  waiting for transfers between devices: 116 us -> 119 us
  other arithmetic: 5.16 us -> 2.85 us
    ppermute x17, waiting for transfers between devices: 116 us -> 118 us  [send(): return lax.ppermute(array, 'expert', route)]
    pallas_call x4 -> x6, Pallas kernels: 26.7 us -> 27.4 us  [the longest x1 6.65 us: per_device(): call(lambda *refs: back_kernel(upper, *refs), [shape((rows_chip, part + 1...]
  transfers between devices with their start and end apart: 21 -> 21, of which waited for: 8 -> 8; matrix products, arithmetic and copies ran while one was open for 3% -> 2% of each run, Pallas kernels for 10% -> 11%
where the time goes in v6:
time: 186 us; the launch traced here: 185 us
  waiting for transfers between devices  119 us (64%)
  Pallas kernels  34.6 us (19%)
  starting transfers between devices  28.1 us (15%)
  other arithmetic  2.85 us (2%)
    ppermute x17, waiting for transfers between devices, send(): return lax.ppermute(array, 'expert', route)  118 us
    ppermute x17, starting transfers between devices, send(): return lax.ppermute(array, 'expert', route)  27.4 us
    pallas_call x1, Pallas kernels, per_device(): call(lambda *refs: back_kernel(upper, *refs), [shape((rows_chip, part + 1...  6.65 us
    pallas_call x1, Pallas kernels, per_device(): call(lambda *refs: gate_up_kernel(upper, *refs), [shape((slots, QUAD * 2...  6.33 us
    pallas_call x1, Pallas kernels, per_device(): call(proj_kernel, [shape((slots, QUAD * ff), f32)], row_specs(rows_chip,...  5.44 us
    pallas_call x1, Pallas kernels, per_device(): call(lambda *refs: prep_kernel(held, capacity, *refs), [shape((2, rows_de...  4.74 us
    pallas_call x1, Pallas kernels, per_device(): call(pack_kernel, [shape((size, 2 * ff), bf16) for size in (packed, split...  4.27 us
  transfers between devices with their start and end apart: 21, of which 8 were waited for; matrix products, arithmetic and copies ran while one was open for 2% of the time, Pallas kernels for 11%

profile of v6, /device:TPU:0, one launch (start us, length us, event | category | flops | bytes accessed | tf_op | source)
XLA Modules:
  0.0 185.1 jit_solution(9863873848969224597)
XLA Ops:
  0.6 4.3 %shard_map.94 = (bf16[5376,256]{1,0:T(8,128)(2,1)}, bf16[2560,256]{1,0:T(8,128)(2,1)}, bf16[2816,256]{1,0:T(8,128)(2,1)}) custom-call(bf16[1,7168,128]{2,1,0:T(8,128)(2,1)} %gate.1, bf16[1,7168,128]{2,1,0:T(8,128)(2,1)} %up.1, bf16[1,128,7168]{2,1,0:T(8,128)(2,1)} %down.1), custom_call_target="tpu_custom_call" | custom-call | bytes 5505024 | tf_op jit(solution)/shard_map/pallas_call | solution.py:368
  4.9 3.0 %collective-permute-start = (bf16[5376,256]{1,0:T(8,128)(2,1)}, bf16[5376,256]{1,0:T(8,128)(2,1)S(1)}, u32[]{:S(2)}, u32[]{:S(2)}) collective-permute-start(bf16[5376,256]{1,0:T(8,128)(2,1)} %get-tuple-element.61.refs_5_.refs_4_), channel_id=1, source_target_pairs={{0,2},{2,0},{4,6},{6,4},{8,10},{10,8},{12,14},{14,12},{16,18},{18,... | collective-permute-start | bytes 8257544 | tf_op jit(solution)/shard_map/ppermute | solution.py:347
  7.9 4.7 %shard_map.95 = (bf16[2,40,3584]{2,1,0:T(8,128)(2,1)}, bf16[2,40,3584]{2,1,0:T(8,128)(2,1)}, bf16[40,128]{1,0:T(8,128)(2,1)}, f32[32,128]{1,0:T(8,128)}, f32[32,128]{1,0:T(8,128)}, /*index=5*/f32[32,128]{1,0:T(8,128)}) custom-call(bf16[128,7168]{1,0:T(8,128)(2,1)} %refs_0_, bf16[128,7168]{1,0:T(8,128)(2,1)} %refs_1_.1, f32[32,128]{1,0:T(8,128)} %bitcast.13, ...), custom_call_target="tpu_custom_call" | custom-call | flops 146800640 | bytes 3670016 | tf_op jit(solution)/shard_map/pallas_call | solution.py:379
  12.7 0.0 collective-permute-start.3
  12.7 1.6 collective-permute-start.2
  14.2 0.5 collective-permute-start.1
  14.8 0.1 collective-permute-done.3
  14.8 1.1 select_bitcast_fusion.3
  16.0 0.1 pad_maximum_fusion.refs_0_
  16.1 2.7 %collective-permute-start.4 = (bf16[160,3584]{1,0:T(8,128)(2,1)S(1)}, bf16[160,3584]{1,0:T(8,128)(2,1)S(1)}, u32[]{:S(2)}, u32[]{:S(2)}) collective-permute-start(bf16[160,3584]{1,0:T(8,128)(2,1)S(1)} %pad_maximum_fusion.refs_0_), channel_id=1, source_target_pairs={{0,16},{2,18},{4,20},{6,22},{8,24},{10,26},{12,28},{14,30},{16,0},... | collective-permute-start | bytes 3440648 | tf_op jit(solution)/shard_map/ppermute | solution.py:347
  18.7 1.3 collective-permute-start.5
  20.0 55.0 %collective-permute-done.1.w2_top.refs_7_.refs_6_ = bf16[2560,256]{1,0:T(8,128)(2,1)} collective-permute-done((bf16[2560,256]{1,0:T(8,128)(2,1)}, bf16[2560,256]{1,0:T(8,128)(2,1)}, u32[]{:S(2)}, u32[]{:S(2)}) %collective-permute-start.1) | collective-permute-done | bytes 1310752 | tf_op jit(solution)/shard_map/ppermute | solution.py:347
  75.1 0.0 collective-permute-done.2.w2_low.refs_8_.refs_7_
  75.1 0.0 collective-permute-done.w1.refs_6_.refs_5_
  75.1 0.0 collective-permute-done.4.refs_1_
  75.1 0.0 collective-permute-done.5.refs_3_
  75.1 0.4 collective-permute-start.8
  75.5 0.1 slice.41
  75.6 0.0 copy-start
  75.6 1.8 collective-permute-start.9
  77.4 0.1 broadcast_select_fusion
  77.5 1.6 collective-permute-start.6
  79.2 0.7 collective-permute-start.7
  79.9 24.0 %collective-permute-done.6.refs_2_ = bf16[160,3584]{1,0:T(8,128)(2,1)S(1)} collective-permute-done((bf16[160,3584]{1,0:T(8,128)(2,1)S(1)}, bf16[160,3584]{1,0:T(8,128)(2,1)S(1)}, u32[]{:S(2)}, u32[]{:S(2)}) %collective-permute-start.6) | collective-permute-done | bytes 1146912 | tf_op jit(solution)/shard_map/ppermute | solution.py:347
  103.8 0.0 collective-permute-done.7.refs_4_
  103.8 1.9 %collective-permute-done.8.refs_9_.refs_8_ = bf16[2560,256]{1,0:T(8,128)(2,1)S(1)} collective-permute-done((bf16[2560,256]{1,0:T(8,128)(2,1)}, bf16[2560,256]{1,0:T(8,128)(2,1)S(1)}, u32[]{:S(2)}, u32[]{:S(2)}) %collective-permute-start.8) | collective-permute-done | bytes 1310752 | tf_op jit(solution)/shard_map/ppermute | solution.py:347
  105.7 3.0 %collective-permute-done.9.refs_10_.refs_8_.refs_9_ = bf16[2816,256]{1,0:T(8,128)(2,1)S(1)} collective-permute-done((bf16[2816,256]{1,0:T(8,128)(2,1)S(1)}, bf16[2816,256]{1,0:T(8,128)(2,1)S(1)}, u32[]{:S(2)}, u32[]{:S(2)}) %collective-permute-start.9) | collective-permute-done | bytes 1441824 | tf_op jit(solution)/shard_map/ppermute | solution.py:347
  108.7 0.0 copy-done
  108.7 6.3 %shard_map.97.mine.refs_0_ = f32[320,1024]{1,0:T(8,128)S(1)} custom-call(bf16[160,3584]{1,0:T(8,128)(2,1)S(1)} %pad_maximum_fusion.refs_0_, bf16[160,3584]{1,0:T(8,128)(2,1)S(1)} %collective-permute-done.4.refs_1_, bf16[160,3584]{1,0:T(8,128)(2,1)S(1)} %collective-permute-done.6.refs_2_, bf16[160,3584]{1,0:T(8,128)(2,1)S(1)} %collective-permute-done.5.refs_3_, ...), custom_call_target="tpu_custom_call" | custom-call | flops 2348810240 | bytes 9633792 | tf_op jit(solution)/shard_map/pallas_call | solution.py:432
  115.1 0.1 collective-permute-start.10
  115.1 5.4 %shard_map.99.refs_2_ = f32[320,512]{1,0:T(8,128)S(1)} custom-call(bf16[160,3584]{1,0:T(8,128)(2,1)S(1)} %pad_maximum_fusion.refs_0_, bf16[160,3584]{1,0:T(8,128)(2,1)S(1)} %collective-permute-done.4.refs_1_, bf16[160,3584]{1,0:T(8,128)(2,1)S(1)} %collective-permute-done.6.refs_2_, bf16[160,3584]{1,0:T(8,128)(2,1)S(1)} %collective-permute-done.5.refs_3_, ...), custom_call_target="tpu_custom_call" | custom-call | flops 1174405120 | bytes 5963776 | tf_op jit(solution)/shard_map/pallas_call | solution.py:445
  120.6 0.5 collective-permute-start.11
  121.1 0.0 collective-permute-done.10.theirs.refs_1_
  121.1 3.7 %shard_map.98 = (bf16[128,3584]{1,0:T(8,128)(2,1)S(1)}, bf16[128,3584]{1,0:T(8,128)(2,1)S(1)}, bf16[128,3584]{1,0:T(8,128)(2,1)S(1)}, bf16[64,3584]{1,0:T(8,128)(2,1)S(1)}, bf16[64,3584]{1,0:T(8,128)(2,1)S(1)}) custom-call(f32[320,1024]{1,0:T(8,128)S(1)} %shard_map.97.mine.refs_0_, f32[320,1024]{1,0:T(8,128)S(1)} %collective-permute-done.10.theirs.refs_1_, ...), custom_call_target="tpu_custom_call" | custom-call | flops 1174405120 | bytes 5963776 | tf_op jit(solution)/shard_map/pallas_call | solution.py:455
  124.8 0.0 collective-permute-done.11.refs_3_
  124.8 1.6 collective-permute-start.14
  126.4 1.5 collective-permute-start.15
  127.9 6.6 %shard_map.100 = (bf16[80,3712]{1,0:T(8,128)(2,1)S(1)}, bf16[80,3712]{1,0:T(8,128)(2,1)S(1)}, bf16[80,3712]{1,0:T(8,128)(2,1)S(1)}, bf16[80,3712]{1,0:T(8,128)(2,1)S(1)}) custom-call(f32[320,1024]{1,0:T(8,128)S(1)} %shard_map.97.mine.refs_0_, f32[320,1024]{1,0:T(8,128)S(1)} %collective-permute-done.10.theirs.refs_1_, f32[320,512]{1,0:T(8,128)S(1)} %shard_map.99.refs_2_, ...), custom_call_target="tpu_custom_call" | custom-call | flops 2348810240 | bytes 9633792 | tf_op jit(solution)/shard_map/pallas_call | solution.py:467
  134.6 1.6 collective-permute-start.12
  136.2 0.7 collective-permute-start.13
  136.9 12.5 %collective-permute-done.12.ends = bf16[80,3712]{1,0:T(8,128)(2,1)S(1)} collective-permute-done((bf16[80,3712]{1,0:T(8,128)(2,1)S(1)}, bf16[80,3712]{1,0:T(8,128)(2,1)S(1)}, u32[]{:S(2)}, u32[]{:S(2)}) %collective-permute-start.12) | collective-permute-done | bytes 593952 | tf_op jit(solution)/shard_map/ppermute | solution.py:347
  149.4 0.0 collective-permute-done.13.middle
  149.4 0.0 collective-permute-done.14
  149.4 0.0 collective-permute-done.15
  149.4 0.1 select_add_fusion
  149.5 5.9 %collective-permute-start.16 = (bf16[80,3712]{1,0:T(8,128)(2,1)S(1)}, bf16[80,3712]{1,0:T(8,128)(2,1)S(1)}, u32[]{:S(2)}, u32[]{:S(2)}) collective-permute-start(bf16[80,3712]{1,0:T(8,128)(2,1)S(1)} %select_add_fusion), channel_id=1, source_target_pairs={{0,16},{2,18},{4,20},{6,22},{8,24},{10,26},{12,28},{14,30},{16,0},... | collective-permute-start | bytes 1781768 | tf_op jit(solution)/shard_map/ppermute | solution.py:347
  155.4 1.3 collective-permute-start.17
  156.7 0.1 slice_add_fusion.1
  156.8 0.6 collective-permute-start.18
  157.5 0.6 collective-permute-start.19
  158.0 21.9 %collective-permute-done.16.far = bf16[80,3712]{1,0:T(8,128)(2,1)S(1)} collective-permute-done((bf16[80,3712]{1,0:T(8,128)(2,1)S(1)}, bf16[80,3712]{1,0:T(8,128)(2,1)S(1)}, u32[]{:S(2)}, u32[]{:S(2)}) %collective-permute-start.16) | collective-permute-done | bytes 593952 | tf_op jit(solution)/shard_map/ppermute | solution.py:347
  179.9 0.0 collective-permute-done.17.outer
  179.9 0.5 shard_map.101
  180.4 0.0 collective-permute-done.18
  180.4 0.0 collective-permute-done.19
  180.5 0.1 collective-permute-start.20
  180.5 0.3 add_convert_fusion.1
  180.9 0.0 copy-start.1
  180.9 0.0 copy-start.2
  180.9 0.0 copy-start.3
  180.9 1.0 maximum_bitcast_fusion
  181.9 0.2 collective-permute-done.20.refs_2_
  182.1 0.0 copy-done.4
  182.1 3.0 %shard_map.102 = (bf16[128,7168]{1,0:T(8,128)(2,1)}, f32[32,128]{1,0:T(8,128)}) custom-call(bf16[40,128]{1,0:T(8,128)(2,1)S(1)} %copy-done.4, bf16[40,3584]{1,0:T(8,128)(2,1)S(1)} %get-tuple-element.90.refs_1_, bf16[40,3584]{1,0:T(8,128)(2,1)S(1)} %collective-permute-done.20.refs_2_, f32[40,128]{1,0:T(8,128)S(1)} %get-tuple-element.97.refs_3_, ...), custom_call_target="tpu_custom_call" | custom-call | flops 73400320 | bytes 2408448 | tf_op jit(solution)/shard_map/pallas_call | solution.py:512
  (6 shorter events, 0.1 us)
Async XLA Ops:
  4.9 70.2 %collective-permute-start = (bf16[5376,256]{1,0:T(8,128)(2,1)}, bf16[5376,256]{1,0:T(8,128)(2,1)S(1)}, u32[]{:S(2)}, u32[]{:S(2)}) collective-permute-start(bf16[5376,256]{1,0:T(8,128)(2,1)} %get-tuple-element.61.refs_5_.refs_4_), channel_id=1, source_target_pairs={{0,2},{2,0},{4,6},{6,4},{8,10},{10,8},{12,14},{14,12},{16,18},{18,... | collective-permute-start | bytes 8257544 | tf_op jit(solution)/shard_map/ppermute | solution.py:347
  12.7 2.2 %collective-permute-start.3 = (bf16[2,40,3584]{2,1,0:T(8,128)(2,1)}, bf16[2,40,3584]{2,1,0:T(8,128)(2,1)S(1)}, u32[]{:S(2)}, u32[]{:S(2)}) collective-permute-start(bf16[2,40,3584]{2,1,0:T(8,128)(2,1)} %get-tuple-element.65), channel_id=1, source_target_pairs={{0,1},{1,0},{2,3},{3,2},{4,5},{5,4},{6,7},{7,6},{8,9},{9,8},{10,11... | collective-permute-start | bytes 1720328 | tf_op jit(solution)/shard_map/ppermute | solution.py:394
  12.7 62.4 %collective-permute-start.2 = (bf16[2816,256]{1,0:T(8,128)(2,1)}, bf16[2816,256]{1,0:T(8,128)(2,1)}, u32[]{:S(2)}, u32[]{:S(2)}) collective-permute-start(bf16[2816,256]{1,0:T(8,128)(2,1)} %get-tuple-element.63), channel_id=1, source_target_pairs={{0,4},{2,6},{4,0},{6,2},{8,12},{10,14},{12,8},{14,10},{16,20},{18,... | collective-permute-start | bytes 4325384 | tf_op jit(solution)/shard_map/ppermute | solution.py:347
  14.2 60.8 %collective-permute-start.1 = (bf16[2560,256]{1,0:T(8,128)(2,1)}, bf16[2560,256]{1,0:T(8,128)(2,1)}, u32[]{:S(2)}, u32[]{:S(2)}) collective-permute-start(bf16[2560,256]{1,0:T(8,128)(2,1)} %get-tuple-element.62), channel_id=1, source_target_pairs={{0,4},{2,6},{4,0},{6,2},{8,12},{10,14},{12,8},{14,10},{16,20},{18,... | collective-permute-start | bytes 3932168 | tf_op jit(solution)/shard_map/ppermute | solution.py:347
  16.1 59.0 %collective-permute-start.4 = (bf16[160,3584]{1,0:T(8,128)(2,1)S(1)}, bf16[160,3584]{1,0:T(8,128)(2,1)S(1)}, u32[]{:S(2)}, u32[]{:S(2)}) collective-permute-start(bf16[160,3584]{1,0:T(8,128)(2,1)S(1)} %pad_maximum_fusion.refs_0_), channel_id=1, source_target_pairs={{0,16},{2,18},{4,20},{6,22},{8,24},{10,26},{12,28},{14,30},{16,0},... | collective-permute-start | bytes 3440648 | tf_op jit(solution)/shard_map/ppermute | solution.py:347
  18.7 56.4 %collective-permute-start.5 = (bf16[160,3584]{1,0:T(8,128)(2,1)S(1)}, bf16[160,3584]{1,0:T(8,128)(2,1)S(1)}, u32[]{:S(2)}, u32[]{:S(2)}) collective-permute-start(bf16[160,3584]{1,0:T(8,128)(2,1)S(1)} %pad_maximum_fusion.refs_0_), channel_id=1, source_target_pairs={{8,0},{10,2},{12,4},{14,6},{16,24},{18,26},{20,28},{22,30},{9,1},{... | collective-permute-start | bytes 3440648 | tf_op jit(solution)/shard_map/ppermute | solution.py:347
  75.1 30.6 %collective-permute-start.8 = (bf16[2560,256]{1,0:T(8,128)(2,1)}, bf16[2560,256]{1,0:T(8,128)(2,1)S(1)}, u32[]{:S(2)}, u32[]{:S(2)}) collective-permute-start(bf16[2560,256]{1,0:T(8,128)(2,1)} %collective-permute-done.1.w2_top.refs_7_.refs_6_), channel_id=1, source_target_pairs={{0,2},{2,0},{4,6},{6,4},{8,10},{10,8},{12,14},{14,12},{16,18},{18,... | collective-permute-start | bytes 3932168 | tf_op jit(solution)/shard_map/ppermute | solution.py:347
  75.6 33.1 %copy-start = (bf16[5376,256]{1,0:T(8,128)(2,1)S(1)}, bf16[5376,256]{1,0:T(8,128)(2,1)}, u32[]{:S(2)}) copy-start(bf16[5376,256]{1,0:T(8,128)(2,1)} %get-tuple-element.61.refs_5_.refs_4_) | copy-start | bytes 8257540
  75.6 33.1 %collective-permute-start.9 = (bf16[2816,256]{1,0:T(8,128)(2,1)S(1)}, bf16[2816,256]{1,0:T(8,128)(2,1)S(1)}, u32[]{:S(2)}, u32[]{:S(2)}) collective-permute-start(bf16[2816,256]{1,0:T(8,128)(2,1)S(1)} %slice.41), channel_id=1, source_target_pairs={{0,4},{2,6},{4,0},{6,2},{8,12},{10,14},{12,8},{14,10},{16,20},{18,... | collective-permute-start | bytes 4325384 | tf_op jit(solution)/shard_map/ppermute | solution.py:347
  77.5 26.3 %collective-permute-start.6 = (bf16[160,3584]{1,0:T(8,128)(2,1)S(1)}, bf16[160,3584]{1,0:T(8,128)(2,1)S(1)}, u32[]{:S(2)}, u32[]{:S(2)}) collective-permute-start(bf16[160,3584]{1,0:T(8,128)(2,1)S(1)} %broadcast_select_fusion), channel_id=1, source_target_pairs={{8,0},{10,2},{12,4},{14,6},{16,24},{18,26},{20,28},{22,30},{0,8},{... | collective-permute-start | bytes 3440648 | tf_op jit(solution)/shard_map/ppermute | solution.py:347
  79.2 24.7 %collective-permute-start.7 = (bf16[160,3584]{1,0:T(8,128)(2,1)S(1)}, bf16[160,3584]{1,0:T(8,128)(2,1)S(1)}, u32[]{:S(2)}, u32[]{:S(2)}) collective-permute-start(bf16[160,3584]{1,0:T(8,128)(2,1)S(1)} %pad_maximum_fusion.refs_0_), channel_id=1, source_target_pairs={{8,16},{10,18},{12,20},{14,22},{16,8},{18,10},{20,12},{22,14},{9,1... | collective-permute-start | bytes 3440648 | tf_op jit(solution)/shard_map/ppermute | solution.py:347
  115.1 6.1 %collective-permute-start.10 = (f32[320,1024]{1,0:T(8,128)S(1)}, f32[320,1024]{1,0:T(8,128)S(1)}, u32[]{:S(2)}, u32[]{:S(2)}) collective-permute-start(f32[320,1024]{1,0:T(8,128)S(1)} %shard_map.97.mine.refs_0_), channel_id=1, source_target_pairs={{0,1},{1,0},{2,3},{3,2},{4,5},{5,4},{6,7},{7,6},{8,9},{9,8},{10,11... | collective-permute-start | bytes 3932168 | tf_op jit(solution)/shard_map/ppermute | solution.py:441
  120.6 4.2 %collective-permute-start.11 = (f32[320,512]{1,0:T(8,128)S(1)}, f32[320,512]{1,0:T(8,128)S(1)}, u32[]{:S(2)}, u32[]{:S(2)}) collective-permute-start(f32[320,512]{1,0:T(8,128)S(1)} %shard_map.99.refs_2_), channel_id=1, source_target_pairs={{0,1},{1,0},{2,3},{3,2},{4,5},{5,4},{6,7},{7,6},{8,9},{9,8},{10,11... | collective-permute-start | bytes 1966088 | tf_op jit(solution)/shard_map/ppermute | solution.py:454
  124.8 24.6 %collective-permute-start.14 = (bf16[128,3584]{1,0:T(8,128)(2,1)S(1)}, bf16[128,3584]{1,0:T(8,128)(2,1)S(1)}, u32[]{:S(2)}, u32[]{:S(2)}) collective-permute-start(bf16[128,3584]{1,0:T(8,128)(2,1)S(1)} %get-tuple-element.80), channel_id=1, source_target_pairs={{0,2},{2,0},{4,6},{6,4},{8,10},{10,8},{12,14},{14,12},{16,18},{18,... | collective-permute-start | bytes 2752520 | tf_op jit(solution)/shard_map/ppermute | solution.py:347
  126.4 23.0 %collective-permute-start.15 = (bf16[128,3584]{1,0:T(8,128)(2,1)S(1)}, bf16[128,3584]{1,0:T(8,128)(2,1)S(1)}, u32[]{:S(2)}, u32[]{:S(2)}) collective-permute-start(bf16[128,3584]{1,0:T(8,128)(2,1)S(1)} %get-tuple-element.81), channel_id=1, source_target_pairs={{0,4},{2,6},{4,0},{6,2},{8,12},{10,14},{12,8},{14,10},{16,20},{18,... | collective-permute-start | bytes 2752520 | tf_op jit(solution)/shard_map/ppermute | solution.py:347
  134.6 14.9 %collective-permute-start.12 = (bf16[80,3712]{1,0:T(8,128)(2,1)S(1)}, bf16[80,3712]{1,0:T(8,128)(2,1)S(1)}, u32[]{:S(2)}, u32[]{:S(2)}) collective-permute-start(bf16[80,3712]{1,0:T(8,128)(2,1)S(1)} %get-tuple-element.78), channel_id=1, source_target_pairs={{8,0},{10,2},{12,4},{14,6},{16,24},{18,26},{20,28},{22,30},{0,8},{... | collective-permute-start | bytes 1781768 | tf_op jit(solution)/shard_map/ppermute | solution.py:347
  136.2 13.2 %collective-permute-start.13 = (bf16[80,3712]{1,0:T(8,128)(2,1)S(1)}, bf16[80,3712]{1,0:T(8,128)(2,1)S(1)}, u32[]{:S(2)}, u32[]{:S(2)}) collective-permute-start(bf16[80,3712]{1,0:T(8,128)(2,1)S(1)} %get-tuple-element.88), channel_id=1, source_target_pairs={{8,16},{10,18},{12,20},{14,22},{16,8},{18,10},{20,12},{22,14},{9,1... | collective-permute-start | bytes 1781768 | tf_op jit(solution)/shard_map/ppermute | solution.py:347
  149.5 30.4 %collective-permute-start.16 = (bf16[80,3712]{1,0:T(8,128)(2,1)S(1)}, bf16[80,3712]{1,0:T(8,128)(2,1)S(1)}, u32[]{:S(2)}, u32[]{:S(2)}) collective-permute-start(bf16[80,3712]{1,0:T(8,128)(2,1)S(1)} %select_add_fusion), channel_id=1, source_target_pairs={{0,16},{2,18},{4,20},{6,22},{8,24},{10,26},{12,28},{14,30},{16,0},... | collective-permute-start | bytes 1781768 | tf_op jit(solution)/shard_map/ppermute | solution.py:347
  155.4 24.5 %collective-permute-start.17 = (bf16[80,3712]{1,0:T(8,128)(2,1)S(1)}, bf16[80,3712]{1,0:T(8,128)(2,1)S(1)}, u32[]{:S(2)}, u32[]{:S(2)}) collective-permute-start(bf16[80,3712]{1,0:T(8,128)(2,1)S(1)} %get-tuple-element.88), channel_id=1, source_target_pairs={{0,8},{2,10},{4,12},{6,14},{24,16},{26,18},{28,20},{30,22},{1,9},{... | collective-permute-start | bytes 1781768 | tf_op jit(solution)/shard_map/ppermute | solution.py:347
  156.8 23.6 %collective-permute-start.18 = (bf16[64,3584]{1,0:T(8,128)(2,1)S(1)}, bf16[64,3584]{1,0:T(8,128)(2,1)S(1)}, u32[]{:S(2)}, u32[]{:S(2)}) collective-permute-start(bf16[64,3584]{1,0:T(8,128)(2,1)S(1)} %slice_add_fusion.1), channel_id=1, source_target_pairs={{0,2},{2,0},{4,6},{6,4},{8,10},{10,8},{12,14},{14,12},{16,18},{18,... | collective-permute-start | bytes 1376264 | tf_op jit(solution)/shard_map/ppermute | solution.py:347
  157.5 23.0 %collective-permute-start.19 = (bf16[64,3584]{1,0:T(8,128)(2,1)S(1)}, bf16[64,3584]{1,0:T(8,128)(2,1)S(1)}, u32[]{:S(2)}, u32[]{:S(2)}) collective-permute-start(bf16[64,3584]{1,0:T(8,128)(2,1)S(1)} %slice_add_fusion), channel_id=1, source_target_pairs={{0,4},{2,6},{4,0},{6,2},{8,12},{10,14},{12,8},{14,10},{16,20},{18,... | collective-permute-start | bytes 1376264 | tf_op jit(solution)/shard_map/ppermute | solution.py:347
  180.5 1.6 collective-permute-start.20
  180.9 1.2 copy-start.1
  180.9 1.2 copy-start.2
  180.9 1.2 copy-start.3
  180.9 1.2 copy-start.4

commit v7 on v6

--- a/solution.py
+++ b/solution.py
@@ -37,11 +37,10 @@
     return total // 2 // 256 * 256
 
 
-def pack_kernel(gate, up, down, weights, top, low, packed, sems):
+def pack_kernel(gate, up, down, weights, packed, sems):
     ff = gate.shape[2]
     wide = 2 * ff
     part = packed.shape[0] * 2 // 3
-    split = top.shape[0]
     start = pl.multiple_of(lax.axis_index("dp") * part, 128)
     half = pl.ds(start, part)
     pairs = [
@@ -52,7 +51,7 @@
         columns = pl.ds(pl.multiple_of(start + c * wide, 128), wide)
         pairs.append((down.at[0, :, columns], packed.at[part + c * ff : part + (c + 1) * ff, :]))
     reads = len(pairs)
-    pairs += [(packed, weights), (packed.at[:split, :], top), (packed.at[split:, :], low)]
+    pairs.append((packed, weights))
     copies = [
         pltpu.make_async_copy(src, dst, sems.at[i]) for i, (src, dst) in enumerate(pairs)
     ]
@@ -66,7 +65,7 @@
         copy.wait()
 
 
-def arrived_kernel(w1, w2_top, w2_low, mark):
+def arrived_kernel(w1, w2, mark):
     mark[...] = jnp.zeros_like(mark)
 
 
@@ -163,46 +162,85 @@
     whole = pl.BlockSpec((step, wide), lambda i: (i, 0))
     top = pl.BlockSpec((step, wide), lambda i: (jnp.minimum(i, upper - 1), 0))
     low = pl.BlockSpec((step, wide), lambda i: (jnp.maximum(i - upper, 0), 0))
-    return [whole, whole, top, low, top, low]
+    return [whole, whole, whole, top, low]
 
 
 def piece_blocks(pieces, upper):
     here = pl.program_id(0) < upper
-    first, second, top2, low2, top3, low3 = [p[...] for p in pieces]
-    return [first, second, jnp.where(here, top2, low2), jnp.where(here, top3, low3)]
-
-
-def gate_up_kernel(upper, *refs):
-    blocks, pieces, out = refs[:5], refs[5:-1], refs[-1]
-    wide = pieces[0].shape[1]
-
-    @pl.when(pl.program_id(0) == 0)
-    def _():
-        out[...] = jnp.zeros_like(out)
-
-    x = slot_rows(blocks)
-    for q, w in enumerate(piece_blocks(pieces, upper)):
-        out[:, q * wide : (q + 1) * wide] += jnp.dot(x, w, preferred_element_type=f32)
+    *whole, top, low = [p[...] for p in pieces]
+    return whole + [jnp.where(here, top, low)]
+
+
+def fetch_rows(blocks, first, rows, either, sems):
+    own, far, ends, outer, middle = blocks
+    count = either.shape[1]
+    take = slice(first, first + count)
+    targets = [rows.at[i * count : (i + 1) * count, :] for i in range(3)]
+    targets += [either.at[0], either.at[1]]
+    return [
+        pltpu.make_async_copy(src.at[take, :], dst, sems.at[i])
+        for i, (src, dst) in enumerate(zip((own, far, ends, outer, middle), targets))
+    ]
+
+
+def finish_rows(copies, rows, either):
+    for copy in copies:
+        copy.wait()
+    count = either.shape[1]
+    rows[3 * count :, :] = jnp.where(inner_chip(), either[1], either[0])
+
+
+def gate_up_kernel(*refs):
+    blocks, pieces, (out, rows, either, buffer, sems) = refs[:5], refs[5:10], refs[10:]
+    *whole, top, low = pieces
+    part, wide = buffer.shape[1:]
+    split = top.shape[0]
+    loads = fetch_rows(blocks, 0, rows, either, sems)
+    pairs = [(p.at[:part, :], buffer.at[q]) for q, p in enumerate(whole)]
+    pairs.append((top, buffer.at[3, :split, :]))
+    pairs.append((low.at[: part - split, :], buffer.at[3, split:, :]))
+    copies = [
+        pltpu.make_async_copy(src, dst, sems.at[5 + i]) for i, (src, dst) in enumerate(pairs)
+    ]
+    for copy in loads + copies:
+        copy.start()
+    finish_rows(loads, rows, either)
+    for q, needed in enumerate((copies[:1], copies[1:2], copies[2:3], copies[3:])):
+        for copy in needed:
+            copy.wait()
+        out[:, q * wide : (q + 1) * wide] = jnp.dot(
+            rows[...], buffer[q], preferred_element_type=f32
+        )
 
 
 def proj_kernel(*refs):
-    blocks, pieces, out = refs[:5], refs[5:-1], refs[-1]
-    rows, wide = pieces[0].shape
+    blocks, pieces, (out, rows, either, buffer, sems) = refs[:5], refs[5:9], refs[9:]
+    height, wide = buffer.shape[1:]
     ff = wide // 2
-
-    @pl.when(pl.program_id(0) == 0)
-    def _():
-        out[...] = jnp.zeros_like(out)
-
-    c = slot_rows(blocks)
-    w = jnp.concatenate(
-        [
-            jnp.concatenate([p[at : at + ff, :] for at in range(0, rows, ff)], axis=1)
-            for p in pieces
-        ],
-        axis=0,
-    )
-    out[...] += lax.dot_general(c, w, CONTRACT1, preferred_element_type=f32)
+    count = either.shape[1]
+    loads = fetch_rows(blocks, count, rows, either, sems)
+    copies = [
+        pltpu.make_async_copy(p.at[p.shape[0] - height :, :], buffer.at[q], sems.at[5 + q])
+        for q, p in enumerate(pieces)
+    ]
+    for copy in loads + copies:
+        copy.start()
+    finish_rows(loads, rows, either)
+    for q in range(0, QUAD, 2):
+        for copy in copies[q : q + 2]:
+            copy.wait()
+        w = jnp.concatenate(
+            [
+                jnp.concatenate(
+                    [buffer[i, at : at + ff, :] for at in range(0, height, ff)], axis=1
+                )
+                for i in (q, q + 1)
+            ],
+            axis=0,
+        )
+        out[:, q * ff : (q + 2) * ff] = lax.dot_general(
+            rows[...], w, CONTRACT1, preferred_element_type=f32
+        )
 
 
 def activations(mine, theirs, q, ff):
@@ -365,17 +403,17 @@
     split = split_of(packed)
     shape = jax.ShapeDtypeStruct
     hbm = pl.BlockSpec(memory_space=pltpu.HBM)
-    weights, w_top, w_low = call(
+    (weights,) = call(
         pack_kernel,
-        [shape((size, 2 * ff), bf16) for size in (packed, split, packed - split)],
+        [shape((packed, 2 * ff), bf16)],
         [hbm] * 3,
-        [pltpu.VMEM((packed, 2 * ff), bf16), pltpu.SemaphoreType.DMA((5 + part // (2 * ff),))],
+        [pltpu.VMEM((packed, 2 * ff), bf16), pltpu.SemaphoreType.DMA((3 + part // (2 * ff),))],
         0,
         12 * part * ff,
         limit=58,
-        out_specs=[hbm] * 3,
+        out_specs=[hbm],
     )(gate_proj, up_proj, down_proj)
-    weights, w_top, w_low, logits, tokens = barrier((weights, w_top, w_low, logits, tokens))
+    weights, logits, tokens = barrier((weights, logits, tokens))
     mine, other, pick, chosen, inv_w, inv_total = call(
         lambda *refs: prep_kernel(held, capacity, *refs),
         [shape((2, rows_dev, part), bf16)] * 2
@@ -388,8 +426,7 @@
         limit=58,
     )(tokens, cotangent, logits.T, expert_ids.T)
     w1 = send(weights, swap1)
-    w2_top = send(w_top, swap2)
-    w2_low = send(w_low, swap2)
+    w2 = send(weights, swap2)
 
     theirs = lax.ppermute(other, "dp", sibling)
     own = jnp.concatenate(
@@ -409,19 +446,17 @@
     (mark,) = call(
         arrived_kernel,
         [shape((8, 128), f32)],
-        [pl.BlockSpec(memory_space=pl.ANY)] * 3,
+        [pl.BlockSpec(memory_space=pl.ANY)] * 2,
         [],
-        8 * slots * part * QUAD * ff * 8,
+        64 * slots * part * QUAD * ff,
         0,
-    )(w1, w2_top, w2_low)
-    w1, w2_top, w2_low, own, far, outer, mark = barrier(
-        (w1, w2_top, w2_low, own, far, outer, mark)
-    )
-    w3_top = send(w2_top, swap1)
+    )(w1, w2)
+    w1, w2, own, far, outer, mark = barrier((w1, w2, own, far, outer, mark))
+    w3_top = send(w2[:split], swap1)
     w3_low = send(w1[split:], swap2)
     ends = send(jnp.where(inner, far, own), outward + inward)
     middle = send(own, middle_swap)
-    w = [weights, w1, w2_top, w2_low, w3_top, w3_low]
+    w = [weights, w1, w2, w3_top, w3_low]
     blocks = [own, far, ends, outer, middle]
 
     matmul = 2 * slots * part * QUAD * ff
@@ -429,28 +464,28 @@
     upper = split // step
     grid = (part // step,)
     w_specs = piece_specs(step, split, 2 * ff)
+    anywhere = pl.BlockSpec(memory_space=pl.ANY)
+    row_scratch = [
+        pltpu.VMEM((slots, part), bf16),
+        pltpu.VMEM((2, rows_chip, part), bf16),
+    ]
     (g_u,) = call(
-        lambda *refs: gate_up_kernel(upper, *refs),
+        gate_up_kernel,
         [shape((slots, QUAD * 2 * ff), f32)],
-        row_specs(rows_chip, step, 0) + w_specs,
-        [],
+        [anywhere] * 10,
+        row_scratch + [pltpu.VMEM((QUAD, part, 2 * ff), bf16), pltpu.SemaphoreType.DMA((10,))],
         2 * matmul,
         2 * part * (slots + QUAD * 2 * ff),
-        grid=grid,
     )(*blocks, *w)
     g_u_sib = lax.ppermute(g_u, "dp", sibling)
-    half = step // 2
-    in_whole = pl.BlockSpec((half, 2 * ff), lambda i: (part // half + i, 0))
-    in_low = pl.BlockSpec((half, 2 * ff), lambda i: ((part - split) // half + i, 0))
     (proj,) = call(
         proj_kernel,
         [shape((slots, QUAD * ff), f32)],
-        row_specs(rows_chip, step, 1) + [in_whole, in_whole, in_low, in_low],
-        [],
+        [anywhere] * 9,
+        row_scratch + [pltpu.VMEM((QUAD, part // 2, 2 * ff), bf16), pltpu.SemaphoreType.DMA((9,))],
         matmul,
         2 * part * (slots + QUAD * ff),
-        grid=grid,
-    )(*blocks, weights, w1, w2_low, w3_low)
+    )(*blocks, weights, w1, w2, w3_low)
     proj_sib = lax.ppermute(proj, "dp", sibling)
     g0, sent1, sent2, kept1, kept2 = call(
         down_kernel,

time: 186 us -> 179 us (0.962)
  starting transfers between devices: 28.1 us -> 22.2 us
  Pallas kernels: 34.6 us -> 32.2 us
    ppermute x17 -> x16, starting transfers between devices: 27.4 us -> 21.5 us  [send(): return lax.ppermute(array, 'expert', route)]
    pallas_call x3, Pallas kernels: 16 us -> 13.7 us  [the longest x1 6.34 us: per_device(): call(gate_up_kernel, [shape((slots, QUAD * 2 * ff), f32)], [anywhere] * 1...]
    ppermute x2, waiting for transfers between devices: 0.29 us -> 2.35 us  [per_device(): theirs = lax.ppermute(other, 'dp', sibling)]
    ppermute x17 -> x16, waiting for transfers between devices: 118 us -> 117 us  [send(): return lax.ppermute(array, 'expert', route)]
  transfers between devices with their start and end apart: 21 -> 20, of which waited for: 8 -> 12; matrix products, arithmetic and copies ran while one was open for 2% -> 2% of each run, Pallas kernels for 11% -> 11%
where the time goes in v7:
time: 179 us
  waiting for transfers between devices  119 us (66%)
  Pallas kernels  32.2 us (18%)
  starting transfers between devices  22.2 us (12%)
  other arithmetic  2.83 us (2%)
    ppermute x16, waiting for transfers between devices, send(): return lax.ppermute(array, 'expert', route)  117 us
    ppermute x16, starting transfers between devices, send(): return lax.ppermute(array, 'expert', route)  21.5 us
    pallas_call x1, Pallas kernels, per_device(): call(lambda *refs: back_kernel(upper, *refs), [shape((rows_chip, part + 1...  6.55 us
    pallas_call x1, Pallas kernels, per_device(): call(gate_up_kernel, [shape((slots, QUAD * 2 * ff), f32)], [anywhere] * 1...  6.34 us
    pallas_call x1, Pallas kernels, per_device(): call(lambda *refs: prep_kernel(held, capacity, *refs), [shape((2, rows_de...  4.76 us
    pallas_call x1, Pallas kernels, per_device(): call(proj_kernel, [shape((slots, QUAD * ff), f32)], [anywhere] * 9, row_s...  4.05 us
    pallas_call x1, Pallas kernels, per_device(): call(down_kernel, [shape((ff, part), bf16)] * 3 + [shape((lowf, part), bf...  3.69 us
  transfers between devices with their start and end apart: 20, of which 12 were waited for; matrix products, arithmetic and copies ran while one was open for 2% of the time, Pallas kernels for 11%

profile of v7, /device:TPU:0, one launch (start us, length us, event | category | flops | bytes accessed | tf_op | source)
XLA Modules:
  0.0 178.8 jit_solution(3648986887881587845)
XLA Ops:
  0.6 3.3 %shard_map.94.refs_5_.refs_4_ = bf16[5376,256]{1,0:T(8,128)(2,1)} custom-call(bf16[1,7168,128]{2,1,0:T(8,128)(2,1)} %gate.1, bf16[1,7168,128]{2,1,0:T(8,128)(2,1)} %up.1, bf16[1,128,7168]{2,1,0:T(8,128)(2,1)} %down.1), custom_call_target="tpu_custom_call" | custom-call | bytes 5505024 | tf_op jit(solution)/shard_map/pallas_call | solution.py:406
  4.0 3.0 %collective-permute-start = (bf16[5376,256]{1,0:T(8,128)(2,1)}, bf16[5376,256]{1,0:T(8,128)(2,1)S(1)}, u32[]{:S(2)}, u32[]{:S(2)}) collective-permute-start(bf16[5376,256]{1,0:T(8,128)(2,1)} %shard_map.94.refs_5_.refs_4_), channel_id=1, source_target_pairs={{0,2},{2,0},{4,6},{6,4},{8,10},{10,8},{12,14},{14,12},{16,18},{18,... | collective-permute-start | bytes 8257544 | tf_op jit(solution)/shard_map/ppermute | solution.py:385
  7.0 1.5 collective-permute-start.1
  8.5 4.8 %shard_map.95 = (bf16[2,40,3584]{2,1,0:T(8,128)(2,1)}, bf16[2,40,3584]{2,1,0:T(8,128)(2,1)}, bf16[40,128]{1,0:T(8,128)(2,1)}, f32[32,128]{1,0:T(8,128)}, f32[32,128]{1,0:T(8,128)}, /*index=5*/f32[32,128]{1,0:T(8,128)}) custom-call(bf16[128,7168]{1,0:T(8,128)(2,1)} %refs_0_, bf16[128,7168]{1,0:T(8,128)(2,1)} %refs_1_.1, f32[32,128]{1,0:T(8,128)} %bitcast.13, ...), custom_call_target="tpu_custom_call" | custom-call | flops 146800640 | bytes 3670016 | tf_op jit(solution)/shard_map/pallas_call | solution.py:417
  13.3 0.0 collective-permute-start.2
  13.3 2.2 %collective-permute-done.2 = bf16[2,40,3584]{2,1,0:T(8,128)(2,1)S(1)} collective-permute-done((bf16[2,40,3584]{2,1,0:T(8,128)(2,1)}, bf16[2,40,3584]{2,1,0:T(8,128)(2,1)S(1)}, u32[]{:S(2)}, u32[]{:S(2)}) %collective-permute-start.2) | collective-permute-done | bytes 573472 | tf_op jit(solution)/shard_map/ppermute | solution.py:431
  15.5 1.1 select_bitcast_fusion.3
  16.6 0.1 pad_maximum_fusion.refs_0_
  16.7 2.7 %collective-permute-start.3 = (bf16[160,3584]{1,0:T(8,128)(2,1)S(1)}, bf16[160,3584]{1,0:T(8,128)(2,1)S(1)}, u32[]{:S(2)}, u32[]{:S(2)}) collective-permute-start(bf16[160,3584]{1,0:T(8,128)(2,1)S(1)} %pad_maximum_fusion.refs_0_), channel_id=1, source_target_pairs={{0,16},{2,18},{4,20},{6,22},{8,24},{10,26},{12,28},{14,30},{16,0},... | collective-permute-start | bytes 3440648 | tf_op jit(solution)/shard_map/ppermute | solution.py:385
  19.3 1.3 collective-permute-start.4
  20.6 46.2 %collective-permute-done.w1.refs_6_.refs_5_ = bf16[5376,256]{1,0:T(8,128)(2,1)S(1)} collective-permute-done((bf16[5376,256]{1,0:T(8,128)(2,1)}, bf16[5376,256]{1,0:T(8,128)(2,1)S(1)}, u32[]{:S(2)}, u32[]{:S(2)}) %collective-permute-start) | collective-permute-done | bytes 2752544 | tf_op jit(solution)/shard_map/ppermute | solution.py:385
  66.9 1.6 collective-permute-done.1.w2.refs_7_.refs_6_
  68.4 1.2 collective-permute-done.3.refs_1_
  69.6 2.1 %collective-permute-done.4.refs_3_ = bf16[160,3584]{1,0:T(8,128)(2,1)S(1)} collective-permute-done((bf16[160,3584]{1,0:T(8,128)(2,1)S(1)}, bf16[160,3584]{1,0:T(8,128)(2,1)S(1)}, u32[]{:S(2)}, u32[]{:S(2)}) %collective-permute-start.4) | collective-permute-done | bytes 1146912 | tf_op jit(solution)/shard_map/ppermute | solution.py:385
  71.7 1.4 slice.44
  73.1 0.6 collective-permute-start.7
  73.7 0.1 slice.45
  73.8 0.0 copy-start
  73.8 0.5 collective-permute-start.8
  74.3 0.1 broadcast_select_fusion
  74.5 0.1 collective-permute-start.5
  74.5 0.9 collective-permute-start.6
  75.4 24.7 %collective-permute-done.5.refs_2_ = bf16[160,3584]{1,0:T(8,128)(2,1)S(1)} collective-permute-done((bf16[160,3584]{1,0:T(8,128)(2,1)S(1)}, bf16[160,3584]{1,0:T(8,128)(2,1)S(1)}, u32[]{:S(2)}, u32[]{:S(2)}) %collective-permute-start.5) | collective-permute-done | bytes 1146912 | tf_op jit(solution)/shard_map/ppermute | solution.py:385
  100.1 0.0 collective-permute-done.6.refs_4_
  100.1 2.7 %collective-permute-done.7.refs_8_.refs_7_ = bf16[2560,256]{1,0:T(8,128)(2,1)S(1)} collective-permute-done((bf16[2560,256]{1,0:T(8,128)(2,1)S(1)}, bf16[2560,256]{1,0:T(8,128)(2,1)S(1)}, u32[]{:S(2)}, u32[]{:S(2)}) %collective-permute-start.7) | collective-permute-done | bytes 1310752 | tf_op jit(solution)/shard_map/ppermute | solution.py:385
  102.8 3.2 %collective-permute-done.8.refs_9_.refs_8_ = bf16[2816,256]{1,0:T(8,128)(2,1)S(1)} collective-permute-done((bf16[2816,256]{1,0:T(8,128)(2,1)S(1)}, bf16[2816,256]{1,0:T(8,128)(2,1)S(1)}, u32[]{:S(2)}, u32[]{:S(2)}) %collective-permute-start.8) | collective-permute-done | bytes 1441824 | tf_op jit(solution)/shard_map/ppermute | solution.py:385
  106.1 0.0 copy-done
  106.1 6.3 %shard_map.97.mine.refs_0_ = f32[320,1024]{1,0:T(8,128)S(1)} custom-call(bf16[160,3584]{1,0:T(8,128)(2,1)S(1)} %pad_maximum_fusion.refs_0_, bf16[160,3584]{1,0:T(8,128)(2,1)S(1)} %collective-permute-done.3.refs_1_, bf16[160,3584]{1,0:T(8,128)(2,1)S(1)} %collective-permute-done.5.refs_2_, bf16[160,3584]{1,0:T(8,128)(2,1)S(1)} %collective-permute-done.4.refs_3_, ...), custom_call_target="tpu_custom_call" | custom-call | flops 2348810240 | bytes 9633792 | tf_op jit(solution)/shard_map/pallas_call | solution.py:472
  112.4 0.1 collective-permute-start.9
  112.5 4.0 %shard_map.99.refs_2_ = f32[320,512]{1,0:T(8,128)S(1)} custom-call(bf16[160,3584]{1,0:T(8,128)(2,1)S(1)} %pad_maximum_fusion.refs_0_, bf16[160,3584]{1,0:T(8,128)(2,1)S(1)} %collective-permute-done.3.refs_1_, bf16[160,3584]{1,0:T(8,128)(2,1)S(1)} %collective-permute-done.5.refs_2_, bf16[160,3584]{1,0:T(8,128)(2,1)S(1)} %collective-permute-done.4.refs_3_, ...), custom_call_target="tpu_custom_call" | custom-call | flops 1174405120 | bytes 5963776 | tf_op jit(solution)/shard_map/pallas_call | solution.py:481
  116.6 0.6 collective-permute-start.10
  117.1 0.0 collective-permute-done.9.theirs.refs_1_
  117.1 3.7 %shard_map.98 = (bf16[128,3584]{1,0:T(8,128)(2,1)S(1)}, bf16[128,3584]{1,0:T(8,128)(2,1)S(1)}, bf16[128,3584]{1,0:T(8,128)(2,1)S(1)}, bf16[64,3584]{1,0:T(8,128)(2,1)S(1)}, bf16[64,3584]{1,0:T(8,128)(2,1)S(1)}) custom-call(f32[320,1024]{1,0:T(8,128)S(1)} %shard_map.97.mine.refs_0_, f32[320,1024]{1,0:T(8,128)S(1)} %collective-permute-done.9.theirs.refs_1_, ...), custom_call_target="tpu_custom_call" | custom-call | flops 1174405120 | bytes 5963776 | tf_op jit(solution)/shard_map/pallas_call | solution.py:490
  120.8 0.0 collective-permute-done.10.refs_3_
  120.8 1.5 collective-permute-start.13
  122.4 0.5 collective-permute-start.14
  122.9 6.5 %shard_map.100 = (bf16[80,3712]{1,0:T(8,128)(2,1)S(1)}, bf16[80,3712]{1,0:T(8,128)(2,1)S(1)}, bf16[80,3712]{1,0:T(8,128)(2,1)S(1)}, bf16[80,3712]{1,0:T(8,128)(2,1)S(1)}) custom-call(f32[320,1024]{1,0:T(8,128)S(1)} %shard_map.97.mine.refs_0_, f32[320,1024]{1,0:T(8,128)S(1)} %collective-permute-done.9.theirs.refs_1_, f32[320,512]{1,0:T(8,128)S(1)} %shard_map.99.refs_2_, ...), custom_call_target="tpu_custom_call" | custom-call | flops 2348810240 | bytes 9633792 | tf_op jit(solution)/shard_map/pallas_call | solution.py:502
  129.4 0.1 collective-permute-start.11
  129.5 0.7 collective-permute-start.12
  130.2 14.1 %collective-permute-done.11.ends = bf16[80,3712]{1,0:T(8,128)(2,1)S(1)} collective-permute-done((bf16[80,3712]{1,0:T(8,128)(2,1)S(1)}, bf16[80,3712]{1,0:T(8,128)(2,1)S(1)}, u32[]{:S(2)}, u32[]{:S(2)}) %collective-permute-start.11) | collective-permute-done | bytes 593952 | tf_op jit(solution)/shard_map/ppermute | solution.py:385
  144.3 0.0 collective-permute-done.12.middle
  144.3 0.0 collective-permute-done.13
  144.3 0.1 collective-permute-done.14
  144.4 0.1 select_add_fusion
  144.5 4.7 %collective-permute-start.15 = (bf16[80,3712]{1,0:T(8,128)(2,1)S(1)}, bf16[80,3712]{1,0:T(8,128)(2,1)S(1)}, u32[]{:S(2)}, u32[]{:S(2)}) collective-permute-start(bf16[80,3712]{1,0:T(8,128)(2,1)S(1)} %select_add_fusion), channel_id=1, source_target_pairs={{0,16},{2,18},{4,20},{6,22},{8,24},{10,26},{12,28},{14,30},{16,0},... | collective-permute-start | bytes 1781768 | tf_op jit(solution)/shard_map/ppermute | solution.py:385
  149.2 1.3 collective-permute-start.16
  150.5 0.1 slice_add_fusion.1
  150.6 0.6 collective-permute-start.17
  151.3 1.5 collective-permute-start.18
  152.8 20.9 %collective-permute-done.15.far = bf16[80,3712]{1,0:T(8,128)(2,1)S(1)} collective-permute-done((bf16[80,3712]{1,0:T(8,128)(2,1)S(1)}, bf16[80,3712]{1,0:T(8,128)(2,1)S(1)}, u32[]{:S(2)}, u32[]{:S(2)}) %collective-permute-start.15) | collective-permute-done | bytes 593952 | tf_op jit(solution)/shard_map/ppermute | solution.py:385
  173.6 0.0 collective-permute-done.16.outer
  173.6 0.5 shard_map.101
  174.1 0.0 collective-permute-done.17
  174.1 0.0 collective-permute-done.18
  174.1 0.1 collective-permute-start.19
  174.2 0.3 add_convert_fusion.1
  174.6 0.0 copy-start.1
  174.6 0.0 copy-start.2
  174.6 0.0 copy-start.3
  174.6 0.0 copy-start.4
  174.6 1.0 maximum_bitcast_fusion
  175.6 0.2 collective-permute-done.19.refs_2_
  175.8 0.0 copy-done.2
  175.8 3.0 %shard_map.102 = (bf16[128,7168]{1,0:T(8,128)(2,1)}, f32[32,128]{1,0:T(8,128)}) custom-call(bf16[40,128]{1,0:T(8,128)(2,1)S(1)} %copy-done.4, bf16[40,3584]{1,0:T(8,128)(2,1)S(1)} %get-tuple-element.78.refs_1_, bf16[40,3584]{1,0:T(8,128)(2,1)S(1)} %collective-permute-done.19.refs_2_, f32[40,128]{1,0:T(8,128)S(1)} %get-tuple-element.85.refs_3_, ...), custom_call_target="tpu_custom_call" | custom-call | flops 73400320 | bytes 2408448 | tf_op jit(solution)/shard_map/pallas_call | solution.py:547
  (5 shorter events, 0.1 us)
Async XLA Ops:
  4.0 62.9 %collective-permute-start = (bf16[5376,256]{1,0:T(8,128)(2,1)}, bf16[5376,256]{1,0:T(8,128)(2,1)S(1)}, u32[]{:S(2)}, u32[]{:S(2)}) collective-permute-start(bf16[5376,256]{1,0:T(8,128)(2,1)} %shard_map.94.refs_5_.refs_4_), channel_id=1, source_target_pairs={{0,2},{2,0},{4,6},{6,4},{8,10},{10,8},{12,14},{14,12},{16,18},{18,... | collective-permute-start | bytes 8257544 | tf_op jit(solution)/shard_map/ppermute | solution.py:385
  7.0 61.4 %collective-permute-start.1 = (bf16[5376,256]{1,0:T(8,128)(2,1)}, bf16[5376,256]{1,0:T(8,128)(2,1)}, u32[]{:S(2)}, u32[]{:S(2)}) collective-permute-start(bf16[5376,256]{1,0:T(8,128)(2,1)} %shard_map.94.refs_5_.refs_4_), channel_id=1, source_target_pairs={{0,4},{2,6},{4,0},{6,2},{8,12},{10,14},{12,8},{14,10},{16,20},{18,... | collective-permute-start | bytes 8257544 | tf_op jit(solution)/shard_map/ppermute | solution.py:385
  13.3 2.2 %collective-permute-start.2 = (bf16[2,40,3584]{2,1,0:T(8,128)(2,1)}, bf16[2,40,3584]{2,1,0:T(8,128)(2,1)S(1)}, u32[]{:S(2)}, u32[]{:S(2)}) collective-permute-start(bf16[2,40,3584]{2,1,0:T(8,128)(2,1)} %get-tuple-element.54), channel_id=1, source_target_pairs={{0,1},{1,0},{2,3},{3,2},{4,5},{5,4},{6,7},{7,6},{8,9},{9,8},{10,11... | collective-permute-start | bytes 1720328 | tf_op jit(solution)/shard_map/ppermute | solution.py:431
  16.7 53.0 %collective-permute-start.3 = (bf16[160,3584]{1,0:T(8,128)(2,1)S(1)}, bf16[160,3584]{1,0:T(8,128)(2,1)S(1)}, u32[]{:S(2)}, u32[]{:S(2)}) collective-permute-start(bf16[160,3584]{1,0:T(8,128)(2,1)S(1)} %pad_maximum_fusion.refs_0_), channel_id=1, source_target_pairs={{0,16},{2,18},{4,20},{6,22},{8,24},{10,26},{12,28},{14,30},{16,0},... | collective-permute-start | bytes 3440648 | tf_op jit(solution)/shard_map/ppermute | solution.py:385
  19.3 52.4 %collective-permute-start.4 = (bf16[160,3584]{1,0:T(8,128)(2,1)S(1)}, bf16[160,3584]{1,0:T(8,128)(2,1)S(1)}, u32[]{:S(2)}, u32[]{:S(2)}) collective-permute-start(bf16[160,3584]{1,0:T(8,128)(2,1)S(1)} %pad_maximum_fusion.refs_0_), channel_id=1, source_target_pairs={{8,0},{10,2},{12,4},{14,6},{16,24},{18,26},{20,28},{22,30},{9,1},{... | collective-permute-start | bytes 3440648 | tf_op jit(solution)/shard_map/ppermute | solution.py:385
  73.1 29.7 %collective-permute-start.7 = (bf16[2560,256]{1,0:T(8,128)(2,1)S(1)}, bf16[2560,256]{1,0:T(8,128)(2,1)S(1)}, u32[]{:S(2)}, u32[]{:S(2)}) collective-permute-start(bf16[2560,256]{1,0:T(8,128)(2,1)S(1)} %slice.44), channel_id=1, source_target_pairs={{0,2},{2,0},{4,6},{6,4},{8,10},{10,8},{12,14},{14,12},{16,18},{18,... | collective-permute-start | bytes 3932168 | tf_op jit(solution)/shard_map/ppermute | solution.py:385
  73.8 32.3 %copy-start = (bf16[5376,256]{1,0:T(8,128)(2,1)S(1)}, bf16[5376,256]{1,0:T(8,128)(2,1)}, u32[]{:S(2)}) copy-start(bf16[5376,256]{1,0:T(8,128)(2,1)} %shard_map.94.refs_5_.refs_4_) | copy-start | bytes 8257540
  73.8 32.3 %collective-permute-start.8 = (bf16[2816,256]{1,0:T(8,128)(2,1)S(1)}, bf16[2816,256]{1,0:T(8,128)(2,1)S(1)}, u32[]{:S(2)}, u32[]{:S(2)}) collective-permute-start(bf16[2816,256]{1,0:T(8,128)(2,1)S(1)} %slice.45), channel_id=1, source_target_pairs={{0,4},{2,6},{4,0},{6,2},{8,12},{10,14},{12,8},{14,10},{16,20},{18,... | collective-permute-start | bytes 4325384 | tf_op jit(solution)/shard_map/ppermute | solution.py:385
  74.5 25.7 %collective-permute-start.5 = (bf16[160,3584]{1,0:T(8,128)(2,1)S(1)}, bf16[160,3584]{1,0:T(8,128)(2,1)S(1)}, u32[]{:S(2)}, u32[]{:S(2)}) collective-permute-start(bf16[160,3584]{1,0:T(8,128)(2,1)S(1)} %broadcast_select_fusion), channel_id=1, source_target_pairs={{8,0},{10,2},{12,4},{14,6},{16,24},{18,26},{20,28},{22,30},{0,8},{... | collective-permute-start | bytes 3440648 | tf_op jit(solution)/shard_map/ppermute | solution.py:385
  74.5 25.6 %collective-permute-start.6 = (bf16[160,3584]{1,0:T(8,128)(2,1)S(1)}, bf16[160,3584]{1,0:T(8,128)(2,1)S(1)}, u32[]{:S(2)}, u32[]{:S(2)}) collective-permute-start(bf16[160,3584]{1,0:T(8,128)(2,1)S(1)} %pad_maximum_fusion.refs_0_), channel_id=1, source_target_pairs={{8,16},{10,18},{12,20},{14,22},{16,8},{18,10},{20,12},{22,14},{9,1... | collective-permute-start | bytes 3440648 | tf_op jit(solution)/shard_map/ppermute | solution.py:385
  112.4 4.7 %collective-permute-start.9 = (f32[320,1024]{1,0:T(8,128)S(1)}, f32[320,1024]{1,0:T(8,128)S(1)}, u32[]{:S(2)}, u32[]{:S(2)}) collective-permute-start(f32[320,1024]{1,0:T(8,128)S(1)} %shard_map.97.mine.refs_0_), channel_id=1, source_target_pairs={{0,1},{1,0},{2,3},{3,2},{4,5},{5,4},{6,7},{7,6},{8,9},{9,8},{10,11... | collective-permute-start | bytes 3932168 | tf_op jit(solution)/shard_map/ppermute | solution.py:480
  116.6 4.3 %collective-permute-start.10 = (f32[320,512]{1,0:T(8,128)S(1)}, f32[320,512]{1,0:T(8,128)S(1)}, u32[]{:S(2)}, u32[]{:S(2)}) collective-permute-start(f32[320,512]{1,0:T(8,128)S(1)} %shard_map.99.refs_2_), channel_id=1, source_target_pairs={{0,1},{1,0},{2,3},{3,2},{4,5},{5,4},{6,7},{7,6},{8,9},{9,8},{10,11... | collective-permute-start | bytes 1966088 | tf_op jit(solution)/shard_map/ppermute | solution.py:489
  120.8 23.5 %collective-permute-start.13 = (bf16[128,3584]{1,0:T(8,128)(2,1)S(1)}, bf16[128,3584]{1,0:T(8,128)(2,1)S(1)}, u32[]{:S(2)}, u32[]{:S(2)}) collective-permute-start(bf16[128,3584]{1,0:T(8,128)(2,1)S(1)} %get-tuple-element.68), channel_id=1, source_target_pairs={{0,2},{2,0},{4,6},{6,4},{8,10},{10,8},{12,14},{14,12},{16,18},{18,... | collective-permute-start | bytes 2752520 | tf_op jit(solution)/shard_map/ppermute | solution.py:385
  122.4 22.0 %collective-permute-start.14 = (bf16[128,3584]{1,0:T(8,128)(2,1)S(1)}, bf16[128,3584]{1,0:T(8,128)(2,1)S(1)}, u32[]{:S(2)}, u32[]{:S(2)}) collective-permute-start(bf16[128,3584]{1,0:T(8,128)(2,1)S(1)} %get-tuple-element.69), channel_id=1, source_target_pairs={{0,4},{2,6},{4,0},{6,2},{8,12},{10,14},{12,8},{14,10},{16,20},{18,... | collective-permute-start | bytes 2752520 | tf_op jit(solution)/shard_map/ppermute | solution.py:385
  129.4 14.9 %collective-permute-start.11 = (bf16[80,3712]{1,0:T(8,128)(2,1)S(1)}, bf16[80,3712]{1,0:T(8,128)(2,1)S(1)}, u32[]{:S(2)}, u32[]{:S(2)}) collective-permute-start(bf16[80,3712]{1,0:T(8,128)(2,1)S(1)} %get-tuple-element.66), channel_id=1, source_target_pairs={{8,0},{10,2},{12,4},{14,6},{16,24},{18,26},{20,28},{22,30},{0,8},{... | collective-permute-start | bytes 1781768 | tf_op jit(solution)/shard_map/ppermute | solution.py:385
  129.5 14.8 %collective-permute-start.12 = (bf16[80,3712]{1,0:T(8,128)(2,1)S(1)}, bf16[80,3712]{1,0:T(8,128)(2,1)S(1)}, u32[]{:S(2)}, u32[]{:S(2)}) collective-permute-start(bf16[80,3712]{1,0:T(8,128)(2,1)S(1)} %get-tuple-element.76), channel_id=1, source_target_pairs={{8,16},{10,18},{12,20},{14,22},{16,8},{18,10},{20,12},{22,14},{9,1... | collective-permute-start | bytes 1781768 | tf_op jit(solution)/shard_map/ppermute | solution.py:385
  144.5 29.2 %collective-permute-start.15 = (bf16[80,3712]{1,0:T(8,128)(2,1)S(1)}, bf16[80,3712]{1,0:T(8,128)(2,1)S(1)}, u32[]{:S(2)}, u32[]{:S(2)}) collective-permute-start(bf16[80,3712]{1,0:T(8,128)(2,1)S(1)} %select_add_fusion), channel_id=1, source_target_pairs={{0,16},{2,18},{4,20},{6,22},{8,24},{10,26},{12,28},{14,30},{16,0},... | collective-permute-start | bytes 1781768 | tf_op jit(solution)/shard_map/ppermute | solution.py:385
  149.2 24.4 %collective-permute-start.16 = (bf16[80,3712]{1,0:T(8,128)(2,1)S(1)}, bf16[80,3712]{1,0:T(8,128)(2,1)S(1)}, u32[]{:S(2)}, u32[]{:S(2)}) collective-permute-start(bf16[80,3712]{1,0:T(8,128)(2,1)S(1)} %get-tuple-element.76), channel_id=1, source_target_pairs={{0,8},{2,10},{4,12},{6,14},{24,16},{26,18},{28,20},{30,22},{1,9},{... | collective-permute-start | bytes 1781768 | tf_op jit(solution)/shard_map/ppermute | solution.py:385
  150.6 23.5 %collective-permute-start.17 = (bf16[64,3584]{1,0:T(8,128)(2,1)S(1)}, bf16[64,3584]{1,0:T(8,128)(2,1)S(1)}, u32[]{:S(2)}, u32[]{:S(2)}) collective-permute-start(bf16[64,3584]{1,0:T(8,128)(2,1)S(1)} %slice_add_fusion.1), channel_id=1, source_target_pairs={{0,2},{2,0},{4,6},{6,4},{8,10},{10,8},{12,14},{14,12},{16,18},{18,... | collective-permute-start | bytes 1376264 | tf_op jit(solution)/shard_map/ppermute | solution.py:385
  151.3 22.9 %collective-permute-start.18 = (bf16[64,3584]{1,0:T(8,128)(2,1)S(1)}, bf16[64,3584]{1,0:T(8,128)(2,1)S(1)}, u32[]{:S(2)}, u32[]{:S(2)}) collective-permute-start(bf16[64,3584]{1,0:T(8,128)(2,1)S(1)} %slice_add_fusion), channel_id=1, source_target_pairs={{0,4},{2,6},{4,0},{6,2},{8,12},{10,14},{12,8},{14,10},{16,20},{18,... | collective-permute-start | bytes 1376264 | tf_op jit(solution)/shard_map/ppermute | solution.py:385
  174.1 1.6 collective-permute-start.19
  174.6 1.2 copy-start.1
  174.6 1.2 copy-start.2
  174.6 1.2 copy-start.3
  174.6 1.2 copy-start.4

commit v8 on v7

--- a/solution.py
+++ b/solution.py
@@ -191,26 +191,23 @@
 
 
 def gate_up_kernel(*refs):
-    blocks, pieces, (out, rows, either, buffer, sems) = refs[:5], refs[5:10], refs[10:]
+    blocks, pieces, (out, rows) = refs[:5], refs[5:10], refs[10:]
+    own, far, ends, outer, middle = blocks
     *whole, top, low = pieces
-    part, wide = buffer.shape[1:]
+    wide = top.shape[1]
     split = top.shape[0]
-    loads = fetch_rows(blocks, 0, rows, either, sems)
-    pairs = [(p.at[:part, :], buffer.at[q]) for q, p in enumerate(whole)]
-    pairs.append((top, buffer.at[3, :split, :]))
-    pairs.append((low.at[: part - split, :], buffer.at[3, split:, :]))
-    copies = [
-        pltpu.make_async_copy(src, dst, sems.at[5 + i]) for i, (src, dst) in enumerate(pairs)
-    ]
-    for copy in loads + copies:
-        copy.start()
-    finish_rows(loads, rows, either)
-    for q, needed in enumerate((copies[:1], copies[1:2], copies[2:3], copies[3:])):
-        for copy in needed:
-            copy.wait()
+    part = rows.shape[1]
+    count = rows.shape[0] // (SPLIT // QUAD)
+    for i, block in enumerate((own, far, ends)):
+        rows[i * count : (i + 1) * count, :] = block[:count, :]
+    rows[3 * count :, :] = jnp.where(inner_chip(), middle[:count, :], outer[:count, :])
+    for q, w in enumerate(whole):
         out[:, q * wide : (q + 1) * wide] = jnp.dot(
-            rows[...], buffer[q], preferred_element_type=f32
+            rows[...], w[:part, :], preferred_element_type=f32
         )
+    out[:, 3 * wide :] = jnp.dot(
+        rows[:, :split], top[...], preferred_element_type=f32
+    ) + jnp.dot(rows[:, split:], low[: part - split, :], preferred_element_type=f32)
 
 
 def proj_kernel(*refs):
@@ -423,7 +420,7 @@
         [],
         4 * rows_dev * tok_count * width,
         4 * tok_count * width,
-        limit=58,
+        limit=16,
     )(tokens, cotangent, logits.T, expert_ids.T)
     w1 = send(weights, swap1)
     w2 = send(weights, swap2)
@@ -472,8 +469,8 @@
     (g_u,) = call(
         gate_up_kernel,
         [shape((slots, QUAD * 2 * ff), f32)],
-        [anywhere] * 10,
-        row_scratch + [pltpu.VMEM((QUAD, part, 2 * ff), bf16), pltpu.SemaphoreType.DMA((10,))],
+        [VMEM] * 10,
+        row_scratch[:1],
         2 * matmul,
         2 * part * (slots + QUAD * 2 * ff),
     )(*blocks, *w)

time: 179 us -> 177 us (0.989)
  Pallas kernels: 32.2 us -> 28.1 us
    pallas_call x1, Pallas kernels: 4.76 us -> 2.55 us  [per_device(): call(lambda *refs: prep_kernel(held, capacity, *refs), [shape((2, rows_de...]
    pallas_call x1, Pallas kernels: 6.34 us -> 4.3 us  [per_device(): call(gate_up_kernel, [shape((slots, QUAD * 2 * ff), f32)], [VMEM] * 10, r...]
  transfers between devices with their start and end apart: 20 -> 20, of which waited for: 12 -> 12; matrix products, arithmetic and copies ran while one was open for 2% -> 2% of each run, Pallas kernels for 11% -> 10%
where the time goes in v8:
time: 177 us; the launch traced here: 176 us
  waiting for transfers between devices  119 us (67%)
  Pallas kernels  28.1 us (16%)
  starting transfers between devices  22.2 us (13%)
  local copies, waits for them, and re-layouts  3.01 us (2%)
  other arithmetic  2.83 us (2%)
    ppermute x16, waiting for transfers between devices, send(): return lax.ppermute(array, 'expert', route)  117 us
    ppermute x16, starting transfers between devices, send(): return lax.ppermute(array, 'expert', route)  21.5 us
    pallas_call x1, Pallas kernels, per_device(): call(lambda *refs: back_kernel(upper, *refs), [shape((rows_chip, part + 1...  6.54 us
    pallas_call x1, Pallas kernels, per_device(): call(gate_up_kernel, [shape((slots, QUAD * 2 * ff), f32)], [VMEM] * 10, r...  4.3 us
    pallas_call x1, Pallas kernels, per_device(): call(proj_kernel, [shape((slots, QUAD * ff), f32)], [anywhere] * 9, row_s...  4.05 us
    pallas_call x1, Pallas kernels, per_device(): call(down_kernel, [shape((ff, part), bf16)] * 3 + [shape((lowf, part), bf...  3.68 us
  transfers between devices with their start and end apart: 20, of which 12 were waited for; matrix products, arithmetic and copies ran while one was open for 2% of the time, Pallas kernels for 10%

profile of v8, /device:TPU:0, one launch (start us, length us, event | category | flops | bytes accessed | tf_op | source)
XLA Modules:
  0.0 176.3 jit_solution(11661191449518061461)
XLA Ops:
  0.6 0.0 copy-start.3
  0.6 0.0 copy-start.1
  0.7 0.0 copy-start.4
  0.7 3.5 %shard_map.94.refs_5_.refs_4_ = bf16[5376,256]{1,0:T(8,128)(2,1)} custom-call(bf16[1,7168,128]{2,1,0:T(8,128)(2,1)} %gate.1, bf16[1,7168,128]{2,1,0:T(8,128)(2,1)} %up.1, bf16[1,128,7168]{2,1,0:T(8,128)(2,1)} %down.1), custom_call_target="tpu_custom_call" | custom-call | bytes 5505024 | tf_op jit(solution)/shard_map/pallas_call | solution.py:403
  4.1 3.0 %collective-permute-start = (bf16[5376,256]{1,0:T(8,128)(2,1)}, bf16[5376,256]{1,0:T(8,128)(2,1)S(1)}, u32[]{:S(2)}, u32[]{:S(2)}) collective-permute-start(bf16[5376,256]{1,0:T(8,128)(2,1)} %shard_map.94.refs_5_.refs_4_), channel_id=1, source_target_pairs={{0,2},{2,0},{4,6},{6,4},{8,10},{10,8},{12,14},{14,12},{16,18},{18,... | collective-permute-start | bytes 8257544 | tf_op jit(solution)/shard_map/ppermute | solution.py:382
  7.1 1.5 collective-permute-start.1
  8.7 0.0 copy-done.3
  8.7 0.0 copy-done.1
  8.7 0.0 copy-done.4
  8.7 1.5 copy-done.2
  10.2 2.5 %shard_map.95 = (bf16[2,40,3584]{2,1,0:T(8,128)(2,1)S(1)}, bf16[2,40,3584]{2,1,0:T(8,128)(2,1)}, bf16[40,128]{1,0:T(8,128)(2,1)S(1)}, f32[32,128]{1,0:T(8,128)S(...) custom-call(bf16[128,7168]{1,0:T(8,128)(2,1)S(1)} %copy-done.1, bf16[128,7168]{1,0:T(8,128)(2,1)S(1)} %copy-done.2, ...), custom_call_target="tpu_custom_call" | custom-call | flops 146800640 | bytes 3670016 | tf_op jit(solution)/shard_map/pallas_call | solution.py:414
  12.7 0.0 collective-permute-start.2
  12.7 2.3 %collective-permute-done.2 = bf16[2,40,3584]{2,1,0:T(8,128)(2,1)} collective-permute-done((bf16[2,40,3584]{2,1,0:T(8,128)(2,1)}, bf16[2,40,3584]{2,1,0:T(8,128)(2,1)}, u32[]{:S(2)}, u32[]{:S(2)}) %collective-permute-start.2) | collective-permute-done | bytes 573472 | tf_op jit(solution)/shard_map/ppermute | solution.py:428
  15.1 1.1 select_bitcast_fusion.3
  16.2 0.1 pad_maximum_fusion.refs_0_
  16.3 2.7 %collective-permute-start.3 = (bf16[160,3584]{1,0:T(8,128)(2,1)S(1)}, bf16[160,3584]{1,0:T(8,128)(2,1)S(1)}, u32[]{:S(2)}, u32[]{:S(2)}) collective-permute-start(bf16[160,3584]{1,0:T(8,128)(2,1)S(1)} %pad_maximum_fusion.refs_0_), channel_id=1, source_target_pairs={{0,16},{2,18},{4,20},{6,22},{8,24},{10,26},{12,28},{14,30},{16,0},... | collective-permute-start | bytes 3440648 | tf_op jit(solution)/shard_map/ppermute | solution.py:382
  18.9 1.3 collective-permute-start.4
  20.2 46.8 %collective-permute-done.w1.refs_6_.refs_5_ = bf16[5376,256]{1,0:T(8,128)(2,1)S(1)} collective-permute-done((bf16[5376,256]{1,0:T(8,128)(2,1)}, bf16[5376,256]{1,0:T(8,128)(2,1)S(1)}, u32[]{:S(2)}, u32[]{:S(2)}) %collective-permute-start) | collective-permute-done | bytes 2752544 | tf_op jit(solution)/shard_map/ppermute | solution.py:382
  67.0 1.6 collective-permute-done.1.w2.refs_7_.refs_6_
  68.6 0.6 collective-permute-done.3.refs_1_
  69.2 2.1 %collective-permute-done.4.refs_3_ = bf16[160,3584]{1,0:T(8,128)(2,1)S(1)} collective-permute-done((bf16[160,3584]{1,0:T(8,128)(2,1)S(1)}, bf16[160,3584]{1,0:T(8,128)(2,1)S(1)}, u32[]{:S(2)}, u32[]{:S(2)}) %collective-permute-start.4) | collective-permute-done | bytes 1146912 | tf_op jit(solution)/shard_map/ppermute | solution.py:382
  71.3 1.4 slice.44
  72.7 0.6 collective-permute-start.7
  73.3 0.1 slice.45
  73.4 0.5 collective-permute-start.8
  73.9 0.1 broadcast_select_fusion
  74.0 0.1 collective-permute-start.5
  74.1 0.9 collective-permute-start.6
  75.0 24.7 %collective-permute-done.5.refs_2_ = bf16[160,3584]{1,0:T(8,128)(2,1)S(1)} collective-permute-done((bf16[160,3584]{1,0:T(8,128)(2,1)S(1)}, bf16[160,3584]{1,0:T(8,128)(2,1)S(1)}, u32[]{:S(2)}, u32[]{:S(2)}) %collective-permute-start.5) | collective-permute-done | bytes 1146912 | tf_op jit(solution)/shard_map/ppermute | solution.py:382
  99.7 0.0 collective-permute-done.6.refs_4_
  99.7 2.7 %collective-permute-done.7.refs_8_.refs_7_ = bf16[2560,256]{1,0:T(8,128)(2,1)S(1)} collective-permute-done((bf16[2560,256]{1,0:T(8,128)(2,1)S(1)}, bf16[2560,256]{1,0:T(8,128)(2,1)S(1)}, u32[]{:S(2)}, u32[]{:S(2)}) %collective-permute-start.7) | collective-permute-done | bytes 1310752 | tf_op jit(solution)/shard_map/ppermute | solution.py:382
  102.4 3.2 %collective-permute-done.8.refs_9_.refs_8_ = bf16[2816,256]{1,0:T(8,128)(2,1)S(1)} collective-permute-done((bf16[2816,256]{1,0:T(8,128)(2,1)S(1)}, bf16[2816,256]{1,0:T(8,128)(2,1)S(1)}, u32[]{:S(2)}, u32[]{:S(2)}) %collective-permute-start.8) | collective-permute-done | bytes 1441824 | tf_op jit(solution)/shard_map/ppermute | solution.py:382
  105.7 4.3 %shard_map.97.mine.refs_0_ = f32[320,1024]{1,0:T(8,128)S(1)} custom-call(bf16[160,3584]{1,0:T(8,128)(2,1)S(1)} %pad_maximum_fusion.refs_0_, bf16[160,3584]{1,0:T(8,128)(2,1)S(1)} %collective-permute-done.3.refs_1_, bf16[160,3584]{1,0:T(8,128)(2,1)S(1)} %collective-permute-done.5.refs_2_, bf16[160,3584]{1,0:T(8,128)(2,1)S(1)} %collective-permute-done.4.refs_3_, ...), custom_call_target="tpu_custom_call" | custom-call | flops 2348810240 | bytes 9633792 | tf_op jit(solution)/shard_map/pallas_call | solution.py:469
  110.0 0.1 collective-permute-start.9
  110.1 4.0 %shard_map.99.refs_2_ = f32[320,512]{1,0:T(8,128)S(1)} custom-call(bf16[160,3584]{1,0:T(8,128)(2,1)S(1)} %pad_maximum_fusion.refs_0_, bf16[160,3584]{1,0:T(8,128)(2,1)S(1)} %collective-permute-done.3.refs_1_, bf16[160,3584]{1,0:T(8,128)(2,1)S(1)} %collective-permute-done.5.refs_2_, bf16[160,3584]{1,0:T(8,128)(2,1)S(1)} %collective-permute-done.4.refs_3_, ...), custom_call_target="tpu_custom_call" | custom-call | flops 1174405120 | bytes 5963776 | tf_op jit(solution)/shard_map/pallas_call | solution.py:478
  114.1 0.6 collective-permute-start.10
  114.7 0.0 collective-permute-done.9.theirs.refs_1_
  114.7 3.7 %shard_map.98 = (bf16[128,3584]{1,0:T(8,128)(2,1)S(1)}, bf16[128,3584]{1,0:T(8,128)(2,1)S(1)}, bf16[128,3584]{1,0:T(8,128)(2,1)S(1)}, bf16[64,3584]{1,0:T(8,128)(2,1)S(1)}, bf16[64,3584]{1,0:T(8,128)(2,1)S(1)}) custom-call(f32[320,1024]{1,0:T(8,128)S(1)} %shard_map.97.mine.refs_0_, f32[320,1024]{1,0:T(8,128)S(1)} %collective-permute-done.9.theirs.refs_1_, ...), custom_call_target="tpu_custom_call" | custom-call | flops 1174405120 | bytes 5963776 | tf_op jit(solution)/shard_map/pallas_call | solution.py:487
  118.4 0.0 collective-permute-done.10.refs_3_
  118.4 1.6 collective-permute-start.13
  119.9 0.5 collective-permute-start.14
  120.4 6.5 %shard_map.100 = (bf16[80,3712]{1,0:T(8,128)(2,1)S(1)}, bf16[80,3712]{1,0:T(8,128)(2,1)S(1)}, bf16[80,3712]{1,0:T(8,128)(2,1)S(1)}, bf16[80,3712]{1,0:T(8,128)(2,1)S(1)}) custom-call(f32[320,1024]{1,0:T(8,128)S(1)} %shard_map.97.mine.refs_0_, f32[320,1024]{1,0:T(8,128)S(1)} %collective-permute-done.9.theirs.refs_1_, f32[320,512]{1,0:T(8,128)S(1)} %shard_map.99.refs_2_, ...), custom_call_target="tpu_custom_call" | custom-call | flops 2348810240 | bytes 9633792 | tf_op jit(solution)/shard_map/pallas_call | solution.py:499
  127.0 0.1 collective-permute-start.11
  127.1 0.7 collective-permute-start.12
  127.8 14.1 %collective-permute-done.11.ends = bf16[80,3712]{1,0:T(8,128)(2,1)S(1)} collective-permute-done((bf16[80,3712]{1,0:T(8,128)(2,1)S(1)}, bf16[80,3712]{1,0:T(8,128)(2,1)S(1)}, u32[]{:S(2)}, u32[]{:S(2)}) %collective-permute-start.11) | collective-permute-done | bytes 593952 | tf_op jit(solution)/shard_map/ppermute | solution.py:382
  141.9 0.0 collective-permute-done.12.middle
  141.9 0.0 collective-permute-done.13
  141.9 0.1 collective-permute-done.14
  141.9 0.1 select_add_fusion
  142.0 4.7 %collective-permute-start.15 = (bf16[80,3712]{1,0:T(8,128)(2,1)S(1)}, bf16[80,3712]{1,0:T(8,128)(2,1)S(1)}, u32[]{:S(2)}, u32[]{:S(2)}) collective-permute-start(bf16[80,3712]{1,0:T(8,128)(2,1)S(1)} %select_add_fusion), channel_id=1, source_target_pairs={{0,16},{2,18},{4,20},{6,22},{8,24},{10,26},{12,28},{14,30},{16,0},... | collective-permute-start | bytes 1781768 | tf_op jit(solution)/shard_map/ppermute | solution.py:382
  146.7 1.3 collective-permute-start.16
  148.0 0.1 slice_add_fusion.1
  148.1 0.7 collective-permute-start.17
  148.8 1.5 collective-permute-start.18
  150.3 20.9 %collective-permute-done.15.far = bf16[80,3712]{1,0:T(8,128)(2,1)S(1)} collective-permute-done((bf16[80,3712]{1,0:T(8,128)(2,1)S(1)}, bf16[80,3712]{1,0:T(8,128)(2,1)S(1)}, u32[]{:S(2)}, u32[]{:S(2)}) %collective-permute-start.15) | collective-permute-done | bytes 593952 | tf_op jit(solution)/shard_map/ppermute | solution.py:382
  171.2 0.0 collective-permute-done.16.outer
  171.2 0.5 shard_map.101
  171.7 0.0 collective-permute-done.17
  171.7 0.0 collective-permute-done.18
  171.7 0.1 collective-permute-start.19
  171.8 0.3 add_convert_fusion.1
  172.1 1.0 maximum_bitcast_fusion
  173.1 0.2 collective-permute-done.19.refs_2_
  173.3 3.0 %shard_map.102 = (bf16[128,7168]{1,0:T(8,128)(2,1)}, f32[32,128]{1,0:T(8,128)}) custom-call(bf16[40,128]{1,0:T(8,128)(2,1)S(1)} %get-tuple-element.51.refs_0_, bf16[40,3584]{1,0:T(8,128)(2,1)S(1)} %get-tuple-element.78.refs_1_, bf16[40,3584]{1,0:T(8,128)(2,1)S(1)} %collective-permute-done.19.refs_2_, f32[40,128]{1,0:T(8,128)S(1)} %get-tuple-element.85.refs_3_, ...), custom_call_target="tpu_custom_call" | custom-call | flops 73400320 | bytes 2408448 | tf_op jit(solution)/shard_map/pallas_call | solution.py:544
  (5 shorter events, 0.1 us)
Async XLA Ops:
  0.6 8.0 %copy-start.3 = (f32[128,32]{0,1:T(8,128)S(1)}, f32[128,32]{0,1:T(8,128)}, u32[]{:S(2)}) copy-start(f32[128,32]{0,1:T(8,128)} %param.9) | copy-start | bytes 49156
  0.6 8.0 %copy-start.1 = (bf16[128,7168]{1,0:T(8,128)(2,1)S(1)}, bf16[128,7168]{1,0:T(8,128)(2,1)}, u32[]{:S(2)}) copy-start(bf16[128,7168]{1,0:T(8,128)(2,1)} %refs_0_) | copy-start | bytes 5505028
  0.7 8.0 %copy-start.4 = (s32[128,8]{0,1:T(8,128)S(1)}, s32[128,8]{0,1:T(8,128)}, u32[]{:S(2)}) copy-start(s32[128,8]{0,1:T(8,128)} %param.10) | copy-start | bytes 12292
  4.1 62.9 %collective-permute-start = (bf16[5376,256]{1,0:T(8,128)(2,1)}, bf16[5376,256]{1,0:T(8,128)(2,1)S(1)}, u32[]{:S(2)}, u32[]{:S(2)}) collective-permute-start(bf16[5376,256]{1,0:T(8,128)(2,1)} %shard_map.94.refs_5_.refs_4_), channel_id=1, source_target_pairs={{0,2},{2,0},{4,6},{6,4},{8,10},{10,8},{12,14},{14,12},{16,18},{18,... | collective-permute-start | bytes 8257544 | tf_op jit(solution)/shard_map/ppermute | solution.py:382
  7.1 61.4 %collective-permute-start.1 = (bf16[5376,256]{1,0:T(8,128)(2,1)}, bf16[5376,256]{1,0:T(8,128)(2,1)}, u32[]{:S(2)}, u32[]{:S(2)}) collective-permute-start(bf16[5376,256]{1,0:T(8,128)(2,1)} %shard_map.94.refs_5_.refs_4_), channel_id=1, source_target_pairs={{0,4},{2,6},{4,0},{6,2},{8,12},{10,14},{12,8},{14,10},{16,20},{18,... | collective-permute-start | bytes 8257544 | tf_op jit(solution)/shard_map/ppermute | solution.py:382
  8.7 1.5 copy-start.2
  12.7 2.3 %collective-permute-start.2 = (bf16[2,40,3584]{2,1,0:T(8,128)(2,1)}, bf16[2,40,3584]{2,1,0:T(8,128)(2,1)}, u32[]{:S(2)}, u32[]{:S(2)}) collective-permute-start(bf16[2,40,3584]{2,1,0:T(8,128)(2,1)} %get-tuple-element.54), channel_id=1, source_target_pairs={{0,1},{1,0},{2,3},{3,2},{4,5},{5,4},{6,7},{7,6},{8,9},{9,8},{10,11... | collective-permute-start | bytes 1720328 | tf_op jit(solution)/shard_map/ppermute | solution.py:428
  16.3 53.0 %collective-permute-start.3 = (bf16[160,3584]{1,0:T(8,128)(2,1)S(1)}, bf16[160,3584]{1,0:T(8,128)(2,1)S(1)}, u32[]{:S(2)}, u32[]{:S(2)}) collective-permute-start(bf16[160,3584]{1,0:T(8,128)(2,1)S(1)} %pad_maximum_fusion.refs_0_), channel_id=1, source_target_pairs={{0,16},{2,18},{4,20},{6,22},{8,24},{10,26},{12,28},{14,30},{16,0},... | collective-permute-start | bytes 3440648 | tf_op jit(solution)/shard_map/ppermute | solution.py:382
  18.9 52.4 %collective-permute-start.4 = (bf16[160,3584]{1,0:T(8,128)(2,1)S(1)}, bf16[160,3584]{1,0:T(8,128)(2,1)S(1)}, u32[]{:S(2)}, u32[]{:S(2)}) collective-permute-start(bf16[160,3584]{1,0:T(8,128)(2,1)S(1)} %pad_maximum_fusion.refs_0_), channel_id=1, source_target_pairs={{8,0},{10,2},{12,4},{14,6},{16,24},{18,26},{20,28},{22,30},{9,1},{... | collective-permute-start | bytes 3440648 | tf_op jit(solution)/shard_map/ppermute | solution.py:382
  72.7 29.7 %collective-permute-start.7 = (bf16[2560,256]{1,0:T(8,128)(2,1)S(1)}, bf16[2560,256]{1,0:T(8,128)(2,1)S(1)}, u32[]{:S(2)}, u32[]{:S(2)}) collective-permute-start(bf16[2560,256]{1,0:T(8,128)(2,1)S(1)} %slice.44), channel_id=1, source_target_pairs={{0,2},{2,0},{4,6},{6,4},{8,10},{10,8},{12,14},{14,12},{16,18},{18,... | collective-permute-start | bytes 3932168 | tf_op jit(solution)/shard_map/ppermute | solution.py:382
  73.4 32.3 %copy-start = (bf16[5376,256]{1,0:T(8,128)(2,1)S(1)}, bf16[5376,256]{1,0:T(8,128)(2,1)}, u32[]{:S(2)}) copy-start(bf16[5376,256]{1,0:T(8,128)(2,1)} %shard_map.94.refs_5_.refs_4_) | copy-start | bytes 8257540
  73.4 32.3 %collective-permute-start.8 = (bf16[2816,256]{1,0:T(8,128)(2,1)S(1)}, bf16[2816,256]{1,0:T(8,128)(2,1)S(1)}, u32[]{:S(2)}, u32[]{:S(2)}) collective-permute-start(bf16[2816,256]{1,0:T(8,128)(2,1)S(1)} %slice.45), channel_id=1, source_target_pairs={{0,4},{2,6},{4,0},{6,2},{8,12},{10,14},{12,8},{14,10},{16,20},{18,... | collective-permute-start | bytes 4325384 | tf_op jit(solution)/shard_map/ppermute | solution.py:382
  74.0 25.7 %collective-permute-start.5 = (bf16[160,3584]{1,0:T(8,128)(2,1)S(1)}, bf16[160,3584]{1,0:T(8,128)(2,1)S(1)}, u32[]{:S(2)}, u32[]{:S(2)}) collective-permute-start(bf16[160,3584]{1,0:T(8,128)(2,1)S(1)} %broadcast_select_fusion), channel_id=1, source_target_pairs={{8,0},{10,2},{12,4},{14,6},{16,24},{18,26},{20,28},{22,30},{0,8},{... | collective-permute-start | bytes 3440648 | tf_op jit(solution)/shard_map/ppermute | solution.py:382
  74.1 25.6 %collective-permute-start.6 = (bf16[160,3584]{1,0:T(8,128)(2,1)S(1)}, bf16[160,3584]{1,0:T(8,128)(2,1)S(1)}, u32[]{:S(2)}, u32[]{:S(2)}) collective-permute-start(bf16[160,3584]{1,0:T(8,128)(2,1)S(1)} %pad_maximum_fusion.refs_0_), channel_id=1, source_target_pairs={{8,16},{10,18},{12,20},{14,22},{16,8},{18,10},{20,12},{22,14},{9,1... | collective-permute-start | bytes 3440648 | tf_op jit(solution)/shard_map/ppermute | solution.py:382
  110.0 4.7 %collective-permute-start.9 = (f32[320,1024]{1,0:T(8,128)S(1)}, f32[320,1024]{1,0:T(8,128)S(1)}, u32[]{:S(2)}, u32[]{:S(2)}) collective-permute-start(f32[320,1024]{1,0:T(8,128)S(1)} %shard_map.97.mine.refs_0_), channel_id=1, source_target_pairs={{0,1},{1,0},{2,3},{3,2},{4,5},{5,4},{6,7},{7,6},{8,9},{9,8},{10,11... | collective-permute-start | bytes 3932168 | tf_op jit(solution)/shard_map/ppermute | solution.py:477
  114.1 4.2 %collective-permute-start.10 = (f32[320,512]{1,0:T(8,128)S(1)}, f32[320,512]{1,0:T(8,128)S(1)}, u32[]{:S(2)}, u32[]{:S(2)}) collective-permute-start(f32[320,512]{1,0:T(8,128)S(1)} %shard_map.99.refs_2_), channel_id=1, source_target_pairs={{0,1},{1,0},{2,3},{3,2},{4,5},{5,4},{6,7},{7,6},{8,9},{9,8},{10,11... | collective-permute-start | bytes 1966088 | tf_op jit(solution)/shard_map/ppermute | solution.py:486
  118.4 23.5 %collective-permute-start.13 = (bf16[128,3584]{1,0:T(8,128)(2,1)S(1)}, bf16[128,3584]{1,0:T(8,128)(2,1)S(1)}, u32[]{:S(2)}, u32[]{:S(2)}) collective-permute-start(bf16[128,3584]{1,0:T(8,128)(2,1)S(1)} %get-tuple-element.68), channel_id=1, source_target_pairs={{0,2},{2,0},{4,6},{6,4},{8,10},{10,8},{12,14},{14,12},{16,18},{18,... | collective-permute-start | bytes 2752520 | tf_op jit(solution)/shard_map/ppermute | solution.py:382
  119.9 22.0 %collective-permute-start.14 = (bf16[128,3584]{1,0:T(8,128)(2,1)S(1)}, bf16[128,3584]{1,0:T(8,128)(2,1)S(1)}, u32[]{:S(2)}, u32[]{:S(2)}) collective-permute-start(bf16[128,3584]{1,0:T(8,128)(2,1)S(1)} %get-tuple-element.69), channel_id=1, source_target_pairs={{0,4},{2,6},{4,0},{6,2},{8,12},{10,14},{12,8},{14,10},{16,20},{18,... | collective-permute-start | bytes 2752520 | tf_op jit(solution)/shard_map/ppermute | solution.py:382
  127.0 14.9 %collective-permute-start.11 = (bf16[80,3712]{1,0:T(8,128)(2,1)S(1)}, bf16[80,3712]{1,0:T(8,128)(2,1)S(1)}, u32[]{:S(2)}, u32[]{:S(2)}) collective-permute-start(bf16[80,3712]{1,0:T(8,128)(2,1)S(1)} %get-tuple-element.66), channel_id=1, source_target_pairs={{8,0},{10,2},{12,4},{14,6},{16,24},{18,26},{20,28},{22,30},{0,8},{... | collective-permute-start | bytes 1781768 | tf_op jit(solution)/shard_map/ppermute | solution.py:382
  127.1 14.8 %collective-permute-start.12 = (bf16[80,3712]{1,0:T(8,128)(2,1)S(1)}, bf16[80,3712]{1,0:T(8,128)(2,1)S(1)}, u32[]{:S(2)}, u32[]{:S(2)}) collective-permute-start(bf16[80,3712]{1,0:T(8,128)(2,1)S(1)} %get-tuple-element.76), channel_id=1, source_target_pairs={{8,16},{10,18},{12,20},{14,22},{16,8},{18,10},{20,12},{22,14},{9,1... | collective-permute-start | bytes 1781768 | tf_op jit(solution)/shard_map/ppermute | solution.py:382
  142.0 29.2 %collective-permute-start.15 = (bf16[80,3712]{1,0:T(8,128)(2,1)S(1)}, bf16[80,3712]{1,0:T(8,128)(2,1)S(1)}, u32[]{:S(2)}, u32[]{:S(2)}) collective-permute-start(bf16[80,3712]{1,0:T(8,128)(2,1)S(1)} %select_add_fusion), channel_id=1, source_target_pairs={{0,16},{2,18},{4,20},{6,22},{8,24},{10,26},{12,28},{14,30},{16,0},... | collective-permute-start | bytes 1781768 | tf_op jit(solution)/shard_map/ppermute | solution.py:382
  146.7 24.5 %collective-permute-start.16 = (bf16[80,3712]{1,0:T(8,128)(2,1)S(1)}, bf16[80,3712]{1,0:T(8,128)(2,1)S(1)}, u32[]{:S(2)}, u32[]{:S(2)}) collective-permute-start(bf16[80,3712]{1,0:T(8,128)(2,1)S(1)} %get-tuple-element.76), channel_id=1, source_target_pairs={{0,8},{2,10},{4,12},{6,14},{24,16},{26,18},{28,20},{30,22},{1,9},{... | collective-permute-start | bytes 1781768 | tf_op jit(solution)/shard_map/ppermute | solution.py:382
  148.1 23.6 %collective-permute-start.17 = (bf16[64,3584]{1,0:T(8,128)(2,1)S(1)}, bf16[64,3584]{1,0:T(8,128)(2,1)S(1)}, u32[]{:S(2)}, u32[]{:S(2)}) collective-permute-start(bf16[64,3584]{1,0:T(8,128)(2,1)S(1)} %slice_add_fusion.1), channel_id=1, source_target_pairs={{0,2},{2,0},{4,6},{6,4},{8,10},{10,8},{12,14},{14,12},{16,18},{18,... | collective-permute-start | bytes 1376264 | tf_op jit(solution)/shard_map/ppermute | solution.py:382
  148.8 22.9 %collective-permute-start.18 = (bf16[64,3584]{1,0:T(8,128)(2,1)S(1)}, bf16[64,3584]{1,0:T(8,128)(2,1)S(1)}, u32[]{:S(2)}, u32[]{:S(2)}) collective-permute-start(bf16[64,3584]{1,0:T(8,128)(2,1)S(1)} %slice_add_fusion), channel_id=1, source_target_pairs={{0,4},{2,6},{4,0},{6,2},{8,12},{10,14},{12,8},{14,10},{16,20},{18,... | collective-permute-start | bytes 1376264 | tf_op jit(solution)/shard_map/ppermute | solution.py:382
  171.7 1.6 collective-permute-start.19

commit v9 on v8

--- a/solution.py
+++ b/solution.py
@@ -165,9 +165,13 @@
     return [whole, whole, whole, top, low]
 
 
-def piece_blocks(pieces, upper):
+def piece_blocks(pieces, upper, step):
+    i = pl.program_id(0)
+    at = [i, i, i, jnp.minimum(i, upper - 1), jnp.maximum(i - upper, 0)]
     here = pl.program_id(0) < upper
-    *whole, top, low = [p[...] for p in pieces]
+    *whole, top, low = [
+        p[pl.ds(pl.multiple_of(k * step, 128), step), :] for p, k in zip(pieces, at)
+    ]
     return whole + [jnp.where(here, top, low)]
 
 
@@ -273,10 +277,10 @@
     kept2[:, columns] = g2[:half]
 
 
-def back_kernel(upper, mine, theirs, proj_mine, proj_theirs, *refs):
+def back_kernel(upper, step, mine, theirs, proj_mine, proj_theirs, *refs):
     members = SPLIT // QUAD
     pieces, outs, scratch = refs[: -members - 1], refs[-members - 1 : -1], refs[-1]
-    step, wide = pieces[0].shape
+    wide = pieces[0].shape[1]
     ff = wide // 2
     rows = outs[0].shape[0]
     part = outs[0].shape[1] - 128
@@ -305,7 +309,7 @@
             ).astype(bf16)
 
     columns = pl.ds(pl.multiple_of(pl.program_id(0) * step, 128), step)
-    w = jnp.concatenate(piece_blocks(pieces, upper), axis=1)
+    w = jnp.concatenate(piece_blocks(pieces, upper, step), axis=1)
     grads = lax.dot_general(scratch[...], w, CONTRACT1, preferred_element_type=f32)
     for i, out in enumerate(outs):
         out[:, columns] = grads[i * rows : (i + 1) * rows].astype(bf16)
@@ -460,7 +464,6 @@
     step = step_of(part, split)
     upper = split // step
     grid = (part // step,)
-    w_specs = piece_specs(step, split, 2 * ff)
     anywhere = pl.BlockSpec(memory_space=pl.ANY)
     row_scratch = [
         pltpu.VMEM((slots, part), bf16),
@@ -497,9 +500,9 @@
     got1 = send(sent1, swap1)
     got2 = send(sent2, swap2)
     b0, b1, b2, b3 = call(
-        lambda *refs: back_kernel(upper, *refs),
+        lambda *refs: back_kernel(upper, step, *refs),
         [shape((rows_chip, part + 128), bf16)] * members,
-        [VMEM] * 4 + w_specs,
+        [VMEM] * 9,
         [pltpu.VMEM((slots, QUAD * 2 * ff), bf16)],
         2 * matmul,
         2 * part * (slots + QUAD * 2 * ff),

time: 177 us -> 176 us (level)
  no operation moved by 1% of the time
where the time goes in v9:
time: 176 us
  waiting for transfers between devices  120 us (68%)
  Pallas kernels  27.6 us (16%)
  starting transfers between devices  21.8 us (12%)
  local copies, waits for them, and re-layouts  3.01 us (2%)
  other arithmetic  2.83 us (2%)
    ppermute x16, waiting for transfers between devices, send(): return lax.ppermute(array, 'expert', route)  117 us
    ppermute x16, starting transfers between devices, send(): return lax.ppermute(array, 'expert', route)  21.1 us
    pallas_call x1, Pallas kernels, per_device(): call(lambda *refs: back_kernel(upper, step, *refs), [shape((rows_chip, pa...  6.13 us
    pallas_call x1, Pallas kernels, per_device(): call(gate_up_kernel, [shape((slots, QUAD * 2 * ff), f32)], [VMEM] * 10, r...  4.3 us
    pallas_call x1, Pallas kernels, per_device(): call(proj_kernel, [shape((slots, QUAD * ff), f32)], [anywhere] * 9, row_s...  4.05 us
    pallas_call x1, Pallas kernels, per_device(): call(down_kernel, [shape((ff, part), bf16)] * 3 + [shape((lowf, part), bf...  3.68 us
  transfers between devices with their start and end apart: 20, of which 12 were waited for; matrix products, arithmetic and copies ran while one was open for 2% of the time, Pallas kernels for 10%

profile of v9, /device:TPU:0, one launch (start us, length us, event | category | flops | bytes accessed | tf_op | source)
XLA Modules:
  0.0 175.9 jit_solution(6503065166354026362)
XLA Ops:
  0.6 0.0 copy-start.3
  0.6 0.0 copy-start.1
  0.7 0.0 copy-start.4
  0.7 3.5 %shard_map.94.refs_5_.refs_4_ = bf16[5376,256]{1,0:T(8,128)(2,1)} custom-call(bf16[1,7168,128]{2,1,0:T(8,128)(2,1)} %gate.1, bf16[1,7168,128]{2,1,0:T(8,128)(2,1)} %up.1, bf16[1,128,7168]{2,1,0:T(8,128)(2,1)} %down.1), custom_call_target="tpu_custom_call" | custom-call | bytes 5505024 | tf_op jit(solution)/shard_map/pallas_call | solution.py:407
  4.1 3.0 %collective-permute-start = (bf16[5376,256]{1,0:T(8,128)(2,1)}, bf16[5376,256]{1,0:T(8,128)(2,1)S(1)}, u32[]{:S(2)}, u32[]{:S(2)}) collective-permute-start(bf16[5376,256]{1,0:T(8,128)(2,1)} %shard_map.94.refs_5_.refs_4_), channel_id=1, source_target_pairs={{0,2},{2,0},{4,6},{6,4},{8,10},{10,8},{12,14},{14,12},{16,18},{18,... | collective-permute-start | bytes 8257544 | tf_op jit(solution)/shard_map/ppermute | solution.py:386
  7.1 1.5 collective-permute-start.1
  8.7 0.0 copy-done.3
  8.7 0.0 copy-done.1
  8.7 0.0 copy-done.4
  8.7 1.5 copy-done.2
  10.2 2.5 %shard_map.95 = (bf16[2,40,3584]{2,1,0:T(8,128)(2,1)S(1)}, bf16[2,40,3584]{2,1,0:T(8,128)(2,1)}, bf16[40,128]{1,0:T(8,128)(2,1)S(1)}, f32[32,128]{1,0:T(8,128)S(...) custom-call(bf16[128,7168]{1,0:T(8,128)(2,1)S(1)} %copy-done.1, bf16[128,7168]{1,0:T(8,128)(2,1)S(1)} %copy-done.2, ...), custom_call_target="tpu_custom_call" | custom-call | flops 146800640 | bytes 3670016 | tf_op jit(solution)/shard_map/pallas_call | solution.py:418
  12.7 0.0 collective-permute-start.2
  12.7 2.3 %collective-permute-done.2 = bf16[2,40,3584]{2,1,0:T(8,128)(2,1)} collective-permute-done((bf16[2,40,3584]{2,1,0:T(8,128)(2,1)}, bf16[2,40,3584]{2,1,0:T(8,128)(2,1)}, u32[]{:S(2)}, u32[]{:S(2)}) %collective-permute-start.2) | collective-permute-done | bytes 573472 | tf_op jit(solution)/shard_map/ppermute | solution.py:432
  15.1 1.1 select_bitcast_fusion.3
  16.2 0.1 pad_maximum_fusion.refs_0_
  16.3 2.7 %collective-permute-start.3 = (bf16[160,3584]{1,0:T(8,128)(2,1)S(1)}, bf16[160,3584]{1,0:T(8,128)(2,1)S(1)}, u32[]{:S(2)}, u32[]{:S(2)}) collective-permute-start(bf16[160,3584]{1,0:T(8,128)(2,1)S(1)} %pad_maximum_fusion.refs_0_), channel_id=1, source_target_pairs={{0,16},{2,18},{4,20},{6,22},{8,24},{10,26},{12,28},{14,30},{16,0},... | collective-permute-start | bytes 3440648 | tf_op jit(solution)/shard_map/ppermute | solution.py:386
  18.9 1.3 collective-permute-start.4
  20.2 46.8 %collective-permute-done.w1.refs_6_.refs_5_ = bf16[5376,256]{1,0:T(8,128)(2,1)S(1)} collective-permute-done((bf16[5376,256]{1,0:T(8,128)(2,1)}, bf16[5376,256]{1,0:T(8,128)(2,1)S(1)}, u32[]{:S(2)}, u32[]{:S(2)}) %collective-permute-start) | collective-permute-done | bytes 2752544 | tf_op jit(solution)/shard_map/ppermute | solution.py:386
  67.0 1.6 collective-permute-done.1.w2.refs_7_.refs_6_
  68.6 0.6 collective-permute-done.3.refs_1_
  69.2 2.1 %collective-permute-done.4.refs_3_ = bf16[160,3584]{1,0:T(8,128)(2,1)S(1)} collective-permute-done((bf16[160,3584]{1,0:T(8,128)(2,1)S(1)}, bf16[160,3584]{1,0:T(8,128)(2,1)S(1)}, u32[]{:S(2)}, u32[]{:S(2)}) %collective-permute-start.4) | collective-permute-done | bytes 1146912 | tf_op jit(solution)/shard_map/ppermute | solution.py:386
  71.3 1.4 slice.44
  72.7 0.6 collective-permute-start.7
  73.3 0.1 slice.45
  73.4 0.5 collective-permute-start.8
  73.9 0.1 broadcast_select_fusion
  74.0 0.1 collective-permute-start.5
  74.1 0.9 collective-permute-start.6
  75.0 24.7 %collective-permute-done.5.refs_2_ = bf16[160,3584]{1,0:T(8,128)(2,1)S(1)} collective-permute-done((bf16[160,3584]{1,0:T(8,128)(2,1)S(1)}, bf16[160,3584]{1,0:T(8,128)(2,1)S(1)}, u32[]{:S(2)}, u32[]{:S(2)}) %collective-permute-start.5) | collective-permute-done | bytes 1146912 | tf_op jit(solution)/shard_map/ppermute | solution.py:386
  99.7 0.0 collective-permute-done.6.refs_4_
  99.7 2.7 %collective-permute-done.7.refs_8_.refs_7_ = bf16[2560,256]{1,0:T(8,128)(2,1)S(1)} collective-permute-done((bf16[2560,256]{1,0:T(8,128)(2,1)S(1)}, bf16[2560,256]{1,0:T(8,128)(2,1)S(1)}, u32[]{:S(2)}, u32[]{:S(2)}) %collective-permute-start.7) | collective-permute-done | bytes 1310752 | tf_op jit(solution)/shard_map/ppermute | solution.py:386
  102.4 3.2 %collective-permute-done.8.refs_9_.refs_8_ = bf16[2816,256]{1,0:T(8,128)(2,1)S(1)} collective-permute-done((bf16[2816,256]{1,0:T(8,128)(2,1)S(1)}, bf16[2816,256]{1,0:T(8,128)(2,1)S(1)}, u32[]{:S(2)}, u32[]{:S(2)}) %collective-permute-start.8) | collective-permute-done | bytes 1441824 | tf_op jit(solution)/shard_map/ppermute | solution.py:386
  105.7 4.3 %shard_map.97.mine.refs_0_ = f32[320,1024]{1,0:T(8,128)S(1)} custom-call(bf16[160,3584]{1,0:T(8,128)(2,1)S(1)} %pad_maximum_fusion.refs_0_, bf16[160,3584]{1,0:T(8,128)(2,1)S(1)} %collective-permute-done.3.refs_1_, bf16[160,3584]{1,0:T(8,128)(2,1)S(1)} %collective-permute-done.5.refs_2_, bf16[160,3584]{1,0:T(8,128)(2,1)S(1)} %collective-permute-done.4.refs_3_, ...), custom_call_target="tpu_custom_call" | custom-call | flops 2348810240 | bytes 9633792 | tf_op jit(solution)/shard_map/pallas_call | solution.py:472
  110.0 0.1 collective-permute-start.9
  110.1 4.0 %shard_map.99.refs_2_ = f32[320,512]{1,0:T(8,128)S(1)} custom-call(bf16[160,3584]{1,0:T(8,128)(2,1)S(1)} %pad_maximum_fusion.refs_0_, bf16[160,3584]{1,0:T(8,128)(2,1)S(1)} %collective-permute-done.3.refs_1_, bf16[160,3584]{1,0:T(8,128)(2,1)S(1)} %collective-permute-done.5.refs_2_, bf16[160,3584]{1,0:T(8,128)(2,1)S(1)} %collective-permute-done.4.refs_3_, ...), custom_call_target="tpu_custom_call" | custom-call | flops 1174405120 | bytes 5963776 | tf_op jit(solution)/shard_map/pallas_call | solution.py:481
  114.1 0.6 collective-permute-start.10
  114.7 0.0 collective-permute-done.9.theirs.refs_1_
  114.7 3.7 %shard_map.98 = (bf16[128,3584]{1,0:T(8,128)(2,1)S(1)}, bf16[128,3584]{1,0:T(8,128)(2,1)S(1)}, bf16[128,3584]{1,0:T(8,128)(2,1)S(1)}, bf16[64,3584]{1,0:T(8,128)(2,1)S(1)}, bf16[64,3584]{1,0:T(8,128)(2,1)S(1)}) custom-call(f32[320,1024]{1,0:T(8,128)S(1)} %shard_map.97.mine.refs_0_, f32[320,1024]{1,0:T(8,128)S(1)} %collective-permute-done.9.theirs.refs_1_, ...), custom_call_target="tpu_custom_call" | custom-call | flops 1174405120 | bytes 5963776 | tf_op jit(solution)/shard_map/pallas_call | solution.py:490
  118.4 0.0 collective-permute-done.10.refs_3_
  118.4 1.6 collective-permute-start.13
  119.9 0.5 collective-permute-start.14
  120.4 6.1 %shard_map.100 = (bf16[80,3712]{1,0:T(8,128)(2,1)S(1)}, bf16[80,3712]{1,0:T(8,128)(2,1)S(1)}, bf16[80,3712]{1,0:T(8,128)(2,1)S(1)}, bf16[80,3712]{1,0:T(8,128)(2,1)S(1)}) custom-call(f32[320,1024]{1,0:T(8,128)S(1)} %shard_map.97.mine.refs_0_, f32[320,1024]{1,0:T(8,128)S(1)} %collective-permute-done.9.theirs.refs_1_, f32[320,512]{1,0:T(8,128)S(1)} %shard_map.99.refs_2_, ...), custom_call_target="tpu_custom_call" | custom-call | flops 2348810240 | bytes 9633792 | tf_op jit(solution)/shard_map/pallas_call | solution.py:502
  126.6 0.1 collective-permute-start.11
  126.7 0.7 collective-permute-start.12
  127.4 14.1 %collective-permute-done.11.ends = bf16[80,3712]{1,0:T(8,128)(2,1)S(1)} collective-permute-done((bf16[80,3712]{1,0:T(8,128)(2,1)S(1)}, bf16[80,3712]{1,0:T(8,128)(2,1)S(1)}, u32[]{:S(2)}, u32[]{:S(2)}) %collective-permute-start.11) | collective-permute-done | bytes 593952 | tf_op jit(solution)/shard_map/ppermute | solution.py:386
  141.4 0.0 collective-permute-done.12.middle
  141.4 0.0 collective-permute-done.13
  141.4 0.5 collective-permute-done.14
  141.9 0.1 select_add_fusion
  142.0 4.1 %collective-permute-start.15 = (bf16[80,3712]{1,0:T(8,128)(2,1)S(1)}, bf16[80,3712]{1,0:T(8,128)(2,1)S(1)}, u32[]{:S(2)}, u32[]{:S(2)}) collective-permute-start(bf16[80,3712]{1,0:T(8,128)(2,1)S(1)} %select_add_fusion), channel_id=1, source_target_pairs={{0,16},{2,18},{4,20},{6,22},{8,24},{10,26},{12,28},{14,30},{16,0},... | collective-permute-start | bytes 1781768 | tf_op jit(solution)/shard_map/ppermute | solution.py:386
  146.2 1.3 collective-permute-start.16
  147.5 0.1 slice_add_fusion.1
  147.5 0.6 collective-permute-start.17
  148.2 1.7 collective-permute-start.18
  149.9 20.8 %collective-permute-done.15.far = bf16[80,3712]{1,0:T(8,128)(2,1)S(1)} collective-permute-done((bf16[80,3712]{1,0:T(8,128)(2,1)S(1)}, bf16[80,3712]{1,0:T(8,128)(2,1)S(1)}, u32[]{:S(2)}, u32[]{:S(2)}) %collective-permute-start.15) | collective-permute-done | bytes 593952 | tf_op jit(solution)/shard_map/ppermute | solution.py:386
  170.7 0.0 collective-permute-done.16.outer
  170.7 0.5 shard_map.101
  171.2 0.0 collective-permute-done.17
  171.2 0.0 collective-permute-done.18
  171.2 0.1 collective-permute-start.19
  171.3 0.3 add_convert_fusion.1
  171.7 1.0 maximum_bitcast_fusion
  172.6 0.2 collective-permute-done.19.refs_2_
  172.9 3.0 %shard_map.102 = (bf16[128,7168]{1,0:T(8,128)(2,1)}, f32[32,128]{1,0:T(8,128)}) custom-call(bf16[40,128]{1,0:T(8,128)(2,1)S(1)} %get-tuple-element.51.refs_0_, bf16[40,3584]{1,0:T(8,128)(2,1)S(1)} %get-tuple-element.78.refs_1_, bf16[40,3584]{1,0:T(8,128)(2,1)S(1)} %collective-permute-done.19.refs_2_, f32[40,128]{1,0:T(8,128)S(1)} %get-tuple-element.85.refs_3_, ...), custom_call_target="tpu_custom_call" | custom-call | flops 73400320 | bytes 2408448 | tf_op jit(solution)/shard_map/pallas_call | solution.py:547
  (5 shorter events, 0.1 us)
Async XLA Ops:
  0.6 8.0 %copy-start.3 = (f32[128,32]{0,1:T(8,128)S(1)}, f32[128,32]{0,1:T(8,128)}, u32[]{:S(2)}) copy-start(f32[128,32]{0,1:T(8,128)} %param.9) | copy-start | bytes 49156
  0.6 8.0 %copy-start.1 = (bf16[128,7168]{1,0:T(8,128)(2,1)S(1)}, bf16[128,7168]{1,0:T(8,128)(2,1)}, u32[]{:S(2)}) copy-start(bf16[128,7168]{1,0:T(8,128)(2,1)} %refs_0_) | copy-start | bytes 5505028
  0.7 8.0 %copy-start.4 = (s32[128,8]{0,1:T(8,128)S(1)}, s32[128,8]{0,1:T(8,128)}, u32[]{:S(2)}) copy-start(s32[128,8]{0,1:T(8,128)} %param.10) | copy-start | bytes 12292
  4.1 62.9 %collective-permute-start = (bf16[5376,256]{1,0:T(8,128)(2,1)}, bf16[5376,256]{1,0:T(8,128)(2,1)S(1)}, u32[]{:S(2)}, u32[]{:S(2)}) collective-permute-start(bf16[5376,256]{1,0:T(8,128)(2,1)} %shard_map.94.refs_5_.refs_4_), channel_id=1, source_target_pairs={{0,2},{2,0},{4,6},{6,4},{8,10},{10,8},{12,14},{14,12},{16,18},{18,... | collective-permute-start | bytes 8257544 | tf_op jit(solution)/shard_map/ppermute | solution.py:386
  7.1 61.4 %collective-permute-start.1 = (bf16[5376,256]{1,0:T(8,128)(2,1)}, bf16[5376,256]{1,0:T(8,128)(2,1)}, u32[]{:S(2)}, u32[]{:S(2)}) collective-permute-start(bf16[5376,256]{1,0:T(8,128)(2,1)} %shard_map.94.refs_5_.refs_4_), channel_id=1, source_target_pairs={{0,4},{2,6},{4,0},{6,2},{8,12},{10,14},{12,8},{14,10},{16,20},{18,... | collective-permute-start | bytes 8257544 | tf_op jit(solution)/shard_map/ppermute | solution.py:386
  8.7 1.5 copy-start.2
  12.7 2.3 %collective-permute-start.2 = (bf16[2,40,3584]{2,1,0:T(8,128)(2,1)}, bf16[2,40,3584]{2,1,0:T(8,128)(2,1)}, u32[]{:S(2)}, u32[]{:S(2)}) collective-permute-start(bf16[2,40,3584]{2,1,0:T(8,128)(2,1)} %get-tuple-element.54), channel_id=1, source_target_pairs={{0,1},{1,0},{2,3},{3,2},{4,5},{5,4},{6,7},{7,6},{8,9},{9,8},{10,11... | collective-permute-start | bytes 1720328 | tf_op jit(solution)/shard_map/ppermute | solution.py:432
  16.3 53.0 %collective-permute-start.3 = (bf16[160,3584]{1,0:T(8,128)(2,1)S(1)}, bf16[160,3584]{1,0:T(8,128)(2,1)S(1)}, u32[]{:S(2)}, u32[]{:S(2)}) collective-permute-start(bf16[160,3584]{1,0:T(8,128)(2,1)S(1)} %pad_maximum_fusion.refs_0_), channel_id=1, source_target_pairs={{0,16},{2,18},{4,20},{6,22},{8,24},{10,26},{12,28},{14,30},{16,0},... | collective-permute-start | bytes 3440648 | tf_op jit(solution)/shard_map/ppermute | solution.py:386
  18.9 52.4 %collective-permute-start.4 = (bf16[160,3584]{1,0:T(8,128)(2,1)S(1)}, bf16[160,3584]{1,0:T(8,128)(2,1)S(1)}, u32[]{:S(2)}, u32[]{:S(2)}) collective-permute-start(bf16[160,3584]{1,0:T(8,128)(2,1)S(1)} %pad_maximum_fusion.refs_0_), channel_id=1, source_target_pairs={{8,0},{10,2},{12,4},{14,6},{16,24},{18,26},{20,28},{22,30},{9,1},{... | collective-permute-start | bytes 3440648 | tf_op jit(solution)/shard_map/ppermute | solution.py:386
  72.7 29.7 %collective-permute-start.7 = (bf16[2560,256]{1,0:T(8,128)(2,1)S(1)}, bf16[2560,256]{1,0:T(8,128)(2,1)S(1)}, u32[]{:S(2)}, u32[]{:S(2)}) collective-permute-start(bf16[2560,256]{1,0:T(8,128)(2,1)S(1)} %slice.44), channel_id=1, source_target_pairs={{0,2},{2,0},{4,6},{6,4},{8,10},{10,8},{12,14},{14,12},{16,18},{18,... | collective-permute-start | bytes 3932168 | tf_op jit(solution)/shard_map/ppermute | solution.py:386
  73.4 32.3 %copy-start = (bf16[5376,256]{1,0:T(8,128)(2,1)S(1)}, bf16[5376,256]{1,0:T(8,128)(2,1)}, u32[]{:S(2)}) copy-start(bf16[5376,256]{1,0:T(8,128)(2,1)} %shard_map.94.refs_5_.refs_4_) | copy-start | bytes 8257540
  73.4 32.3 %collective-permute-start.8 = (bf16[2816,256]{1,0:T(8,128)(2,1)S(1)}, bf16[2816,256]{1,0:T(8,128)(2,1)S(1)}, u32[]{:S(2)}, u32[]{:S(2)}) collective-permute-start(bf16[2816,256]{1,0:T(8,128)(2,1)S(1)} %slice.45), channel_id=1, source_target_pairs={{0,4},{2,6},{4,0},{6,2},{8,12},{10,14},{12,8},{14,10},{16,20},{18,... | collective-permute-start | bytes 4325384 | tf_op jit(solution)/shard_map/ppermute | solution.py:386
  74.0 25.7 %collective-permute-start.5 = (bf16[160,3584]{1,0:T(8,128)(2,1)S(1)}, bf16[160,3584]{1,0:T(8,128)(2,1)S(1)}, u32[]{:S(2)}, u32[]{:S(2)}) collective-permute-start(bf16[160,3584]{1,0:T(8,128)(2,1)S(1)} %broadcast_select_fusion), channel_id=1, source_target_pairs={{8,0},{10,2},{12,4},{14,6},{16,24},{18,26},{20,28},{22,30},{0,8},{... | collective-permute-start | bytes 3440648 | tf_op jit(solution)/shard_map/ppermute | solution.py:386
  74.1 25.6 %collective-permute-start.6 = (bf16[160,3584]{1,0:T(8,128)(2,1)S(1)}, bf16[160,3584]{1,0:T(8,128)(2,1)S(1)}, u32[]{:S(2)}, u32[]{:S(2)}) collective-permute-start(bf16[160,3584]{1,0:T(8,128)(2,1)S(1)} %pad_maximum_fusion.refs_0_), channel_id=1, source_target_pairs={{8,16},{10,18},{12,20},{14,22},{16,8},{18,10},{20,12},{22,14},{9,1... | collective-permute-start | bytes 3440648 | tf_op jit(solution)/shard_map/ppermute | solution.py:386
  110.0 4.7 %collective-permute-start.9 = (f32[320,1024]{1,0:T(8,128)S(1)}, f32[320,1024]{1,0:T(8,128)S(1)}, u32[]{:S(2)}, u32[]{:S(2)}) collective-permute-start(f32[320,1024]{1,0:T(8,128)S(1)} %shard_map.97.mine.refs_0_), channel_id=1, source_target_pairs={{0,1},{1,0},{2,3},{3,2},{4,5},{5,4},{6,7},{7,6},{8,9},{9,8},{10,11... | collective-permute-start | bytes 3932168 | tf_op jit(solution)/shard_map/ppermute | solution.py:480
  114.1 4.2 %collective-permute-start.10 = (f32[320,512]{1,0:T(8,128)S(1)}, f32[320,512]{1,0:T(8,128)S(1)}, u32[]{:S(2)}, u32[]{:S(2)}) collective-permute-start(f32[320,512]{1,0:T(8,128)S(1)} %shard_map.99.refs_2_), channel_id=1, source_target_pairs={{0,1},{1,0},{2,3},{3,2},{4,5},{5,4},{6,7},{7,6},{8,9},{9,8},{10,11... | collective-permute-start | bytes 1966088 | tf_op jit(solution)/shard_map/ppermute | solution.py:489
  118.4 23.1 %collective-permute-start.13 = (bf16[128,3584]{1,0:T(8,128)(2,1)S(1)}, bf16[128,3584]{1,0:T(8,128)(2,1)S(1)}, u32[]{:S(2)}, u32[]{:S(2)}) collective-permute-start(bf16[128,3584]{1,0:T(8,128)(2,1)S(1)} %get-tuple-element.68), channel_id=1, source_target_pairs={{0,2},{2,0},{4,6},{6,4},{8,10},{10,8},{12,14},{14,12},{16,18},{18,... | collective-permute-start | bytes 2752520 | tf_op jit(solution)/shard_map/ppermute | solution.py:386
  119.9 22.0 %collective-permute-start.14 = (bf16[128,3584]{1,0:T(8,128)(2,1)S(1)}, bf16[128,3584]{1,0:T(8,128)(2,1)S(1)}, u32[]{:S(2)}, u32[]{:S(2)}) collective-permute-start(bf16[128,3584]{1,0:T(8,128)(2,1)S(1)} %get-tuple-element.69), channel_id=1, source_target_pairs={{0,4},{2,6},{4,0},{6,2},{8,12},{10,14},{12,8},{14,10},{16,20},{18,... | collective-permute-start | bytes 2752520 | tf_op jit(solution)/shard_map/ppermute | solution.py:386
  126.6 14.9 %collective-permute-start.11 = (bf16[80,3712]{1,0:T(8,128)(2,1)S(1)}, bf16[80,3712]{1,0:T(8,128)(2,1)S(1)}, u32[]{:S(2)}, u32[]{:S(2)}) collective-permute-start(bf16[80,3712]{1,0:T(8,128)(2,1)S(1)} %get-tuple-element.66), channel_id=1, source_target_pairs={{8,0},{10,2},{12,4},{14,6},{16,24},{18,26},{20,28},{22,30},{0,8},{... | collective-permute-start | bytes 1781768 | tf_op jit(solution)/shard_map/ppermute | solution.py:386
  126.7 14.8 %collective-permute-start.12 = (bf16[80,3712]{1,0:T(8,128)(2,1)S(1)}, bf16[80,3712]{1,0:T(8,128)(2,1)S(1)}, u32[]{:S(2)}, u32[]{:S(2)}) collective-permute-start(bf16[80,3712]{1,0:T(8,128)(2,1)S(1)} %get-tuple-element.76), channel_id=1, source_target_pairs={{8,16},{10,18},{12,20},{14,22},{16,8},{18,10},{20,12},{22,14},{9,1... | collective-permute-start | bytes 1781768 | tf_op jit(solution)/shard_map/ppermute | solution.py:386
  142.0 28.7 %collective-permute-start.15 = (bf16[80,3712]{1,0:T(8,128)(2,1)S(1)}, bf16[80,3712]{1,0:T(8,128)(2,1)S(1)}, u32[]{:S(2)}, u32[]{:S(2)}) collective-permute-start(bf16[80,3712]{1,0:T(8,128)(2,1)S(1)} %select_add_fusion), channel_id=1, source_target_pairs={{0,16},{2,18},{4,20},{6,22},{8,24},{10,26},{12,28},{14,30},{16,0},... | collective-permute-start | bytes 1781768 | tf_op jit(solution)/shard_map/ppermute | solution.py:386
  146.2 24.6 %collective-permute-start.16 = (bf16[80,3712]{1,0:T(8,128)(2,1)S(1)}, bf16[80,3712]{1,0:T(8,128)(2,1)S(1)}, u32[]{:S(2)}, u32[]{:S(2)}) collective-permute-start(bf16[80,3712]{1,0:T(8,128)(2,1)S(1)} %get-tuple-element.76), channel_id=1, source_target_pairs={{0,8},{2,10},{4,12},{6,14},{24,16},{26,18},{28,20},{30,22},{1,9},{... | collective-permute-start | bytes 1781768 | tf_op jit(solution)/shard_map/ppermute | solution.py:386
  147.5 23.7 %collective-permute-start.17 = (bf16[64,3584]{1,0:T(8,128)(2,1)S(1)}, bf16[64,3584]{1,0:T(8,128)(2,1)S(1)}, u32[]{:S(2)}, u32[]{:S(2)}) collective-permute-start(bf16[64,3584]{1,0:T(8,128)(2,1)S(1)} %slice_add_fusion.1), channel_id=1, source_target_pairs={{0,2},{2,0},{4,6},{6,4},{8,10},{10,8},{12,14},{14,12},{16,18},{18,... | collective-permute-start | bytes 1376264 | tf_op jit(solution)/shard_map/ppermute | solution.py:386
  148.2 23.0 %collective-permute-start.18 = (bf16[64,3584]{1,0:T(8,128)(2,1)S(1)}, bf16[64,3584]{1,0:T(8,128)(2,1)S(1)}, u32[]{:S(2)}, u32[]{:S(2)}) collective-permute-start(bf16[64,3584]{1,0:T(8,128)(2,1)S(1)} %slice_add_fusion), channel_id=1, source_target_pairs={{0,4},{2,6},{4,0},{6,2},{8,12},{10,14},{12,8},{14,10},{16,20},{18,... | collective-permute-start | bytes 1376264 | tf_op jit(solution)/shard_map/ppermute | solution.py:386
  171.2 1.6 collective-permute-start.19
